TPU v7x, 32 devices: a whole 2x2x4 slice. The times are simulated.
32 devices in a mesh: tile: 2 (over y), date: 4 (over x, core), row: 4 (over z).
Axes of the slice: x: 2, y: 2, z: 4, core: 2. Of those that a mesh axis runs over, the one named last changes fastest.
Arguments:
- intensity: bfloat16 [64, 2, 512, 512], P('date', None, ('tile', 'row')), parts along dimension 2, may hold values from 0.019897461 to 1
- valid_mask: int32 [64, 8, 16, 2048], P(None, 'tile', ('date', 'row')), parts along dimension 1, may hold values 0 or 1
- day_index: int32 [64], replicated, may hold values from 0 to 364
Outputs:
- state_field: float32 [6, 8, 16, 2048], P(None, 'tile', ('date', 'row')), parts along dimension 1
There are 2 independent parts, one for each index of `tile`. A program takes and returns all parts, laid end to end along the dimension named above; an argument that names none is the same for every part. Nothing has to cross between parts.
All inputs are finite; a program needn't handle non-finite values. No bound on the sum of `valid_mask` on one device may be relied on, other than what follows from the above.
Results may differ from a plain program's by a relative error of at most 0.0009.
Values may be sent and summed in bfloat16 or wider, within the bound.
No kernel may reach another device: no remote copies, remote signals or barrier semaphores. Data moves between devices by JAX's collectives and lax.ppermute only.
A program may use at most 64 MiB of HBM per device.

v0:
```python
import math

import jax
import jax.numpy as jnp
from jax import lax
from jax.sharding import PartitionSpec as P

DATES = 64
RADIUS = 3
STATES = 6


obs_noise = 0.05


def extended(cells, sides, width):
    for axis, dim in sides:
        count = lax.axis_size(axis)
        ends = count - 1
        head = lax.slice_in_dim(cells, 0, width, axis=dim)
        tail = lax.slice_in_dim(cells, cells.shape[dim] - width, cells.shape[dim], axis=dim)
        cells = jnp.concatenate(
            [
                lax.ppermute(tail, axis, [(i, (i + 1) % count) for i in range(ends)]),
                cells,
                lax.ppermute(head, axis, [((i + 1) % count, i) for i in range(ends)]),
            ],
            axis=dim,
        )
    return cells


def edge_count(positions, length):
    lower = jnp.maximum(positions - RADIUS, 0)
    upper = jnp.minimum(positions + RADIUS, length - 1)
    return (upper - lower + 1).astype(jnp.float32)


def make_band(width):
    positions = lax.iota(jnp.int32, width)
    near = jnp.abs(positions[:, None] - positions[None, :]) <= RADIUS
    return (near.astype(jnp.bfloat16), edge_count(positions, width))


def harmonic_fit(vv_series, vh_series, keep_flags, day_vector):
    phase_angle = day_vector.astype(jnp.float32) * (2.0 * math.pi / 365.0)
    ones_row = jnp.ones_like(phase_angle)
    zero_row = jnp.zeros_like(phase_angle)
    base_rows = [
        ones_row,
        jnp.cos(phase_angle),
        jnp.sin(phase_angle),
        jnp.cos(2.0 * phase_angle),
        jnp.sin(2.0 * phase_angle),
    ]
    design_vv = jnp.stack(base_rows + [zero_row])
    design_vh = jnp.stack(base_rows + [ones_row])
    pair_list = [(a, b) for a in range(STATES) for b in range(a, STATES)]
    pair_table = jnp.stack(
        [design_vv[a] * design_vv[b] + design_vh[a] * design_vh[b] for a, b in pair_list]
    )
    highest = lax.Precision.HIGHEST
    pair_sums = (
        jnp.dot(pair_table, keep_flags, precision=highest, preferred_element_type=jnp.float32)
        / obs_noise
    )
    vv_obs = jnp.log(vv_series.astype(jnp.float32)) * keep_flags
    vh_obs = jnp.log(vh_series.astype(jnp.float32)) * keep_flags
    right = jnp.dot(design_vv, vv_obs, precision=highest, preferred_element_type=jnp.float32)
    right = (
        right + jnp.dot(design_vh, vh_obs, precision=highest, preferred_element_type=jnp.float32)
    ) / obs_noise
    normal = {}
    for index, (a, b) in enumerate(pair_list):
        entry = pair_sums[index]
        if a == b:
            entry = entry + 1.0
        normal[b, a] = entry
    lower = {}
    for i in range(STATES):
        for j in range(i + 1):
            total = normal[i, j]
            for k in range(j):
                total = total - lower[i, k] * lower[j, k]
            if i == j:
                lower[i, i] = jnp.sqrt(total)
            else:
                lower[i, j] = total / lower[j, j]
    middle = []
    for i in range(STATES):
        total = right[i]
        for k in range(i):
            total = total - lower[i, k] * middle[k]
        middle.append(total / lower[i, i])
    solved = [None] * STATES
    for i in reversed(range(STATES)):
        total = middle[i]
        for k in range(i + 1, STATES):
            total = total - lower[k, i] * solved[k]
        solved[i] = total / lower[i, i]
    return jnp.stack(solved)


def body(intensity, valid_mask, day_index):
    local_dates = intensity.shape[0]
    local_rows = intensity.shape[2]
    local_cols = intensity.shape[3]
    date_devices = lax.axis_size("date")
    row_devices = lax.axis_size("row")
    segment = local_rows * local_cols // (date_devices * row_devices)
    all_dates = local_dates * date_devices
    mask_wire = valid_mask.astype(jnp.bfloat16)
    mask_moved = lax.all_to_all(mask_wire, "row", split_axis=1, concat_axis=2, tiled=True)
    mask_moved = mask_moved.reshape(valid_mask.shape[0], row_devices * segment)
    band_matrix, col_count = make_band(local_cols)
    height = local_rows * row_devices
    row_start = lax.axis_index("row") * local_rows
    row_count = edge_count(row_start + lax.iota(jnp.int32, local_rows), height)
    padded = extended(intensity, (("row", 2),), RADIUS)
    summed = jnp.einsum("tprc,cd->tprd", padded, band_matrix, preferred_element_type=jnp.float32)
    window = sum([summed[:, :, k : k + local_rows] for k in range(2 * RADIUS + 1)])
    box_mean = window / (row_count[:, None] * col_count[None, :])
    partial_sum = jnp.sum(intensity.astype(jnp.float32) / box_mean, axis=0)
    ratio_total = lax.psum(partial_sum, "date")
    filtered = (box_mean * (ratio_total / DATES)).astype(jnp.bfloat16)
    blocks_out = filtered.reshape(local_dates, 2, date_devices, row_devices * segment)
    series = lax.all_to_all(blocks_out, "date", split_axis=2, concat_axis=0, tiled=True)
    series = series.reshape(all_dates, 2, row_devices * segment)
    keep_flags = mask_moved.astype(jnp.float32)
    state_rows = harmonic_fit(series[:, 0], series[:, 1], keep_flags, day_index)
    state_rows = state_rows.reshape(STATES, 1, row_devices, segment)
    return lax.all_to_all(state_rows, "row", split_axis=2, concat_axis=1, tiled=True)


def solution(mesh):
    return jax.shard_map(
        body,
        mesh=mesh,
        in_specs=(
            P("date", None, ("tile", "row"), None),
            P(None, "tile", ("date", "row"), None),
            P(),
        ),
        out_specs=P(None, "tile", ("date", "row"), None),
        check_vma=False,
    )
```

profile of v0, /device:TPU:0, one launch (start us, length us, event | category | flops | bytes accessed | tf_op | source)
XLA Modules:
  0.0 143.9 jit_solution(11418211320767622561)
XLA Ops:
  6.5 1.1 fusion.92
  7.7 5.6 %collective-permute-start = (bf16[16,2,3,512]{3,2,1,0:T(4,128)(2,1)S(1)}, bf16[16,2,3,512]{3,2,1,0:T(4,128)(2,1)}, u32[]{:S(2)}, u32[]{:S(2)}) collective-permute-start(bf16[16,2,3,512]{3,2,1,0:T(4,128)(2,1)S(1)} %get-tuple-element.33), channel_id=1, source_target_pairs={{0,1},{1,2},{2,3},{4,5},{5,6},{6,7},{8,9},{9,10},{10,11},{12,13},{... | collective-permute-start | bytes 294920 | tf_op jit(solution)/shard_map/ppermute | solution.py:24
  13.3 1.3 collective-permute-start.1
  14.6 3.2 %fusion.93 = bf16[4,64,1,2048]{3,2,1,0:T(2,128)(2,1)S(1)} fusion(s32[64,4,1,2048]{3,2,1,0:T(1,128)} %param.4), kind=kLoop, calls=%fused_computation.163 | loop fusion | flops 524288 | bytes 3145728
  17.8 0.5 broadcast.219
  18.3 7.0 %reduce = bf16[4,64,2048]{2,1,0:T(8,128)(2,1)S(1)} reduce(bf16[4,64,1,2048]{3,2,1,0:T(2,128)(2,1)S(1)} %fusion.93, bf16[]{:T(256)} %broadcast.219), dimensions={2}, to_apply=%fusion.93.reduce_sub_computation | reduce | bytes 2097154
  25.3 0.0 copy-start
  25.3 2.0 %reshape.82 = bf16[4,2,65536]{2,1,0:T(2,128)(2,1)} reshape(bf16[4,64,2048]{2,1,0:T(8,128)(2,1)S(1)} %reduce) | data formatting | bytes 2097152
  27.3 5.9 %all-to-all-start.1 = ((bf16[4,2,65536]{2,1,0:T(2,128)(2,1)}), bf16[4,2,65536]{2,1,0:T(2,128)(2,1)S(1)}, u32[]{:S(2)}, u32[]{:S(2)}) async-start(bf16[4,2,65536]{2,1,0:T(2,128)(2,1)} %reshape.82), calls=%async_computation.1 | async-start | bytes 2097152 | tf_op jit(solution)/shard_map/all_to_all | solution.py:113
  33.3 0.0 all-reduce.2.cloned.1.call-start
  33.3 0.1 broadcast_multiply_fusion.1
  33.4 0.0 collective-permute-done
  33.4 0.0 collective-permute-done.1
  33.4 0.0 copy-done
  33.4 2.4 %fusion.2 = f32[16,2,70,512]{3,2,1,0:T(8,128)S(1)} fusion(bf16[16,2,3,512]{3,2,1,0:T(4,128)(2,1)} %collective-permute-done.1, bf16[16,2,64,512]{3,2,1,0:T(8,128)(2,1)S(1)} %copy-done, bf16[16,2,3,512]{3,2,1,0:T(4,128)(2,1)} %collective-permute-done), kind=kOutput, calls=%fused_computation.14 | convolution fusion | flops 1182072832 | bytes 6881280 | tf_op jit(solution)/shard_map/tprc,cd->tprd/dot_general | solution.py:120
  35.8 5.4 %fusion.1 = (f32[2,64,512]{2,1,0:T(8,128)}, f32[16,2,64,512]{3,2,1,0:T(8,128)}) fusion(bf16[16,2,64,512]{3,2,1,0:T(8,128)(2,1)S(1)} %copy-done, f32[64,512]{1,0:T(8,128)S(1)} %broadcast_multiply_fusion.1, f32[16,2,70,512]{3,2,1,0:T(8,128)S(1)} %fusion.2), kind=kLoop, calls=%fused_computation.11 | loop fusion | flops 10420224 | bytes 36044800 | tf_op jit(solution)/shard_map/reduce_sum | solution.py:123
  41.2 0.0 all-reduce.2.cloned.1.call-update
  41.2 33.6 %all-reduce.2.cloned.1.call-done = f32[2,64,512]{2,1,0:T(8,128)} async-done(((f32[2,64,512]{2,1,0:T(8,128)}), f32[2,64,512]{2,1,0:T(8,128)}) %all-reduce.2.cloned.1.call-update) | async-done | bytes 262160 | tf_op jit(solution)/shard_map/psum | solution.py:124
  74.8 1.0 broadcast_multiply_fusion
  75.8 2.9 %multiply_convert_fusion = bf16[16,2,64,512]{3,2,1,0:T(8,128)(2,1)S(1)} fusion(f32[16,2,64,512]{3,2,1,0:T(8,128)} %get-tuple-element.27, f32[2,64,512]{2,1,0:T(8,128)S(1)} %broadcast_multiply_fusion, f32[64,512]{1,0:T(8,128)S(1)} %broadcast_multiply_fusion.1), kind=kLoop, calls=%fused_computation.9 | loop fusion | flops 3145728 | bytes 6684672 | tf_op jit(solution)/shard_map/convert_element_type | solution.py:125
  78.6 2.8 %reshape.78 = bf16[16,2,4,8192]{3,2,1,0:T(4,128)(2,1)} reshape(bf16[16,2,64,512]{3,2,1,0:T(8,128)(2,1)S(1)} %multiply_convert_fusion) | data formatting | bytes 4194304 | tf_op jit(solution)/shard_map/reshape | solution.py:126
  81.4 4.1 %copy.28 = bf16[16,2,4,8192]{3,0,1,2:T(8,128)(2,1)} copy(bf16[16,2,4,8192]{3,2,1,0:T(4,128)(2,1)} %reshape.78) | data formatting | bytes 4194304 | tf_op jit(solution)/shard_map/reshape | solution.py:126
  85.5 0.0 copy-start.1
  85.5 0.0 all-to-all-done.1
  85.5 4.8 %all-to-all-start = ((bf16[16,2,4,8192]{3,0,1,2:T(8,128)(2,1)}), bf16[16,2,4,8192]{3,0,1,2:T(8,128)(2,1)}, u32[]{:S(2)}, u32[]{:S(2)}) async-start(bf16[16,2,4,8192]{3,0,1,2:T(8,128)(2,1)} %copy.28), calls=%async_computation | async-start | bytes 4194304 | tf_op jit(solution)/shard_map/all_to_all | solution.py:127
  90.3 0.0 copy-done.1
  90.3 0.1 fusion.69
  90.5 0.1 stack.128
  90.6 1.0 reshape.83
  91.5 1.4 copy.31
  92.9 0.6 copy.41
  93.5 0.5 convolution_multiply_fusion
  94.1 21.8 %all-to-all-done = bf16[16,2,4,8192]{3,0,1,2:T(8,128)(2,1)} async-done(((bf16[16,2,4,8192]{3,0,1,2:T(8,128)(2,1)}), bf16[16,2,4,8192]{3,0,1,2:T(8,128)(2,1)}, u32[]{:S(2)}, u32[]{:S(2)}) %all-to-all-start) | async-done | bytes 2097184 | tf_op jit(solution)/shard_map/all_to_all | solution.py:127
  115.9 1.7 %copy.29 = bf16[16,2,4,8192]{3,0,2,1:T(8,128)(2,1)S(1)} copy(bf16[16,2,4,8192]{3,0,1,2:T(8,128)(2,1)} %all-to-all-done) | data formatting | bytes 4194304 | tf_op jit(solution)/shard_map/all_to_all | solution.py:127
  117.6 1.5 %fusion.8 = f32[6,8192]{1,0:T(8,128)S(1)} fusion(f32[6,64]{1,0:T(8,128)S(1)} %stack.107, bf16[64,8192]{1,0:T(8,128)(2,1)S(1)} %bitcast.87, bf16[64,2,8192]{2,0,1:T(8,128)(2,1)S(1)} %bitcast.90), kind=kOutput, calls=%fused_computation.20 | convolution fusion | flops 39321600 | bytes 2297856 | tf_op jit(solution)/shard_map/dot_general | solution.py:69
  119.1 1.5 %fusion = f32[6,8192]{1,0:T(8,128)S(1)} fusion(f32[6,8192]{1,0:T(8,128)S(1)} %fusion.8, f32[6,64]{1,0:T(8,128)S(1)} %stack.108, bf16[64,8192]{1,0:T(8,128)(2,1)S(1)} %bitcast.88, bf16[64,2,8192]{2,0,1:T(8,128)(2,1)S(1)} %bitcast.91), kind=kOutput, calls=%fused_computation.2 | convolution fusion | flops 39419904 | bytes 2560000 | tf_op jit(solution)/shard_map/dot_general | solution.py:71
  120.5 1.3 subtract_divide_fusion.6
  121.9 0.9 subtract_divide_fusion.5
  122.8 1.3 subtract_divide_fusion
  124.2 11.9 %all_to_all.36 = f32[6,1,4,2048]{3,1,0,2:T(1,128)S(1)} all-to-all(f32[6,1,4,2048]{3,1,0,2:T(1,128)S(1)} %constant_dynamic-update-slice_fusion), channel_id=1, replica_groups=mesh['tile'=2,'date'=4,'row'=4] {'row'}, dimensions={2} | all-to-all | bytes 393216 | tf_op jit(solution)/shard_map/all_to_all | solution.py:132
  136.0 0.1 copy.46
  136.2 0.9 copy.39
  (13 shorter events, 0.1 us)
Async XLA Ops:
  7.7 25.7 %collective-permute-start = (bf16[16,2,3,512]{3,2,1,0:T(4,128)(2,1)S(1)}, bf16[16,2,3,512]{3,2,1,0:T(4,128)(2,1)}, u32[]{:S(2)}, u32[]{:S(2)}) collective-permute-start(bf16[16,2,3,512]{3,2,1,0:T(4,128)(2,1)S(1)} %get-tuple-element.33), channel_id=1, source_target_pairs={{0,1},{1,2},{2,3},{4,5},{5,6},{6,7},{8,9},{9,10},{10,11},{12,13},{... | collective-permute-start | bytes 294920 | tf_op jit(solution)/shard_map/ppermute | solution.py:24
  13.3 20.1 %collective-permute-start.1 = (bf16[16,2,3,512]{3,2,1,0:T(4,128)(2,1)S(1)}, bf16[16,2,3,512]{3,2,1,0:T(4,128)(2,1)}, u32[]{:S(2)}, u32[]{:S(2)}) collective-permute-start(bf16[16,2,3,512]{3,2,1,0:T(4,128)(2,1)S(1)} %get-tuple-element.34), channel_id=1, source_target_pairs={{1,0},{2,1},{3,2},{5,4},{6,5},{7,6},{9,8},{10,9},{11,10},{13,12},{... | collective-permute-start | bytes 294920 | tf_op jit(solution)/shard_map/ppermute | solution.py:26
  25.3 8.1 %copy-start = (bf16[16,2,64,512]{3,2,1,0:T(8,128)(2,1)S(1)}, bf16[16,2,64,512]{3,2,1,0:T(8,128)(2,1)}, u32[]{:S(2)}) copy-start(bf16[16,2,64,512]{3,2,1,0:T(8,128)(2,1)} %param.3) | copy-start | bytes 6291460
  27.3 58.2 %all-to-all-start.1 = ((bf16[4,2,65536]{2,1,0:T(2,128)(2,1)}), bf16[4,2,65536]{2,1,0:T(2,128)(2,1)S(1)}, u32[]{:S(2)}, u32[]{:S(2)}) async-start(bf16[4,2,65536]{2,1,0:T(2,128)(2,1)} %reshape.82), calls=%async_computation.1 | async-start | bytes 2097152 | tf_op jit(solution)/shard_map/all_to_all | solution.py:113
  33.3 41.5 %all-reduce.2.cloned.1.call-start = ((), (), s32[]{:S(2)}) async-start(), calls=%async_computation.3 | async-start | bytes 524288 | tf_op jit(solution)/shard_map/psum | solution.py:124
  85.5 4.8 %copy-start.1 = (s32[64]{0:T(128)S(1)}, s32[64]{0:T(128)}, u32[]{:S(2)}) copy-start(s32[64]{0:T(128)} %param.5) | copy-start | bytes 772
  85.5 30.4 %all-to-all-start = ((bf16[16,2,4,8192]{3,0,1,2:T(8,128)(2,1)}), bf16[16,2,4,8192]{3,0,1,2:T(8,128)(2,1)}, u32[]{:S(2)}, u32[]{:S(2)}) async-start(bf16[16,2,4,8192]{3,0,1,2:T(8,128)(2,1)} %copy.28), calls=%async_computation | async-start | bytes 4194304 | tf_op jit(solution)/shard_map/all_to_all | solution.py:127
Sparse Core Ops, SparseCore 0:
  41.3 33.4 all-reduce.1
where the time goes:
time: 144 us
  waiting for transfers between devices  55.4 us (38%)
  other arithmetic  23.1 us (16%)
  starting transfers between devices  17.6 us (12%)
  local copies, waits for them, and re-layouts  16.4 us (11%)
  between operations  13.6 us (9%)
  blocking collectives  11.9 us (8%)
  matrix products  5.86 us (4%)
    psum x1, waiting for transfers between devices, body(): ratio_total = lax.psum(partial_sum, 'date')  33.6 us
    all_to_all x1, waiting for transfers between devices, body(): lax.all_to_all(blocks_out, 'date', split_axis=2, concat_axis=0, tiled=True)  21.8 us
    all_to_all x1, blocking collectives, body(): lax.all_to_all(state_rows, 'row', split_axis=2, concat_axis=1, tiled=True)  11.9 us
    unnamed x2, other arithmetic  10.2 us
    reshape x2, local copies, waits for them, and re-layouts, body(): filtered.reshape(local_dates, 2, date_devices, row_devices * segment)  6.86 us
    all_to_all x1, starting transfers between devices, body(): lax.all_to_all(mask_wire, 'row', split_axis=1, concat_axis=2, tiled=True)  5.94 us
    ppermute x1, starting transfers between devices, extended(): lax.ppermute(tail, axis, [(i, (i + 1) % count) for i in range(ends)])  5.59 us
    reduce_sum x1, other arithmetic, body(): partial_sum = jnp.sum(intensity.astype(jnp.float32) / box_mean, axis=0)  5.36 us
  transfers between devices with their start and end apart: 5, of which 2 were waited for; matrix products, arithmetic and copies ran while one was open for 24% of the time, Pallas kernels for 0%

commit v1 on v0

v1 whole, which is shorter than its diff:
```python
import functools
import math

import jax
import jax.numpy as jnp
from jax import lax
from jax.experimental import pallas as pl
from jax.experimental.pallas import tpu as pltpu
from jax.sharding import PartitionSpec as P

RADIUS = 3
STATES = 6
HALO = 4
LANES = 128
HARMONICS = 9
NOISE = 0.05
CODE_STEPS = 8192.0
VMEM_BYTES = 40 * 1024 * 1024

f32 = jnp.float32
PAIRS = [(i, j) for i in range(STATES) for j in range(i)]


def partners(count, k):
    return [(i, i ^ k) for i in range(count)]


def edge_count(positions, length):
    lower = jnp.maximum(positions - RADIUS, 0)
    upper = jnp.minimum(positions + RADIUS, length - 1)
    return (upper - lower + 1).astype(f32)


def whole():
    return pl.BlockSpec(memory_space=pltpu.VMEM)


def scalars():
    return pl.BlockSpec(memory_space=pltpu.SMEM)


def params():
    return pltpu.CompilerParams(vmem_limit_bytes=VMEM_BYTES)


def flags_kernel(mask_ref, *out_refs):
    r = lax.axis_index("row")
    for k, out_ref in enumerate(out_refs):
        out_ref[...] = mask_ref[:, r ^ k].astype(f32).astype(jnp.bfloat16)


def cast_flags(mask, pieces):
    dates, blocks, chunks, lanes = mask.shape
    step = 16 if dates % 16 == 0 else dates
    return pl.pallas_call(
        flags_kernel,
        grid=(dates // step,),
        in_specs=[pl.BlockSpec((step, blocks, chunks, lanes), lambda t: (t, 0, 0, 0))],
        out_specs=[pl.BlockSpec((step, chunks, lanes), lambda t: (t, 0, 0))] * pieces,
        out_shape=[jax.ShapeDtypeStruct((dates, chunks, lanes), jnp.bfloat16)] * pieces,
        compiler_params=params(),
        name="cast_flags",
    )(mask)


def box_kernel(
    ks, x_ref, top_ref, bottom_ref, *refs
):
    code_refs = refs[: len(ks)]
    ratio_refs = refs[len(ks) : 2 * len(ks)]
    band, edges, scale, sums = refs[2 * len(ks) :]
    step = pl.program_id(0)
    d = lax.axis_index("date")
    r = lax.axis_index("row")
    dates, pols, rows, cols = x_ref.shape
    quarter = code_refs[0].shape[2]
    tiles = cols // LANES
    half = (d ^ ks[0]) // 2
    span = rows // 2 + 16
    first = pl.multiple_of(half * (rows // 2 - 16), 16)

    @pl.when(step == 0)
    def _():
        near = (
            jnp.abs(
                lax.broadcasted_iota(jnp.int32, (cols, cols), 0)
                - lax.broadcasted_iota(jnp.int32, (cols, cols), 1)
            )
            <= RADIUS
        )
        band[...] = near.astype(f32).astype(jnp.bfloat16)
        for side, ref in enumerate((top_ref, bottom_ref)):
            edge = jnp.dot(ref[...], band[...], preferred_element_type=f32)
            for c in range(tiles):
                edges[side, c] = edge[:, c * LANES : (c + 1) * LANES]
        height = rows * lax.axis_size("row")
        col = edge_count(lax.broadcasted_iota(jnp.int32, (quarter, cols), 1), cols)
        for n, k in enumerate(ks):
            row = edge_count(
                r * rows
                + quarter * (d ^ k)
                + lax.broadcasted_iota(jnp.int32, (quarter, cols), 0),
                height,
            )
            scale[n] = 1.0 / (row * col)
            ratio_refs[n][...] = jnp.zeros_like(ratio_refs[n])

    images = dates * pols
    x = x_ref[:, :, pl.ds(first, span), :].reshape(images * span, cols)
    summed = jnp.dot(x, band[...], preferred_element_type=f32)
    for i in range(images):
        at = (step * images + i) * HALO
        for c in range(tiles):
            lanes = slice(c * LANES, (c + 1) * LANES)
            sums[i, c, 8 : 8 + span] = summed[i * span : (i + 1) * span, lanes]
            sums[i, c, 8 - HALO : 8] = edges[0, c, pl.ds(at, HALO)]
            sums[i, c, 8 + span : 8 + span + HALO] = edges[1, c, pl.ds(at, HALO)]
    for n, k in enumerate(ks):
        q = d ^ k
        base = 8 + half * 16 + quarter * (q % 2)
        for pol in range(pols):
            for c in range(tiles):
                lanes = slice(c * LANES, (c + 1) * LANES)
                total = ratio_refs[n][pol, :, lanes]
                for t in range(dates):
                    i = t * pols + pol
                    window = sums[i, c, pl.ds(base - RADIUS, quarter)]
                    for shift in range(1 - RADIUS, RADIUS + 1):
                        window = window + sums[i, c, pl.ds(base + shift, quarter)]
                    mean = window * scale[n, :, lanes]
                    cells = x_ref[t, pol, pl.ds(pl.multiple_of(quarter * q, 16), quarter), lanes]
                    total = total + cells.astype(f32) / mean
                    code = jnp.log(mean) * CODE_STEPS - 0.5
                    code_refs[n][t, pol, :, lanes] = code.astype(jnp.int32).astype(jnp.int16)
                ratio_refs[n][pol, :, lanes] = total


def box_codes(intensity, top, bottom, ks, quarter):
    dates, pols, rows, cols = intensity.shape
    step = 2 if dates % 2 == 0 else 1
    images = step * pols
    tiles = cols // LANES
    count = len(ks)
    return pl.pallas_call(
        functools.partial(box_kernel, ks),
        grid=(dates // step,),
        in_specs=[
            pl.BlockSpec((step, pols, rows, cols), lambda t: (t, 0, 0, 0)),
            pl.BlockSpec(top.shape, lambda t: (0, 0)),
            pl.BlockSpec(bottom.shape, lambda t: (0, 0)),
        ],
        out_specs=[pl.BlockSpec((step, pols, quarter, cols), lambda t: (t, 0, 0, 0))] * count
        + [pl.BlockSpec((pols, quarter, cols), lambda t: (0, 0, 0))] * count,
        out_shape=[jax.ShapeDtypeStruct((dates, pols, quarter, cols), jnp.int16)] * count
        + [jax.ShapeDtypeStruct((pols, quarter, cols), f32)] * count,
        scratch_shapes=[
            pltpu.VMEM((cols, cols), jnp.bfloat16),
            pltpu.VMEM((2, tiles, dates * pols * HALO, LANES), f32),
            pltpu.VMEM((count, quarter, cols), f32),
            pltpu.VMEM((images, tiles, rows // 2 + 32, LANES), f32),
        ],
        compiler_params=params(),
        name="box_codes",
    )(intensity, top, bottom)


def factor_kernel(chunked, table_ref, *refs):
    piece_refs = refs[:-3]
    flags_ref, factor_ref, lines = refs[-3:]
    r = lax.axis_index("row")
    dates, quarter, cols = flags_ref.shape
    tiles = cols // LANES
    for k, piece_ref in enumerate(piece_refs):
        chunks = piece_ref.shape[1]
        at = pl.multiple_of((r ^ k) * chunks, 16) if chunked else 0
        lines[:, pl.ds(at, chunks)] = piece_ref[...].astype(f32)
    for h in range(quarter // 8):
        down = slice(h * 8, (h + 1) * 8)

        def add_date(t, totals):
            new = []
            for c in range(tiles):
                flag = lines[t, pl.ds(h * 8 * tiles + c, 8, stride=tiles)]
                flags_ref[t, down, c * LANES : (c + 1) * LANES] = flag
                new.append(totals[c * HARMONICS] + flag)
                for n in range(1, HARMONICS):
                    new.append(totals[c * HARMONICS + n] + flag * table_ref[n, t])
            return tuple(new)

        zero = jnp.zeros((8, LANES), f32)
        totals = lax.fori_loop(0, dates, add_date, (zero,) * (tiles * HARMONICS), unroll=4)
        for c in range(tiles):
            lanes = slice(c * LANES, (c + 1) * LANES)
            m0, c1, s1, c2, s2, c3, s3, c4, s4 = totals[c * HARMONICS : (c + 1) * HARMONICS]
            normal = {
                (0, 0): 2.0 * m0 + NOISE,
                (1, 0): 2.0 * c1,
                (2, 0): 2.0 * s1,
                (3, 0): 2.0 * c2,
                (4, 0): 2.0 * s2,
                (1, 1): m0 + c2 + NOISE,
                (2, 1): s2,
                (3, 1): c1 + c3,
                (4, 1): s1 + s3,
                (2, 2): m0 - c2 + NOISE,
                (3, 2): s3 - s1,
                (4, 2): c1 - c3,
                (3, 3): m0 + c4 + NOISE,
                (4, 3): s4,
                (4, 4): m0 - c4 + NOISE,
                (5, 0): m0,
                (5, 1): c1,
                (5, 2): s1,
                (5, 3): c2,
                (5, 4): s2,
                (5, 5): m0 + NOISE,
            }
            lower = {}
            inverse = {}
            for i in range(STATES):
                for j in range(i + 1):
                    total = normal[i, j]
                    for k in range(j):
                        total = total - lower[i, k] * lower[j, k]
                    if i == j:
                        inverse[i] = 1.0 / jnp.sqrt(total)
                    else:
                        lower[i, j] = total * inverse[j]
            planes = [lower[p] for p in PAIRS] + [inverse[i] for i in range(STATES)]
            planes += [m0, c1, s1, c2, s2]
            for n, plane in enumerate(planes):
                factor_ref[n, down, lanes] = plane


PLANES = len(PAIRS) + STATES + STATES - 1


def factor(table, pieces, quarter, cols):
    dates = pieces[0].shape[0]
    return pl.pallas_call(
        functools.partial(factor_kernel, len(pieces) > 1),
        in_specs=[scalars()] + [whole()] * len(pieces),
        out_specs=[whole()] * 2,
        out_shape=[
            jax.ShapeDtypeStruct((dates, quarter, cols), f32),
            jax.ShapeDtypeStruct((PLANES, quarter, cols), f32),
        ],
        scratch_shapes=[pltpu.VMEM((dates, quarter * cols // LANES, LANES), f32)],
        compiler_params=params(),
        name="factor",
    )(table, *pieces)


def right_sums(ks, table_ref, flags_ref, code_refs, lanes):
    d = lax.axis_index("date")
    quarter = flags_ref.shape[1]
    sums = [jnp.zeros((quarter, LANES), f32) for _ in range(STATES)]
    for k, code_ref in zip(ks, code_refs):
        dates = code_ref.shape[0]
        for t in range(dates):
            at = (d ^ k) * dates + t
            flag = flags_ref[at, :, lanes]
            vv = code_ref[t, 0, :, lanes].astype(jnp.int32).astype(f32)
            vh = code_ref[t, 1, :, lanes].astype(jnp.int32).astype(f32) * flag
            both = vv * flag + vh
            sums[0] = sums[0] + both
            for n in range(1, STATES - 1):
                sums[n] = sums[n] + both * table_ref[n, at]
            sums[STATES - 1] = sums[STATES - 1] + vh
    return sums


def right_kernel(ks, table_ref, flags_ref, *refs):
    code_refs, out_ref = refs[:-1], refs[-1]
    for c in range(flags_ref.shape[2] // LANES):
        lanes = slice(c * LANES, (c + 1) * LANES)
        for n, total in enumerate(right_sums(ks, table_ref, flags_ref, code_refs, lanes)):
            out_ref[n, :, lanes] = total


def right_part(table, flags, codes, ks):
    dates, quarter, cols = flags.shape
    return pl.pallas_call(
        functools.partial(right_kernel, ks),
        in_specs=[scalars()] + [whole()] * (1 + len(codes)),
        out_specs=whole(),
        out_shape=jax.ShapeDtypeStruct((STATES, quarter, cols), f32),
        compiler_params=params(),
        name="right_part",
    )(table, flags, *codes)


def solve_kernel(ks, ratios, pieces, table_ref, flags_ref, factor_ref, part_ref, *refs):
    code_refs = refs[: len(ks)]
    ratio_refs = refs[len(ks) : len(ks) + ratios]
    out_refs = refs[len(ks) + ratios : -1]
    lines = refs[-1]
    r = lax.axis_index("row")
    dates, quarter, cols = flags_ref.shape
    tiles = cols // LANES
    for c in range(tiles):
        lanes = slice(c * LANES, (c + 1) * LANES)
        sums = right_sums(ks, table_ref, flags_ref, code_refs, lanes)
        logs = []
        for pol in range(2):
            total = ratio_refs[0][pol, :, lanes]
            for ratio_ref in ratio_refs[1:]:
                total = total + ratio_ref[pol, :, lanes]
            logs.append(jnp.log(total * (1.0 / dates)))
        bases = [factor_ref[len(PAIRS) + STATES + n, :, lanes] for n in range(STATES - 1)]
        right = [
            (sums[n] + part_ref[n, :, lanes]) * (1.0 / CODE_STEPS) for n in range(STATES)
        ]
        both = logs[0] + logs[1]
        for n in range(STATES - 1):
            right[n] = right[n] + both * bases[n]
        right[STATES - 1] = right[STATES - 1] + logs[1] * bases[0]
        lower = {p: factor_ref[n, :, lanes] for n, p in enumerate(PAIRS)}
        inverse = [factor_ref[len(PAIRS) + n, :, lanes] for n in range(STATES)]
        middle = []
        for i in range(STATES):
            total = right[i]
            for k in range(i):
                total = total - lower[i, k] * middle[k]
            middle.append(total * inverse[i])
        solved = [None] * STATES
        for i in reversed(range(STATES)):
            total = middle[i]
            for k in range(i + 1, STATES):
                total = total - lower[k, i] * solved[k]
            solved[i] = total * inverse[i]
        for n in range(STATES):
            for h in range(quarter // 8):
                lines[n, pl.ds(h * 8 * tiles + c, 8, stride=tiles)] = solved[n][
                    h * 8 : (h + 1) * 8
                ]
    for k, out_ref in enumerate(out_refs):
        chunks = out_ref.shape[1]
        at = pl.multiple_of((r ^ k) * chunks, 8) if pieces > 1 else 0
        out_ref[...] = lines[:, pl.ds(at, chunks)]


def solve(table, flags, factors, part, codes, ratios, ks, pieces):
    dates, quarter, cols = flags.shape
    chunks = quarter * cols // LANES
    return pl.pallas_call(
        functools.partial(solve_kernel, ks, len(ratios), pieces),
        in_specs=[scalars()] + [whole()] * (3 + len(codes) + len(ratios)),
        out_specs=[whole()] * pieces,
        out_shape=[jax.ShapeDtypeStruct((STATES, chunks // pieces, LANES), f32)] * pieces,
        scratch_shapes=[pltpu.VMEM((STATES, chunks, LANES), f32)],
        compiler_params=params(),
        name="solve",
    )(table, flags, factors, part, *codes, *ratios)


def gather_kernel(*refs):
    r = lax.axis_index("row")
    for k, in_ref in enumerate(refs[:-1]):
        refs[-1][:, r ^ k] = in_ref[...]


def gather_states(parts):
    states, chunks, lanes = parts[0].shape
    return pl.pallas_call(
        gather_kernel,
        in_specs=[whole()] * len(parts),
        out_specs=whole(),
        out_shape=jax.ShapeDtypeStruct((states, len(parts), chunks, lanes), f32),
        compiler_params=params(),
        name="gather_states",
    )(*parts)


def harmonics(day_index):
    phase = day_index.astype(f32) * (2.0 * math.pi / 365.0)
    row = lax.broadcasted_iota(jnp.int32, (HARMONICS, day_index.shape[0]), 0)
    angle = ((row + 1) // 2).astype(f32) * phase[None, :]
    return jnp.where(row % 2 == 1, jnp.cos(angle), jnp.where(row == 0, 1.0, jnp.sin(angle)))


def body(intensity, valid_mask, day_index):
    rows, cols = intensity.shape[2:]
    date_devices = lax.axis_size("date")
    row_devices = lax.axis_size("row")
    quarter = rows // date_devices
    all_dates = valid_mask.shape[0]
    segment = quarter * cols // row_devices
    chunks = segment // LANES
    direct = row_devices in (2, 4) and chunks % 16 == 0

    edges = [
        cells.reshape(-1, cols)
        for cells in (intensity[:, :, rows - HALO :], intensity[:, :, :HALO])
    ]
    ring = range(row_devices - 1)
    top = lax.ppermute(edges[0], "row", [(i, i + 1) for i in ring])
    bottom = lax.ppermute(edges[1], "row", [(i + 1, i) for i in ring])

    if direct:
        lines = valid_mask.reshape(all_dates, row_devices, chunks, LANES)
        flags = cast_flags(lines, row_devices)
        flags = [flags[0]] + [
            lax.ppermute(flags[k], "row", partners(row_devices, k)) for k in range(1, row_devices)
        ]
    else:
        moved = lax.all_to_all(
            valid_mask.astype(jnp.bfloat16), "row", split_axis=1, concat_axis=2, tiled=True
        )
        flags = [moved.reshape(all_dates, row_devices * chunks, LANES)]

    table = harmonics(day_index)

    far = box_codes(intensity, top, bottom, (2, 3), quarter)
    moved_codes = {}
    moved_ratios = {}
    for n, k in enumerate((2, 3)):
        moved_ratios[k] = lax.ppermute(far[2 + n], "date", partners(date_devices, k))
        moved_codes[k] = lax.ppermute(far[n], "date", partners(date_devices, k))
    near = box_codes(intensity, top, bottom, (0, 1), quarter)
    moved_codes[0], moved_ratios[0] = near[0], near[2]
    moved_codes[1] = lax.ppermute(near[1], "date", partners(date_devices, 1))
    moved_ratios[1] = lax.ppermute(near[3], "date", partners(date_devices, 1))

    image_flags, factors = factor(table, flags, quarter, cols)
    part = right_part(table, image_flags, [moved_codes[0], moved_codes[1]], (0, 1))
    pieces = row_devices if direct else 1
    states = solve(
        table,
        image_flags,
        factors,
        part,
        [moved_codes[2], moved_codes[3]],
        [moved_ratios[k] for k in range(date_devices)],
        (2, 3),
        pieces,
    )
    if direct:
        states = [states[0]] + [
            lax.ppermute(states[k], "row", partners(row_devices, k)) for k in range(1, row_devices)
        ]
        return gather_states(states).reshape(STATES, row_devices, 1, segment)
    states = states[0].reshape(STATES, 1, row_devices, segment)
    return lax.all_to_all(states, "row", split_axis=2, concat_axis=1, tiled=True)


def solution(mesh):
    return jax.shard_map(
        body,
        mesh=mesh,
        in_specs=(
            P("date", None, ("tile", "row"), None),
            P(None, "tile", ("date", "row"), None),
            P(),
        ),
        out_specs=P(None, "tile", ("date", "row"), None),
        check_vma=False,
    )
```

time: 144 us -> 64.7 us (0.45)
  waiting for transfers between devices: 55.4 us -> 24.6 us
  other arithmetic: 23.1 us -> 0.14 us
  Pallas kernels: 0 us -> 16.5 us
  between operations: 13.6 us -> 0.13 us
  local copies, waits for them, and re-layouts: 16.4 us -> 2.95 us
  blocking collectives: 11.9 us -> 0 us
  matrix products: 5.86 us -> 0 us
  starting transfers between devices: 17.6 us -> 20.1 us
    psum x1 -> x0, waiting for transfers between devices: 33.6 us -> none  [body(): ratio_total = lax.psum(partial_sum, 'date')]
    ppermute x2 -> x14, waiting for transfers between devices: 0.01 us -> 24.6 us  [the longest x2 10.7 us: body(): lax.ppermute(far[2 + n], 'date', partners(date_devices, k))]
    all_to_all x2 -> x0, waiting for transfers between devices: 21.8 us -> none  [the longest x1 21.8 us: body(): lax.all_to_all(blocks_out, 'date', split_axis=2, concat_axis=0, tiled=True)]
    pallas_call x0 -> x7, Pallas kernels: none -> 16.5 us  [the longest x2 8.64 us: box_codes(): pl.pallas_call(functools.partial(box_kernel, ks), grid=(dates // step,),...]
    ppermute x2 -> x14, starting transfers between devices: 6.87 us -> 20.1 us  [the longest x3 5.3 us: body(): lax.ppermute(flags[k], 'row', partners(row_devices, k))]
    all_to_all x1 -> x0, blocking collectives: 11.9 us -> none  [body(): lax.all_to_all(state_rows, 'row', split_axis=2, concat_axis=1, tiled=True)]
    all_to_all x2 -> x0, starting transfers between devices: 10.8 us -> none  [the longest x1 5.94 us: body(): lax.all_to_all(mask_wire, 'row', split_axis=1, concat_axis=2, tiled=True)]
    unnamed x2 -> x0, other arithmetic: 10.2 us -> none
  transfers between devices with their start and end apart: 5 -> 14, of which waited for: 2 -> 5; matrix products, arithmetic and copies ran while one was open for 24% -> 0% of each run, Pallas kernels for 0% -> 22%
where the time goes in v1:
time: 64.7 us; the launch traced here: 64.5 us
  waiting for transfers between devices  24.6 us (38%)
  starting transfers between devices  20.1 us (31%)
  Pallas kernels  16.5 us (26%)
  local copies, waits for them, and re-layouts  2.95 us (5%)
    ppermute x2, waiting for transfers between devices, body(): lax.ppermute(far[2 + n], 'date', partners(date_devices, k))  10.7 us
    pallas_call x2, Pallas kernels, box_codes(): pl.pallas_call(functools.partial(box_kernel, ks), grid=(dates // step,),...  8.64 us
    ppermute x3, waiting for transfers between devices, body(): lax.ppermute(flags[k], 'row', partners(row_devices, k))  8.05 us
    ppermute x3, waiting for transfers between devices, body(): lax.ppermute(states[k], 'row', partners(row_devices, k))  5.88 us
    ppermute x3, starting transfers between devices, body(): lax.ppermute(flags[k], 'row', partners(row_devices, k))  5.3 us
    ppermute x1, starting transfers between devices, body(): top = lax.ppermute(edges[0], 'row', [(i, i + 1) for i in ring])  4.94 us
    ppermute x3, starting transfers between devices, body(): lax.ppermute(states[k], 'row', partners(row_devices, k))  4.45 us
    pallas_call x1, Pallas kernels, factor(): pl.pallas_call(functools.partial(factor_kernel, len(pieces) > 1), in_spec...  3.92 us
  transfers between devices with their start and end apart: 14, of which 5 were waited for; matrix products, arithmetic and copies ran while one was open for 0% of the time, Pallas kernels for 22%

profile of v1, /device:TPU:0, one launch (start us, length us, event | category | flops | bytes accessed | tf_op | source)
XLA Modules:
  0.0 64.5 jit_solution(8338468018674687739)
XLA Ops:
  0.0 0.0 copy-start
  0.0 1.3 %fusion = (bf16[16,2,4,512]{3,2,1,0:T(4,128)(2,1)S(1)}, bf16[16,2,4,512]{3,2,1,0:T(4,128)(2,1)S(1)}) fusion(bf16[16,2,64,512]{3,2,1,0:T(8,128)(2,1)} %x_ref.3), kind=kLoop, calls=%fused_computation.13 | loop fusion | bytes 524288 | tf_op jit(solution)/shard_map/slice | solution.py:394
  1.3 4.9 %collective-permute-start.3 = (bf16[128,512]{1,0:T(8,128)(2,1)S(1)}, bf16[128,512]{1,0:T(8,128)(2,1)S(1)}, u32[]{:S(2)}, u32[]{:S(2)}) collective-permute-start(bf16[128,512]{1,0:T(8,128)(2,1)S(1)} %reshape.14), channel_id=1, source_target_pairs={{0,1},{1,2},{2,3},{4,5},{5,6},{6,7},{8,9},{9,10},{10,11},{12,13},{... | collective-permute-start | bytes 393224 | tf_op jit(solution)/shard_map/ppermute | solution.py:397
  6.3 1.3 %collective-permute-start.4 = (bf16[128,512]{1,0:T(8,128)(2,1)S(1)}, bf16[128,512]{1,0:T(8,128)(2,1)S(1)}, u32[]{:S(2)}, u32[]{:S(2)}) collective-permute-start(bf16[128,512]{1,0:T(8,128)(2,1)S(1)} %reshape.15), channel_id=1, source_target_pairs={{1,0},{2,1},{3,2},{5,4},{6,5},{7,6},{9,8},{10,9},{11,10},{13,12},{... | collective-permute-start | bytes 393224 | tf_op jit(solution)/shard_map/ppermute | solution.py:398
  7.6 0.0 copy-start.1
  7.6 1.6 %copy-done.1 = s32[64,4,1,2048]{3,2,1,0:T(1,128)S(1)} copy-done((s32[64,4,1,2048]{3,2,1,0:T(1,128)S(1)}, s32[64,4,1,2048]{3,2,1,0:T(1,128)}, u32[]{:S(2)}) %copy-start.1) | copy-done | bytes 2097176
  9.2 0.2 cast_flags.1
  9.4 2.7 %collective-permute-start = (bf16[64,16,128]{2,1,0:T(8,128)(2,1)S(1)}, bf16[64,16,128]{2,1,0:T(8,128)(2,1)S(1)}, u32[]{:S(2)}, u32[]{:S(2)}) collective-permute-start(bf16[64,16,128]{2,1,0:T(8,128)(2,1)S(1)} %get-tuple-element.24), channel_id=1, source_target_pairs={{0,1},{1,0},{2,3},{3,2},{4,5},{5,4},{6,7},{7,6},{8,9},{9,8},{10,11... | collective-permute-start | bytes 786440 | tf_op jit(solution)/shard_map/ppermute | solution.py:404
  12.1 2.6 %collective-permute-start.1 = (bf16[64,16,128]{2,1,0:T(8,128)(2,1)S(1)}, bf16[64,16,128]{2,1,0:T(8,128)(2,1)S(1)}, u32[]{:S(2)}, u32[]{:S(2)}) collective-permute-start(bf16[64,16,128]{2,1,0:T(8,128)(2,1)S(1)} %get-tuple-element.25), channel_id=1, source_target_pairs={{0,2},{1,3},{2,0},{3,1},{4,6},{5,7},{6,4},{7,5},{8,10},{9,11},{10,... | collective-permute-start | bytes 786440 | tf_op jit(solution)/shard_map/ppermute | solution.py:404
  14.7 0.0 collective-permute-start.2
  14.7 0.0 copy-start.2
  14.7 0.0 collective-permute-done.3.top_ref
  14.7 0.0 collective-permute-done.4.bottom_ref
  14.7 0.0 copy-done
  14.8 4.3 %box_codes.2 = (s16[16,2,16,512]{3,2,1,0:T(8,128)(2,1)S(1)}, s16[16,2,16,512]{3,2,1,0:T(8,128)(2,1)S(1)}, f32[2,16,512]{2,1,0:T(8,128)S(1)}, f32[2,16,512]{2,1,0:T(8,128)S(1)}) custom-call(bf16[16,2,64,512]{3,2,1,0:T(8,128)(2,1)S(1)} %copy-done, bf16[128,512]{1,0:T(8,128)(2,1)S(1)} %collective-permute-done.3.top_ref, ...), custom_call_target="tpu_custom_call" | custom-call | tf_op jit(solution)/shard_map/box_codes/pallas_call | solution.py:144
  19.1 0.1 collective-permute-start.5
  19.2 4.3 %box_codes.3 = (s16[16,2,16,512]{3,2,1,0:T(8,128)(2,1)S(1)}, s16[16,2,16,512]{3,2,1,0:T(8,128)(2,1)S(1)}, f32[2,16,512]{2,1,0:T(8,128)S(1)}, f32[2,16,512]{2,1,0:T(8,128)S(1)}) custom-call(bf16[16,2,64,512]{3,2,1,0:T(8,128)(2,1)S(1)} %copy-done, bf16[128,512]{1,0:T(8,128)(2,1)S(1)} %collective-permute-done.3.top_ref, ...), custom_call_target="tpu_custom_call" | custom-call | tf_op jit(solution)/shard_map/box_codes/pallas_call | solution.py:144
  23.5 1.6 %collective-permute-start.6 = (s16[16,2,16,512]{3,2,1,0:T(8,128)(2,1)S(1)}, s16[16,2,16,512]{3,2,1,0:T(8,128)(2,1)S(1)}, u32[]{:S(2)}, u32[]{:S(2)}) collective-permute-start(s16[16,2,16,512]{3,2,1,0:T(8,128)(2,1)S(1)} %get-tuple-element.31), channel_id=1, source_target_pairs={{0,8},{4,12},{8,0},{12,4},{1,9},{5,13},{9,1},{13,5},{2,10},{6,14},... | collective-permute-start | bytes 1572872 | tf_op jit(solution)/shard_map/ppermute | solution.py:419
  25.1 0.0 collective-permute-done.refs_1_
  25.1 0.4 collective-permute-start.7
  25.5 0.0 copy-done.2
  25.5 8.0 %collective-permute-done.1.refs_2_ = bf16[64,16,128]{2,1,0:T(8,128)(2,1)S(1)} collective-permute-done((bf16[64,16,128]{2,1,0:T(8,128)(2,1)S(1)}, bf16[64,16,128]{2,1,0:T(8,128)(2,1)S(1)}, u32[]{:S(2)}, u32[]{:S(2)}) %collective-permute-start.1) | collective-permute-done | bytes 262176 | tf_op jit(solution)/shard_map/ppermute | solution.py:404
  33.5 0.0 collective-permute-start.10
  33.5 0.0 collective-permute-done.2.refs_3_
  33.5 1.6 %collective-permute-start.8 = (f32[2,16,512]{2,1,0:T(8,128)S(1)}, f32[2,16,512]{2,1,0:T(8,128)S(1)}, u32[]{:S(2)}, u32[]{:S(2)}) collective-permute-start(f32[2,16,512]{2,1,0:T(8,128)S(1)} %get-tuple-element.34), channel_id=1, source_target_pairs={{0,4},{4,0},{8,12},{12,8},{1,5},{5,1},{9,13},{13,9},{2,6},{6,2},{1... | collective-permute-start | bytes 196616 | tf_op jit(solution)/shard_map/ppermute | solution.py:423
  35.1 0.0 collective-permute-done.5.refs_1_
  35.1 0.5 collective-permute-start.9
  35.7 0.1 select_select_fusion.table_ref
  35.8 3.9 %factor.1 = (f32[64,16,512]{2,1,0:T(8,128)S(1)}, f32[26,16,512]{2,1,0:T(8,128)S(1)}) custom-call(f32[9,64]{1,0:T(8,128)S(1)} %select_select_fusion.table_ref, bf16[64,16,128]{2,1,0:T(8,128)(2,1)S(1)} %get-tuple-element.23.refs_0_, bf16[64,16,128]{2,1,0:T(8,128)(2,1)S(1)} %collective-permute-done.refs_1_, ...), custom_call_target="tpu_custom_call" | custom-call | tf_op jit(solution)/shard_map/factor/pallas_call | solution.py:240
  39.7 1.6 %right_part.1.part_ref = f32[6,16,512]{2,1,0:T(8,128)S(1)} custom-call(f32[9,64]{1,0:T(8,128)S(1)} %select_select_fusion.table_ref, f32[64,16,512]{2,1,0:T(8,128)S(1)} %get-tuple-element.27.flags_ref, s16[16,2,16,512]{3,2,1,0:T(8,128)(2,1)S(1)} %get-tuple-element.29.refs_0_, s16[16,2,16,512]{3,2,1,0:T(8,128)(2,1)S(1)} %collective-permute-done.5.refs_1_), custom_call_target="tpu_custom_call" | custom-call | tf_op jit(solution)/shard_map/right_part/pallas_call | solution.py:283
  41.3 8.9 %collective-permute-done.10.refs_5_ = f32[2,16,512]{2,1,0:T(8,128)S(1)} collective-permute-done((f32[2,16,512]{2,1,0:T(8,128)S(1)}, f32[2,16,512]{2,1,0:T(8,128)S(1)}, u32[]{:S(2)}, u32[]{:S(2)}) %collective-permute-start.10) | collective-permute-done | bytes 65568 | tf_op jit(solution)/shard_map/ppermute | solution.py:418
  50.2 0.0 collective-permute-done.8.refs_3_
  50.2 1.8 %collective-permute-done.9.refs_4_ = f32[2,16,512]{2,1,0:T(8,128)S(1)} collective-permute-done((f32[2,16,512]{2,1,0:T(8,128)S(1)}, f32[2,16,512]{2,1,0:T(8,128)S(1)}, u32[]{:S(2)}, u32[]{:S(2)}) %collective-permute-start.9) | collective-permute-done | bytes 65568 | tf_op jit(solution)/shard_map/ppermute | solution.py:418
  52.0 0.0 collective-permute-done.6.refs_0_
  52.0 0.0 collective-permute-done.7.refs_1_
  52.0 1.5 %solve.1 = (f32[6,16,128]{2,1,0:T(8,128)S(1)}, f32[6,16,128]{2,1,0:T(8,128)S(1)}, f32[6,16,128]{2,1,0:T(8,128)S(1)}, f32[6,16,128]{2,1,0:T(8,128)S(1)}) custom-call(f32[9,64]{1,0:T(8,128)S(1)} %select_select_fusion.table_ref, f32[64,16,512]{2,1,0:T(8,128)S(1)} %get-tuple-element.27.flags_ref, f32[26,16,512]{2,1,0:T(8,128)S(1)} %get-tuple-element.28.factor_ref, ...), custom_call_target="tpu_custom_call" | custom-call | tf_op jit(solution)/shard_map/solve/pallas_call | solution.py:346
  53.5 1.0 %collective-permute-start.11 = (f32[6,16,128]{2,1,0:T(8,128)S(1)}, f32[6,16,128]{2,1,0:T(8,128)S(1)}, u32[]{:S(2)}, u32[]{:S(2)}) collective-permute-start(f32[6,16,128]{2,1,0:T(8,128)S(1)} %get-tuple-element.38), channel_id=1, source_target_pairs={{0,1},{1,0},{2,3},{3,2},{4,5},{5,4},{6,7},{7,6},{8,9},{9,8},{10,11... | collective-permute-start | bytes 147464 | tf_op jit(solution)/shard_map/ppermute | solution.py:440
  54.5 3.5 %collective-permute-start.12 = (f32[6,16,128]{2,1,0:T(8,128)S(1)}, f32[6,16,128]{2,1,0:T(8,128)S(1)}, u32[]{:S(2)}, u32[]{:S(2)}) collective-permute-start(f32[6,16,128]{2,1,0:T(8,128)S(1)} %get-tuple-element.39), channel_id=1, source_target_pairs={{0,2},{1,3},{2,0},{3,1},{4,6},{5,7},{6,4},{7,5},{8,10},{9,11},{10,... | collective-permute-start | bytes 147464 | tf_op jit(solution)/shard_map/ppermute | solution.py:440
  57.9 0.0 collective-permute-start.13
  58.0 0.0 collective-permute-done.11.refs_1_
  58.0 3.1 %collective-permute-done.12.refs_2_ = f32[6,16,128]{2,1,0:T(8,128)S(1)} collective-permute-done((f32[6,16,128]{2,1,0:T(8,128)S(1)}, f32[6,16,128]{2,1,0:T(8,128)S(1)}, u32[]{:S(2)}, u32[]{:S(2)}) %collective-permute-start.12) | collective-permute-done | bytes 49184 | tf_op jit(solution)/shard_map/ppermute | solution.py:440
  61.0 2.8 %collective-permute-done.13.refs_3_ = f32[6,16,128]{2,1,0:T(8,128)S(1)} collective-permute-done((f32[6,16,128]{2,1,0:T(8,128)S(1)}, f32[6,16,128]{2,1,0:T(8,128)S(1)}, u32[]{:S(2)}, u32[]{:S(2)}) %collective-permute-start.13) | collective-permute-done | bytes 49184 | tf_op jit(solution)/shard_map/ppermute | solution.py:440
  63.8 0.7 %gather_states.1 = f32[6,4,16,128]{3,2,1,0:T(8,128)} custom-call(f32[6,16,128]{2,1,0:T(8,128)S(1)} %get-tuple-element.37.refs_0_, f32[6,16,128]{2,1,0:T(8,128)S(1)} %collective-permute-done.11.refs_1_, f32[6,16,128]{2,1,0:T(8,128)S(1)} %collective-permute-done.12.refs_2_, f32[6,16,128]{2,1,0:T(8,128)S(1)} %collective-permute-done.13.refs_3_), custom_call_target="tpu_custom_call" | custom-call | tf_op jit(solution)/shard_map/gather_states/pallas_call | solution.py:365
  (7 shorter events, 0.1 us)
Async XLA Ops:
  0.0 14.7 %copy-start = (bf16[16,2,64,512]{3,2,1,0:T(8,128)(2,1)S(1)}, bf16[16,2,64,512]{3,2,1,0:T(8,128)(2,1)}, u32[]{:S(2)}) copy-start(bf16[16,2,64,512]{3,2,1,0:T(8,128)(2,1)} %x_ref.3) | copy-start | bytes 6291460
  1.3 13.4 %collective-permute-start.3 = (bf16[128,512]{1,0:T(8,128)(2,1)S(1)}, bf16[128,512]{1,0:T(8,128)(2,1)S(1)}, u32[]{:S(2)}, u32[]{:S(2)}) collective-permute-start(bf16[128,512]{1,0:T(8,128)(2,1)S(1)} %reshape.14), channel_id=1, source_target_pairs={{0,1},{1,2},{2,3},{4,5},{5,6},{6,7},{8,9},{9,10},{10,11},{12,13},{... | collective-permute-start | bytes 393224 | tf_op jit(solution)/shard_map/ppermute | solution.py:397
  6.3 8.4 %collective-permute-start.4 = (bf16[128,512]{1,0:T(8,128)(2,1)S(1)}, bf16[128,512]{1,0:T(8,128)(2,1)S(1)}, u32[]{:S(2)}, u32[]{:S(2)}) collective-permute-start(bf16[128,512]{1,0:T(8,128)(2,1)S(1)} %reshape.15), channel_id=1, source_target_pairs={{1,0},{2,1},{3,2},{5,4},{6,5},{7,6},{9,8},{10,9},{11,10},{13,12},{... | collective-permute-start | bytes 393224 | tf_op jit(solution)/shard_map/ppermute | solution.py:398
  7.6 1.6 %copy-start.1 = (s32[64,4,1,2048]{3,2,1,0:T(1,128)S(1)}, s32[64,4,1,2048]{3,2,1,0:T(1,128)}, u32[]{:S(2)}) copy-start(s32[64,4,1,2048]{3,2,1,0:T(1,128)} %param.4) | copy-start | bytes 6291460
  9.4 15.7 %collective-permute-start = (bf16[64,16,128]{2,1,0:T(8,128)(2,1)S(1)}, bf16[64,16,128]{2,1,0:T(8,128)(2,1)S(1)}, u32[]{:S(2)}, u32[]{:S(2)}) collective-permute-start(bf16[64,16,128]{2,1,0:T(8,128)(2,1)S(1)} %get-tuple-element.24), channel_id=1, source_target_pairs={{0,1},{1,0},{2,3},{3,2},{4,5},{5,4},{6,7},{7,6},{8,9},{9,8},{10,11... | collective-permute-start | bytes 786440 | tf_op jit(solution)/shard_map/ppermute | solution.py:404
  12.1 21.4 %collective-permute-start.1 = (bf16[64,16,128]{2,1,0:T(8,128)(2,1)S(1)}, bf16[64,16,128]{2,1,0:T(8,128)(2,1)S(1)}, u32[]{:S(2)}, u32[]{:S(2)}) collective-permute-start(bf16[64,16,128]{2,1,0:T(8,128)(2,1)S(1)} %get-tuple-element.25), channel_id=1, source_target_pairs={{0,2},{1,3},{2,0},{3,1},{4,6},{5,7},{6,4},{7,5},{8,10},{9,11},{10,... | collective-permute-start | bytes 786440 | tf_op jit(solution)/shard_map/ppermute | solution.py:404
  14.7 18.8 %collective-permute-start.2 = (bf16[64,16,128]{2,1,0:T(8,128)(2,1)S(1)}, bf16[64,16,128]{2,1,0:T(8,128)(2,1)S(1)}, u32[]{:S(2)}, u32[]{:S(2)}) collective-permute-start(bf16[64,16,128]{2,1,0:T(8,128)(2,1)S(1)} %get-tuple-element.26), channel_id=1, source_target_pairs={{0,3},{1,2},{2,1},{3,0},{4,7},{5,6},{6,5},{7,4},{8,11},{9,10},{10,... | collective-permute-start | bytes 786440 | tf_op jit(solution)/shard_map/ppermute | solution.py:404
  14.7 10.7 %copy-start.2 = (s32[64]{0:T(128)S(1)}, s32[64]{0:T(128)}, u32[]{:S(2)}) copy-start(s32[64]{0:T(128)} %param.5) | copy-start | bytes 772
  19.1 16.0 %collective-permute-start.5 = (s16[16,2,16,512]{3,2,1,0:T(8,128)(2,1)S(1)}, s16[16,2,16,512]{3,2,1,0:T(8,128)(2,1)S(1)}, u32[]{:S(2)}, u32[]{:S(2)}) collective-permute-start(s16[16,2,16,512]{3,2,1,0:T(8,128)(2,1)S(1)} %get-tuple-element.30), channel_id=1, source_target_pairs={{0,4},{4,0},{8,12},{12,8},{1,5},{5,1},{9,13},{13,9},{2,6},{6,2},{1... | collective-permute-start | bytes 1572872 | tf_op jit(solution)/shard_map/ppermute | solution.py:422
  23.5 28.5 %collective-permute-start.6 = (s16[16,2,16,512]{3,2,1,0:T(8,128)(2,1)S(1)}, s16[16,2,16,512]{3,2,1,0:T(8,128)(2,1)S(1)}, u32[]{:S(2)}, u32[]{:S(2)}) collective-permute-start(s16[16,2,16,512]{3,2,1,0:T(8,128)(2,1)S(1)} %get-tuple-element.31), channel_id=1, source_target_pairs={{0,8},{4,12},{8,0},{12,4},{1,9},{5,13},{9,1},{13,5},{2,10},{6,14},... | collective-permute-start | bytes 1572872 | tf_op jit(solution)/shard_map/ppermute | solution.py:419
  25.1 26.9 %collective-permute-start.7 = (s16[16,2,16,512]{3,2,1,0:T(8,128)(2,1)S(1)}, s16[16,2,16,512]{3,2,1,0:T(8,128)(2,1)S(1)}, u32[]{:S(2)}, u32[]{:S(2)}) collective-permute-start(s16[16,2,16,512]{3,2,1,0:T(8,128)(2,1)S(1)} %get-tuple-element.32), channel_id=1, source_target_pairs={{0,12},{4,8},{8,4},{12,0},{1,13},{5,9},{9,5},{13,1},{2,14},{6,10},... | collective-permute-start | bytes 1572872 | tf_op jit(solution)/shard_map/ppermute | solution.py:419
  33.5 16.7 %collective-permute-start.10 = (f32[2,16,512]{2,1,0:T(8,128)S(1)}, f32[2,16,512]{2,1,0:T(8,128)S(1)}, u32[]{:S(2)}, u32[]{:S(2)}) collective-permute-start(f32[2,16,512]{2,1,0:T(8,128)S(1)} %get-tuple-element.36), channel_id=1, source_target_pairs={{0,12},{4,8},{8,4},{12,0},{1,13},{5,9},{9,5},{13,1},{2,14},{6,10},... | collective-permute-start | bytes 196616 | tf_op jit(solution)/shard_map/ppermute | solution.py:418
  33.5 16.7 %collective-permute-start.8 = (f32[2,16,512]{2,1,0:T(8,128)S(1)}, f32[2,16,512]{2,1,0:T(8,128)S(1)}, u32[]{:S(2)}, u32[]{:S(2)}) collective-permute-start(f32[2,16,512]{2,1,0:T(8,128)S(1)} %get-tuple-element.34), channel_id=1, source_target_pairs={{0,4},{4,0},{8,12},{12,8},{1,5},{5,1},{9,13},{13,9},{2,6},{6,2},{1... | collective-permute-start | bytes 196616 | tf_op jit(solution)/shard_map/ppermute | solution.py:423
  35.1 16.8 %collective-permute-start.9 = (f32[2,16,512]{2,1,0:T(8,128)S(1)}, f32[2,16,512]{2,1,0:T(8,128)S(1)}, u32[]{:S(2)}, u32[]{:S(2)}) collective-permute-start(f32[2,16,512]{2,1,0:T(8,128)S(1)} %get-tuple-element.35), channel_id=1, source_target_pairs={{0,8},{4,12},{8,0},{12,4},{1,9},{5,13},{9,1},{13,5},{2,10},{6,14},... | collective-permute-start | bytes 196616 | tf_op jit(solution)/shard_map/ppermute | solution.py:418
  53.5 4.5 %collective-permute-start.11 = (f32[6,16,128]{2,1,0:T(8,128)S(1)}, f32[6,16,128]{2,1,0:T(8,128)S(1)}, u32[]{:S(2)}, u32[]{:S(2)}) collective-permute-start(f32[6,16,128]{2,1,0:T(8,128)S(1)} %get-tuple-element.38), channel_id=1, source_target_pairs={{0,1},{1,0},{2,3},{3,2},{4,5},{5,4},{6,7},{7,6},{8,9},{9,8},{10,11... | collective-permute-start | bytes 147464 | tf_op jit(solution)/shard_map/ppermute | solution.py:440
  54.5 6.6 %collective-permute-start.12 = (f32[6,16,128]{2,1,0:T(8,128)S(1)}, f32[6,16,128]{2,1,0:T(8,128)S(1)}, u32[]{:S(2)}, u32[]{:S(2)}) collective-permute-start(f32[6,16,128]{2,1,0:T(8,128)S(1)} %get-tuple-element.39), channel_id=1, source_target_pairs={{0,2},{1,3},{2,0},{3,1},{4,6},{5,7},{6,4},{7,5},{8,10},{9,11},{10,... | collective-permute-start | bytes 147464 | tf_op jit(solution)/shard_map/ppermute | solution.py:440
  57.9 5.9 %collective-permute-start.13 = (f32[6,16,128]{2,1,0:T(8,128)S(1)}, f32[6,16,128]{2,1,0:T(8,128)S(1)}, u32[]{:S(2)}, u32[]{:S(2)}) collective-permute-start(f32[6,16,128]{2,1,0:T(8,128)S(1)} %get-tuple-element.40), channel_id=1, source_target_pairs={{0,3},{1,2},{2,1},{3,0},{4,7},{5,6},{6,5},{7,4},{8,11},{9,10},{10,... | collective-permute-start | bytes 147464 | tf_op jit(solution)/shard_map/ppermute | solution.py:440

commit v2 on v0

v2 whole, which is shorter than its diff:
```python
import functools
import math

import jax
import jax.numpy as jnp
import numpy as np
from jax import lax
from jax.experimental import pallas as pl
from jax.experimental.pallas import tpu as pltpu
from jax.sharding import PartitionSpec as P

RADIUS = 3
STATES = 6
HALO = 4
GROUP = 8
LANES = 128
HARMONICS = 9
NOISE = 0.05
CODE_STEPS = 8192.0
REST_STEPS = 32768.0
VMEM_BYTES = 16 * 1024 * 1024

SHORT = pl.CostEstimate(flops=1000, bytes_accessed=1000, transcendentals=0)

f32 = jnp.float32
i32 = jnp.int32
PAIRS = [(i, j) for i in range(STATES) for j in range(i)]
PLANES = len(PAIRS) + STATES


def partners(count, k):
    return [(i, i ^ k) for i in range(count)]


def ratio_steps(dates):
    return 2.0 ** math.floor(math.log2(32767 / ((2 * RADIUS + 1) ** 2 * dates)))


def edge_count(positions, length):
    lower = jnp.maximum(positions - RADIUS, 0)
    upper = jnp.minimum(positions + RADIUS, length - 1)
    return (upper - lower + 1).astype(f32)


def whole():
    return pl.BlockSpec(memory_space=pltpu.VMEM)


def anywhere():
    return pl.BlockSpec(memory_space=pl.ANY)


def scalars():
    return pl.BlockSpec(memory_space=pltpu.SMEM)


def params():
    return pltpu.CompilerParams(vmem_limit_bytes=VMEM_BYTES)


def tiles_of(width):
    return [slice(c, c + LANES) for c in range(0, width, LANES)]


def flags_kernel(pieces, mask_ref, *refs):
    r = lax.axis_index("row")
    for k, out_ref in enumerate(refs[-pieces:]):
        chunks = out_ref.shape[1]
        at = pl.multiple_of((r ^ k) * chunks, 16)
        out_ref[...] = mask_ref[:, pl.ds(at, chunks)].astype(f32).astype(jnp.bfloat16)


def cast_flags(lines, pieces, after=()):
    dates, count, lanes = lines.shape
    return pl.pallas_call(
        functools.partial(flags_kernel, pieces),
        in_specs=[whole()] + [anywhere()] * len(after),
        out_specs=[whole()] * pieces,
        out_shape=[pltpu.VMEM((dates, count // pieces, lanes), jnp.bfloat16)] * pieces,
        compiler_params=params(),
        cost_estimate=SHORT,
        name="cast_flags",
    )(lines, *after)


def box_kernel(ks, parts, x_ref, *refs):
    first_call = 1 not in parts
    if first_call:
        outs = refs[-7:-5]
        refs[-5][...] = jnp.zeros_like(refs[-5])
        band, sums, cells_ref, arrived = refs[-4:]
        batch = x_ref.shape[0] // arrived.shape[0]
        copies = [
            pltpu.make_async_copy(
                x_ref.at[pl.ds(n * batch, batch)],
                cells_ref.at[pl.ds(n * batch, batch)],
                arrived.at[n],
            )
            for n in range(arrived.shape[0])
        ]
        for copy in copies:
            copy.start()
        x_ref = cells_ref
    else:
        outs = refs[-6:-4]
        refs[-4][...] = jnp.zeros_like(refs[-4])
        band, sums, edges = refs[-3:]
        batch = 4
    d = lax.axis_index("date")
    r = lax.axis_index("row")
    dates, pols, rows, cols = x_ref.shape
    quarter = rows // lax.axis_size("date")
    half = (d ^ ks[0]) // 2
    span = rows // 2 + 16
    first = pl.multiple_of(half * (rows // 2 - 16), 16)
    images = dates * pols

    near = (
        jnp.abs(
            lax.broadcasted_iota(i32, (cols, cols), 0) - lax.broadcasted_iota(i32, (cols, cols), 1)
        )
        <= RADIUS
    )
    band[...] = near.astype(f32).astype(jnp.bfloat16)
    if 1 in parts:
        edges[...] = jnp.dot(refs[0][...], band[...], preferred_element_type=f32)
        place = jnp.where(half == 0, GROUP - HALO, GROUP + span)
        for i in range(images):
            for c, lanes in enumerate(tiles_of(cols)):
                sums[i, c, pl.ds(place, HALO)] = edges[i * HALO : (i + 1) * HALO, lanes]
    for t in range(0, dates, batch):
        if first_call:
            copies[t // batch].wait()
        x = x_ref[t : t + batch, :, pl.ds(first, span), :].reshape(batch * pols * span, cols)
        summed = jnp.dot(x, band[...], preferred_element_type=f32)
        for i in range(batch * pols):
            for c, lanes in enumerate(tiles_of(cols)):
                sums[t * pols + i, c, GROUP : GROUP + span] = summed[
                    i * span : (i + 1) * span, lanes
                ]

    height = rows * lax.axis_size("row")
    col = edge_count(lax.broadcasted_iota(i32, (GROUP, cols), 1), cols)
    steps = ratio_steps(dates)
    for n, k in enumerate(ks):
        q = d ^ k
        for p, part in enumerate(parts):
            group = half if part else 1 - half
            top = quarter * q + GROUP * group
            base = GROUP + top - first
            row = edge_count(r * rows + top + lax.broadcasted_iota(i32, (GROUP, cols), 0), height)
            scale = 1.0 / (row * col)
            out = outs[n].at[p] if len(parts) > 1 else outs[n]
            cells_at = pl.multiple_of(quarter * q, 16)

            def add_date(t, totals):
                new = []
                for c, lanes in enumerate(tiles_of(cols)):
                    codes = []
                    for pol in range(pols):
                        i = t * pols + pol
                        window = sums[i, c, pl.ds(base - RADIUS, GROUP)]
                        for shift in range(1 - RADIUS, RADIUS + 1):
                            window = window + sums[i, c, pl.ds(base + shift, GROUP)]
                        mean = window * scale[:, lanes]
                        both = x_ref[t, pol, pl.ds(cells_at, quarter), lanes].astype(f32)
                        cells = jnp.where(group == 0, both[:GROUP], both[GROUP:])
                        new.append(totals[c * pols + pol] + cells / mean)
                        codes.append((jnp.log(mean) * CODE_STEPS - 0.5).astype(i32))
                    out[t, :, lanes] = jnp.concatenate(codes, axis=0).astype(jnp.int16)
                return tuple(new)

            zero = jnp.zeros((GROUP, LANES), f32)
            totals = lax.fori_loop(
                0, dates, add_date, (zero,) * (pols * (cols // LANES)), unroll=2
            )
            for c, lanes in enumerate(tiles_of(cols)):
                total = jnp.concatenate(totals[c * pols : (c + 1) * pols], axis=0) * steps
                high = total.astype(i32)
                rest = ((total - high.astype(f32)) * REST_STEPS).astype(i32)
                out[dates, :, lanes] = high.astype(jnp.int16)
                out[dates + 1, :, lanes] = rest.astype(jnp.int16)


def copy_edges(x_ref, out, bottom, dates):
    pols = x_ref.shape[1]
    for t in range(0, dates, 2):
        for lanes in tiles_of(x_ref.shape[3]):
            images = []
            for n in range(2 * pols):
                image = x_ref[t + n // pols, n % pols, :, lanes].astype(f32)
                images.append(jnp.where(bottom == 1, image[16 - HALO :], image[:HALO]))
            line = t * pols * HALO
            out[line : line + 16, lanes] = jnp.concatenate(images, axis=0).astype(out.dtype)


def edges_kernel(x_ref, far_ref, near_ref, rows_ref, arrived):
    half = lax.axis_index("date") // 2
    dates, _, rows, _ = x_ref.shape
    sides = (half, 1 - half)
    copies = []
    for n, side in enumerate(sides):
        at = pl.multiple_of(side * (rows - 16), 16)
        copies.append(
            pltpu.make_async_copy(x_ref.at[:, :, pl.ds(at, 16)], rows_ref.at[n], arrived.at[n])
        )
        copies[n].start()
    for n, out_ref in enumerate((far_ref, near_ref)):
        copies[n].wait()
        copy_edges(rows_ref.at[n], out_ref, sides[n], dates)


def edge_rows(intensity):
    dates, pols, _, cols = intensity.shape
    return pl.pallas_call(
        edges_kernel,
        in_specs=[pl.BlockSpec(memory_space=pltpu.HBM)],
        out_specs=[whole()] * 2,
        out_shape=[pltpu.VMEM((dates * pols * HALO, cols), intensity.dtype)] * 2,
        scratch_shapes=[
            pltpu.VMEM((2, dates, pols, 16, cols), intensity.dtype),
            pltpu.SemaphoreType.DMA((2,)),
        ],
        compiler_params=params(),
        cost_estimate=SHORT,
        name="edge_rows",
    )(intensity)


def box_codes(intensity, halos, ks, parts, after=()):
    dates, pols, rows, cols = intensity.shape
    shape = (dates + 2, pols * GROUP, cols)
    if len(parts) > 1:
        shape = (len(parts),) + shape
    out_shape = [pltpu.VMEM(shape, jnp.int16)] * len(ks)
    scratch = [
        pltpu.VMEM((cols, cols), jnp.bfloat16),
        pltpu.VMEM((dates * pols, cols // LANES, rows // 2 + 32, LANES), f32),
    ]
    first_spec = whole()
    out_shape += [pltpu.VMEM((GROUP, LANES), f32)]
    if halos:
        scratch += [pltpu.VMEM((dates * pols * HALO, cols), f32)]
    else:
        first_spec = pl.BlockSpec(memory_space=pltpu.HBM)
        scratch += [pltpu.VMEM(intensity.shape, intensity.dtype), pltpu.SemaphoreType.DMA((4,))]
    return pl.pallas_call(
        functools.partial(box_kernel, ks, parts),
        in_specs=[first_spec] + [whole()] * len(halos) + [anywhere()] * len(after),
        out_specs=[whole()] * len(out_shape),
        out_shape=out_shape,
        scratch_shapes=scratch,
        compiler_params=params(),
        cost_estimate=SHORT,
        name="box_codes",
    )(intensity, *halos, *after)


def factor_kernel(table_ref, mask_ref, *refs):
    factor_ref = refs[-1]
    dates, lines, _ = mask_ref.shape

    width = 4

    def tiles(n, unused):
        ats = [pl.multiple_of((n * width + i) * GROUP, GROUP) for i in range(width)]

        def add_date(t, totals):
            flags = [mask_ref[t, pl.ds(at, GROUP)].astype(f32) for at in ats]
            new = [totals[0][i] + flags[i] for i in range(width)]
            weights = [table_ref[h, t] for h in range(HARMONICS)]
            return (new,) + tuple(
                [totals[h][i] + flags[i] * weights[h] for i in range(width)]
                for h in range(1, HARMONICS)
            )

        zero = jnp.zeros((GROUP, LANES), f32)
        totals = lax.fori_loop(0, dates, add_date, ([zero] * width,) * HARMONICS, unroll=8)
        for i, at in enumerate(ats):
            factor_tile(factor_ref, at, *[total[i] for total in totals])
        return unused

    lax.fori_loop(0, lines // (GROUP * width), tiles, 0)


def factor_tile(factor_ref, at, m0, c1, s1, c2, s2, c3, s3, c4, s4):
    normal = {
        (0, 0): 2.0 * m0 + NOISE,
        (1, 0): 2.0 * c1,
        (2, 0): 2.0 * s1,
        (3, 0): 2.0 * c2,
        (4, 0): 2.0 * s2,
        (1, 1): m0 + c2 + NOISE,
        (2, 1): s2,
        (3, 1): c1 + c3,
        (4, 1): s1 + s3,
        (2, 2): m0 - c2 + NOISE,
        (3, 2): s3 - s1,
        (4, 2): c1 - c3,
        (3, 3): m0 + c4 + NOISE,
        (4, 3): s4,
        (4, 4): m0 - c4 + NOISE,
        (5, 0): m0,
        (5, 1): c1,
        (5, 2): s1,
        (5, 3): c2,
        (5, 4): s2,
        (5, 5): m0 + NOISE,
    }
    lower = {}
    inverse = {}
    for i in range(STATES):
        for j in range(i + 1):
            total = normal[i, j]
            for k in range(j):
                total = total - lower[i, k] * lower[j, k]
            if i == j:
                inverse[i] = 1.0 / jnp.sqrt(total)
            else:
                lower[i, j] = total * inverse[j]
    planes = [lower[p] for p in PAIRS] + [inverse[i] for i in range(STATES)]
    for h, plane in enumerate(planes):
        factor_ref[h, pl.ds(at, GROUP)] = plane


def factor(table, lines, after=()):
    return pl.pallas_call(
        factor_kernel,
        in_specs=[scalars(), whole()] + [anywhere()] * len(after),
        out_specs=whole(),
        out_shape=jax.ShapeDtypeStruct((PLANES,) + lines.shape[1:], f32),
        compiler_params=params(),
        cost_estimate=SHORT,
        name="factor",
    )(table, lines, *after)


class Joined:
    def __init__(self, refs, start, length):
        self.lines = [(ref, n) for ref in refs for n in range(ref.shape[0])]
        self.lines = self.lines[start : start + length]
        self.shape = (length,)

    def __getitem__(self, index):
        ref, n = self.lines[index[0]]
        return ref[(n, *index[1:])]


def decode_ratio(block, dates, lanes):
    high = block[dates, :, lanes].astype(i32).astype(f32)
    rest = block[dates + 1, :, lanes].astype(i32).astype(f32)
    return high + rest * (1.0 / REST_STEPS)


def add_logs(block, table_ref, start, flag_of, sums, tiles):
    for t in range(block.shape[0] - 2):
        weights = [table_ref[n, start + t] for n in range(STATES - 1)]
        for c, lanes in enumerate(tiles):
            logs = block[t, :, lanes].astype(i32).astype(f32)
            flag = flag_of(t, c, lanes)
            vh = logs[GROUP:] * flag
            both = logs[:GROUP] * flag + vh
            sums[c][0] = sums[c][0] + both
            for n in range(1, STATES - 1):
                sums[c][n] = sums[c][n] + both * weights[n]
            sums[c][STATES - 1] = sums[c][STATES - 1] + vh


def right_of(sums, flag_sums, ratio, steps):
    logs = jnp.log(ratio * (1.0 / steps))
    both = logs[:GROUP] + logs[GROUP:]
    right = [total * (1.0 / CODE_STEPS) for total in sums]
    for n in range(STATES - 1):
        right[n] = right[n] + both * flag_sums[n]
    right[STATES - 1] = right[STATES - 1] + logs[GROUP:] * flag_sums[0]
    return right


def right_kernel(pieces, table_ref, *refs):
    flags_refs, near_ref = refs[:pieces], refs[pieces]
    other_refs = refs[pieces + 1 : pieces + 3]
    part_ref, ratio_ref, flags_out, lines = refs[-4:]
    d = lax.axis_index("date")
    r = lax.axis_index("row")
    dates, chunks, _ = flags_refs[0].shape
    parts, count, _, cols = near_ref.shape
    local = count - 2
    tiles = tiles_of(cols)
    zero = jnp.zeros((GROUP, LANES), f32)
    for k, flags_ref in enumerate(flags_refs):
        at = pl.multiple_of((r ^ k) * chunks, 16) if pieces > 1 else 0
        lines[:, pl.ds(at, chunks)] = flags_ref[...].astype(f32)
    for part in range(parts):
        start = (d // 2 if part else 1 - d // 2) * GROUP * len(tiles)
        sums = [[zero] * STATES for _ in tiles]
        flag_sums = [[zero] * (STATES - 1) for _ in tiles]
        blocks = [near_ref.at[part], Joined(other_refs, part * count, count)]
        for k in range(4):
            date = (d ^ k) * local

            def weigh(t, c, lanes):
                flag = lines[date + t, pl.ds(start + c, GROUP, stride=len(tiles))]
                if k >= 2:
                    flags_out[part, (k - 2) * local + t, :, lanes] = flag
                flag_sums[c][0] = flag_sums[c][0] + flag
                for n in range(1, STATES - 1):
                    flag_sums[c][n] = flag_sums[c][n] + flag * table_ref[n, date + t]
                return flag

            if k < 2:
                add_logs(blocks[k], table_ref, date, weigh, sums, tiles)
            else:
                for t in range(local):
                    for c, lanes in enumerate(tiles):
                        weigh(t, c, lanes)
        for c, lanes in enumerate(tiles):
            ratios = [decode_ratio(block, local, lanes) for block in blocks]
            ratio_ref[part, :, lanes] = ratios[0] + ratios[1]
            for n, total in enumerate(sums[c] + flag_sums[c]):
                part_ref[part, n, :, lanes] = total


def right_sides(table, flags, near):
    dates, chunks, _ = flags[0].shape
    parts, _, _, cols = near[0].shape
    local = near[0].shape[1] - 2
    shapes = [
        (parts, 2 * STATES - 1, GROUP, cols),
        (parts, 2 * GROUP, cols),
        (parts, 2 * local, GROUP, cols),
    ]
    return pl.pallas_call(
        functools.partial(right_kernel, len(flags)),
        in_specs=[scalars()] + [whole()] * (len(flags) + len(near)),
        out_specs=[whole()] * len(shapes),
        out_shape=[pltpu.VMEM(shape, f32) for shape in shapes],
        scratch_shapes=[pltpu.VMEM((dates, len(flags) * chunks, LANES), f32)],
        compiler_params=params(),
        cost_estimate=SHORT,
        name="right_sides",
    )(table, *flags, *near)


def finish_kernel(dates, table_ref, part_ref, ratio_ref, flags_ref, far_2, far_3, *refs):
    out_refs, right = refs[:-1], refs[-1]
    d = lax.axis_index("date")
    r = lax.axis_index("row")
    parts, _, _, cols = far_2.shape
    local = far_2.shape[1] - 2
    tiles = tiles_of(cols)
    for part in range(parts):
        sums = [[part_ref[part, n, :, lanes] for n in range(STATES)] for lanes in tiles]
        blocks = (far_2.at[part], far_3.at[part])
        for k, block in enumerate(blocks):

            def flag_of(t, c, lanes):
                return flags_ref[part, k * local + t, :, lanes]

            add_logs(block, table_ref, (d ^ (k + 2)) * local, flag_of, sums, tiles)
        start = (d // 2 if part else 1 - d // 2) * GROUP * len(tiles)
        for c, lanes in enumerate(tiles):
            ratio = ratio_ref[part, :, lanes]
            for block in blocks:
                ratio = ratio + decode_ratio(block, local, lanes)
            flag_sums = [part_ref[part, STATES + n, :, lanes] for n in range(STATES - 1)]
            rights = right_of(sums[c], flag_sums, ratio, ratio_steps(local) * dates)
            for n, total in enumerate(rights):
                right[n, pl.ds(start + c, GROUP, stride=len(tiles))] = total
    for k, out_ref in enumerate(out_refs):
        chunks = out_ref.shape[1]
        at = pl.multiple_of((r ^ k) * chunks, GROUP) if len(out_refs) > 1 else 0
        out_ref[...] = right[:, pl.ds(at, chunks)]


def finish_sides(table, parts, far, dates, pieces):
    cols = far[0].shape[3]
    lines = 2 * GROUP * cols // LANES
    return pl.pallas_call(
        functools.partial(finish_kernel, dates),
        in_specs=[scalars()] + [whole()] * (len(parts) + len(far)),
        out_specs=[whole()] * pieces,
        out_shape=[pltpu.VMEM((STATES, lines // pieces, LANES), f32)] * pieces,
        scratch_shapes=[pltpu.VMEM((STATES, lines, LANES), f32)],
        compiler_params=params(),
        cost_estimate=SHORT,
        name="finish_sides",
    )(table, *parts, *far)


def solve_kernel(factor_ref, *refs):
    out_ref = refs[-1]
    r = lax.axis_index("row")
    for n, right_ref in enumerate(refs[:-1]):
        chunks = right_ref.shape[1]
        start = (r ^ n) * chunks if len(refs) > 2 else 0
        for line in range(0, chunks, GROUP):
            at = pl.ds(pl.multiple_of(start + line, GROUP), GROUP)
            lower = {p: factor_ref[h, at] for h, p in enumerate(PAIRS)}
            inverse = [factor_ref[len(PAIRS) + h, at] for h in range(STATES)]
            middle = []
            for i in range(STATES):
                total = right_ref[i, line : line + GROUP]
                for k in range(i):
                    total = total - lower[i, k] * middle[k]
                middle.append(total * inverse[i])
            solved = [None] * STATES
            for i in reversed(range(STATES)):
                total = middle[i]
                for k in range(i + 1, STATES):
                    total = total - lower[k, i] * solved[k]
                solved[i] = total * inverse[i]
                out_ref[i, at] = solved[i]


def solve(factors, rights):
    return pl.pallas_call(
        solve_kernel,
        in_specs=[whole()] * (1 + len(rights)),
        out_specs=whole(),
        out_shape=jax.ShapeDtypeStruct((STATES,) + factors.shape[1:], f32),
        compiler_params=params(),
        cost_estimate=SHORT,
        name="solve",
    )(factors, *rights)


def harmonics(day_index):
    phase = day_index.astype(f32) * (2.0 * math.pi / 365.0)
    order = (np.arange(HARMONICS)[:, None] + 1) // 2
    sines = np.arange(HARMONICS)[:, None] % 2 == 0
    sines[0] = False
    angle = order.astype(np.float32) * phase[None, :]
    return jnp.where(sines, jnp.sin(angle), jnp.cos(angle))


def body(intensity, valid_mask, day_index):
    rows, cols = intensity.shape[2:]
    date_devices = lax.axis_size("date")
    row_devices = lax.axis_size("row")
    all_dates = valid_mask.shape[0]
    lines_count = rows * cols // date_devices // LANES
    chunks = lines_count // row_devices
    direct = row_devices in (2, 4) and chunks % 16 == 0

    def exchange(piece, axis, k):
        return lax.ppermute(piece, axis, partners(lax.axis_size(axis), k))

    lines = valid_mask.reshape(all_dates, lines_count, LANES)
    table = harmonics(day_index)
    half = date_devices // 2

    def halo(cells, upwards):
        pairs = []
        for d in range(date_devices):
            for r in range(row_devices - 1):
                pair = (d * row_devices + r, d * row_devices + r + 1)
                pairs.append(pair[::-1] if (d < half) == upwards else pair)
        return lax.ppermute(cells, ("date", "row"), pairs)

    in_hbm = pltpu.with_memory_space_constraint(intensity, pltpu.HBM)
    far_edge, near_edge = edge_rows(in_hbm)
    far_halo = halo(far_edge, True)
    near_halo = halo(near_edge, False)
    if direct:
        flags = cast_flags(lines, row_devices, after=(far_edge,))
        ready = flags[:1]
        flags = [flags[0]] + [exchange(flags[k], "row", k) for k in range(1, row_devices)]
    else:
        ready = ()
        flags = lax.all_to_all(
            valid_mask.astype(jnp.bfloat16), "row", split_axis=1, concat_axis=2, tiled=True
        )
        flags = [flags.reshape(all_dates, lines_count, LANES)]
    *far, done = box_codes(intensity, (far_halo,), (2, 3), (0, 1), after=(table, *ready))
    far = [exchange(far[0], "date", 2), exchange(far[1], "date", 3)]
    *near, done = box_codes(intensity, (near_halo,), (0, 1), (0, 1), after=(done,))
    other = near[1].reshape(-1, *near[1].shape[2:])
    count = other.shape[0]
    cut = 2 * count // 3
    other = [other[:cut], other[cut:]]
    other, flags = lax.optimization_barrier((other, flags))
    near = [near[0]] + [exchange(codes, "date", 1) for codes in other]
    factors = factor(table, lines, after=(done,))

    pieces = row_devices if direct else 1
    parts = right_sides(table, flags, near)
    rights = finish_sides(table, parts, far, all_dates, pieces)
    if direct:
        rights = [rights[0]] + [exchange(rights[k], "row", k) for k in range(1, row_devices)]
    else:
        rights = rights[0].reshape(STATES, 1, row_devices, chunks * LANES)
        rights = lax.all_to_all(rights, "row", split_axis=2, concat_axis=1, tiled=True)
        rights = [rights.reshape(STATES, lines_count, LANES)]
    return solve(factors, rights).reshape(STATES, row_devices, 1, chunks * LANES)


def solution(mesh):
    return jax.shard_map(
        body,
        mesh=mesh,
        in_specs=(
            P("date", None, ("tile", "row"), None),
            P(None, "tile", ("date", "row"), None),
            P(),
        ),
        out_specs=P(None, "tile", ("date", "row"), None),
        check_vma=False,
    )
```

time: 144 us -> 55.7 us (0.39)
  waiting for transfers between devices: 55.4 us -> 19 us
  other arithmetic: 23.1 us -> 0.12 us
  Pallas kernels: 0 us -> 16.3 us
  local copies, waits for them, and re-layouts: 16.4 us -> 1.65 us
  between operations: 13.6 us -> 0.17 us
  blocking collectives: 11.9 us -> 0 us
  matrix products: 5.86 us -> 0 us
    psum x1 -> x0, waiting for transfers between devices: 33.6 us -> none  [body(): ratio_total = lax.psum(partial_sum, 'date')]
    all_to_all x2 -> x0, waiting for transfers between devices: 21.8 us -> none  [the longest x1 21.8 us: body(): lax.all_to_all(blocks_out, 'date', split_axis=2, concat_axis=0, tiled=True)]
    ppermute x2 -> x12, waiting for transfers between devices: 0.01 us -> 19 us  [the longest x10 19 us: exchange(): return lax.ppermute(piece, axis, partners(lax.axis_size(axis), k))]
    pallas_call x0 -> x8, Pallas kernels: none -> 16.3 us  [the longest x2 7.5 us: box_codes(): pl.pallas_call(functools.partial(box_kernel, ks, parts), in_specs=[first_...]
    all_to_all x1 -> x0, blocking collectives: 11.9 us -> none  [body(): lax.all_to_all(state_rows, 'row', split_axis=2, concat_axis=1, tiled=True)]
    ppermute x2 -> x12, starting transfers between devices: 6.87 us -> 18.3 us  [the longest x10 12 us: exchange(): return lax.ppermute(piece, axis, partners(lax.axis_size(axis), k))]
    all_to_all x2 -> x0, starting transfers between devices: 10.8 us -> none  [the longest x1 5.94 us: body(): lax.all_to_all(mask_wire, 'row', split_axis=1, concat_axis=2, tiled=True)]
    unnamed x2 -> x0, other arithmetic: 10.2 us -> none
  transfers between devices with their start and end apart: 5 -> 12, of which waited for: 2 -> 4; matrix products, arithmetic and copies ran while one was open for 24% -> 0% of each run, Pallas kernels for 0% -> 23%
where the time goes in v2:
time: 55.7 us; the launch traced here: 55.5 us
  waiting for transfers between devices  19 us (34%)
  starting transfers between devices  18.3 us (33%)
  Pallas kernels  16.3 us (29%)
  local copies, waits for them, and re-layouts  1.65 us (3%)
    ppermute x10, waiting for transfers between devices, exchange(): return lax.ppermute(piece, axis, partners(lax.axis_size(axis), k))  19 us
    ppermute x10, starting transfers between devices, exchange(): return lax.ppermute(piece, axis, partners(lax.axis_size(axis), k))  12 us
    pallas_call x2, Pallas kernels, box_codes(): pl.pallas_call(functools.partial(box_kernel, ks, parts), in_specs=[first_...  7.5 us
    ppermute x2, starting transfers between devices, halo(): return lax.ppermute(cells, ('date', 'row'), pairs)  6.24 us
    pallas_call x1, Pallas kernels, right_sides(): pl.pallas_call(functools.partial(right_kernel, len(flags)), in_specs=[sca...  2.54 us
    pallas_call x1, Pallas kernels, factor(): pl.pallas_call(factor_kernel, in_specs=[scalars(), whole()] + [anywhere()...  2.48 us
    unnamed x12, local copies, waits for them, and re-layouts  1.6 us
    pallas_call x1, Pallas kernels, edge_rows(): pl.pallas_call(edges_kernel, in_specs=[pl.BlockSpec(memory_space=pltpu.HB...  1.48 us
  transfers between devices with their start and end apart: 12, of which 4 were waited for; matrix products, arithmetic and copies ran while one was open for 0% of the time, Pallas kernels for 23%

profile of v2, /device:TPU:0, one launch (start us, length us, event | category | flops | bytes accessed | tf_op | source)
XLA Modules:
  0.0 55.5 jit_solution(13336057119764080534)
XLA Ops:
  0.0 0.0 copy-start.3
  0.0 0.0 copy-start.4
  0.0 0.0 copy-start
  0.0 0.0 copy-start.5
  0.0 1.5 %edge_rows.1 = (bf16[128,512]{1,0:T(8,128)(2,1)S(1)}, bf16[128,512]{1,0:T(8,128)(2,1)S(1)}) custom-call(bf16[16,2,64,512]{3,2,1,0:T(8,128)(2,1)} %x_ref.5), custom_call_target="tpu_custom_call" | custom-call | flops 1000 | bytes 1000 | tf_op jit(solution)/shard_map/edge_rows/pallas_call | solution.py:215
  1.5 4.9 %collective-permute-start = (bf16[128,512]{1,0:T(8,128)(2,1)S(1)}, bf16[128,512]{1,0:T(8,128)(2,1)S(1)}, u32[]{:S(2)}, u32[]{:S(2)}) collective-permute-start(bf16[128,512]{1,0:T(8,128)(2,1)S(1)} %get-tuple-element.30), channel_id=1, source_target_pairs={{0,1},{1,2},{2,3},{4,5},{5,6},{6,7},{9,8},{10,9},{11,10},{13,12},{... | collective-permute-start | bytes 393224 | tf_op jit(solution)/shard_map/ppermute | solution.py:558
  6.5 1.3 %collective-permute-start.1 = (bf16[128,512]{1,0:T(8,128)(2,1)S(1)}, bf16[128,512]{1,0:T(8,128)(2,1)S(1)}, u32[]{:S(2)}, u32[]{:S(2)}) collective-permute-start(bf16[128,512]{1,0:T(8,128)(2,1)S(1)} %get-tuple-element.31.refs_0_), channel_id=1, source_target_pairs={{1,0},{2,1},{3,2},{5,4},{6,5},{7,6},{8,9},{9,10},{10,11},{12,13},{... | collective-permute-start | bytes 393224 | tf_op jit(solution)/shard_map/ppermute | solution.py:558
  7.8 0.0 copy-start.1
  7.8 1.6 %copy-done.1 = s32[64,4,1,2048]{3,2,1,0:T(1,128)S(1)} copy-done((s32[64,4,1,2048]{3,2,1,0:T(1,128)S(1)}, s32[64,4,1,2048]{3,2,1,0:T(1,128)}, u32[]{:S(2)}) %copy-start.1) | copy-done | bytes 2097176
  9.3 0.1 cast_flags.1
  9.5 2.7 %collective-permute-start.2 = (bf16[64,16,128]{2,1,0:T(8,128)(2,1)S(1)}, bf16[64,16,128]{2,1,0:T(8,128)(2,1)S(1)}, u32[]{:S(2)}, u32[]{:S(2)}) collective-permute-start(bf16[64,16,128]{2,1,0:T(8,128)(2,1)S(1)} %get-tuple-element.36), channel_id=1, source_target_pairs={{0,1},{1,0},{2,3},{3,2},{4,5},{5,4},{6,7},{7,6},{8,9},{9,8},{10,11... | collective-permute-start | bytes 786440 | tf_op jit(solution)/shard_map/ppermute | solution.py:546
  12.2 2.6 %collective-permute-start.3 = (bf16[64,16,128]{2,1,0:T(8,128)(2,1)S(1)}, bf16[64,16,128]{2,1,0:T(8,128)(2,1)S(1)}, u32[]{:S(2)}, u32[]{:S(2)}) collective-permute-start(bf16[64,16,128]{2,1,0:T(8,128)(2,1)S(1)} %get-tuple-element.37), channel_id=1, source_target_pairs={{0,2},{1,3},{2,0},{3,1},{4,6},{5,7},{6,4},{7,5},{8,10},{9,11},{10,... | collective-permute-start | bytes 786440 | tf_op jit(solution)/shard_map/ppermute | solution.py:546
  14.8 0.0 collective-permute-start.4
  14.8 0.0 copy-done.5
  14.8 0.0 copy-done.3
  14.8 0.0 copy-done.4
  14.8 0.1 fusion.refs_1_.table_ref
  14.9 0.0 collective-permute-done.1.refs_0_
  15.0 0.0 copy-done
  15.0 3.7 %box_codes.2 = (s16[2,18,16,512]{3,2,1,0:T(8,128)(2,1)S(1)}, s16[2,18,16,512]{3,2,1,0:T(8,128)(2,1)S(1)}, f32[8,128]{1,0:T(8,128)S(1)}) custom-call(bf16[16,2,64,512]{3,2,1,0:T(8,128)(2,1)S(1)} %copy-done, bf16[128,512]{1,0:T(8,128)(2,1)S(1)} %collective-permute-done.1.refs_0_, f32[9,64]{1,0:T(8,128)S(1)} %fusion.refs_1_.table_ref, ...), custom_call_target="tpu_custom_call" | custom-call | flops 1000 | bytes 1000 | tf_op jit(solution)/shard_map/box_codes/pallas_call | solution.py:247
  18.7 1.8 %collective-permute-start.7 = (s16[2,18,16,512]{3,2,1,0:T(8,128)(2,1)S(1)}, s16[2,18,16,512]{3,2,1,0:T(8,128)(2,1)S(1)}, u32[]{:S(2)}, u32[]{:S(2)}) collective-permute-start(s16[2,18,16,512]{3,2,1,0:T(8,128)(2,1)S(1)} %get-tuple-element.49), channel_id=1, source_target_pairs={{0,8},{4,12},{8,0},{12,4},{1,9},{5,13},{9,1},{13,5},{2,10},{6,14},... | collective-permute-start | bytes 1769480 | tf_op jit(solution)/shard_map/ppermute | solution.py:546
  20.5 0.0 collective-permute-done.refs_0_
  20.5 0.0 collective-permute-start.8
  20.5 3.7 %box_codes.3 = (s16[2,18,16,512]{3,2,1,0:T(8,128)(2,1)S(1)}, s16[2,18,16,512]{3,2,1,0:T(8,128)(2,1)S(1)}, f32[8,128]{1,0:T(8,128)S(1)}) custom-call(bf16[16,2,64,512]{3,2,1,0:T(8,128)(2,1)S(1)} %copy-done, bf16[128,512]{1,0:T(8,128)(2,1)S(1)} %collective-permute-done.refs_0_, f32[8,128]{1,0:T(8,128)S(1)} %get-tuple-element.33.refs_1_), custom_call_target="tpu_custom_call" | custom-call | flops 1000 | bytes 1000 | tf_op jit(solution)/shard_map/box_codes/pallas_call | solution.py:247
  24.3 0.0 collective-permute-done.2.refs_1_
  24.3 9.3 %collective-permute-done.3.refs_2_ = bf16[64,16,128]{2,1,0:T(8,128)(2,1)S(1)} collective-permute-done((bf16[64,16,128]{2,1,0:T(8,128)(2,1)S(1)}, bf16[64,16,128]{2,1,0:T(8,128)(2,1)S(1)}, u32[]{:S(2)}, u32[]{:S(2)}) %collective-permute-start.3) | collective-permute-done | bytes 262176 | tf_op jit(solution)/shard_map/ppermute | solution.py:546
  33.6 0.0 collective-permute-done.4.refs_3_
  33.6 0.0 collective-permute-start.5
  33.6 0.5 collective-permute-start.6
  34.1 1.5 %collective-permute-done.6.refs_6_ = s16[12,16,512]{2,1,0:T(8,128)(2,1)S(1)} collective-permute-done((s16[12,16,512]{2,1,0:T(8,128)(2,1)S(1)}, s16[12,16,512]{2,1,0:T(8,128)(2,1)S(1)}, u32[]{:S(2)}, u32[]{:S(2)}) %collective-permute-start.6) | collective-permute-done | bytes 196640 | tf_op jit(solution)/shard_map/ppermute | solution.py:546
  35.6 0.0 collective-permute-done.5.refs_5_
  35.6 0.0 copy-start.2
  35.6 2.5 %right_sides.1 = (f32[2,11,8,512]{3,2,1,0:T(8,128)S(1)}, f32[2,16,512]{2,1,0:T(8,128)S(1)}, f32[2,32,8,512]{3,2,1,0:T(8,128)S(1)}) custom-call(f32[9,64]{1,0:T(8,128)S(1)} %fusion.refs_1_.table_ref, bf16[64,16,128]{2,1,0:T(8,128)(2,1)S(1)} %get-tuple-element.39.refs_2_.refs_0_, bf16[64,16,128]{2,1,0:T(8,128)(2,1)S(1)} %collective-permute-done.2.refs_1_, ...), custom_call_target="tpu_custom_call" | custom-call | flops 1000 | bytes 1000 | tf_op jit(solution)/shard_map/right_sides/pallas_call | solution.py:432
  38.1 0.0 collective-permute-done.7.far_2
  38.2 6.2 %collective-permute-done.8.far_3 = s16[2,18,16,512]{3,2,1,0:T(8,128)(2,1)S(1)} collective-permute-done((s16[2,18,16,512]{3,2,1,0:T(8,128)(2,1)S(1)}, s16[2,18,16,512]{3,2,1,0:T(8,128)(2,1)S(1)}, u32[]{:S(2)}, u32[]{:S(2)}) %collective-permute-start.8) | collective-permute-done | bytes 589856 | tf_op jit(solution)/shard_map/ppermute | solution.py:546
  44.3 1.4 %finish_sides.1 = (f32[6,16,128]{2,1,0:T(8,128)S(1)}, f32[6,16,128]{2,1,0:T(8,128)S(1)}, f32[6,16,128]{2,1,0:T(8,128)S(1)}, f32[6,16,128]{2,1,0:T(8,128)S(1)}) custom-call(f32[9,64]{1,0:T(8,128)S(1)} %fusion.refs_1_.table_ref, f32[2,11,8,512]{3,2,1,0:T(8,128)S(1)} %get-tuple-element.46.part_ref, f32[2,16,512]{2,1,0:T(8,128)S(1)} %get-tuple-element.47.ratio_ref, ...), custom_call_target="tpu_custom_call" | custom-call | flops 1000 | bytes 1000 | tf_op jit(solution)/shard_map/finish_sides/pallas_call | solution.py:478
  45.7 0.7 %collective-permute-start.9 = (f32[6,16,128]{2,1,0:T(8,128)S(1)}, f32[6,16,128]{2,1,0:T(8,128)S(1)}, u32[]{:S(2)}, u32[]{:S(2)}) collective-permute-start(f32[6,16,128]{2,1,0:T(8,128)S(1)} %get-tuple-element.52), channel_id=1, source_target_pairs={{0,1},{1,0},{2,3},{3,2},{4,5},{5,4},{6,7},{7,6},{8,9},{9,8},{10,11... | collective-permute-start | bytes 147464 | tf_op jit(solution)/shard_map/ppermute | solution.py:546
  46.4 2.3 %collective-permute-start.10 = (f32[6,16,128]{2,1,0:T(8,128)S(1)}, f32[6,16,128]{2,1,0:T(8,128)S(1)}, u32[]{:S(2)}, u32[]{:S(2)}) collective-permute-start(f32[6,16,128]{2,1,0:T(8,128)S(1)} %get-tuple-element.53), channel_id=1, source_target_pairs={{0,2},{1,3},{2,0},{3,1},{4,6},{5,7},{6,4},{7,5},{8,10},{9,11},{10,... | collective-permute-start | bytes 147464 | tf_op jit(solution)/shard_map/ppermute | solution.py:546
  48.7 1.4 %collective-permute-start.11 = (f32[6,16,128]{2,1,0:T(8,128)S(1)}, f32[6,16,128]{2,1,0:T(8,128)S(1)}, u32[]{:S(2)}, u32[]{:S(2)}) collective-permute-start(f32[6,16,128]{2,1,0:T(8,128)S(1)} %get-tuple-element.54), channel_id=1, source_target_pairs={{0,3},{1,2},{2,1},{3,0},{4,7},{5,6},{6,5},{7,4},{8,11},{9,10},{10,... | collective-permute-start | bytes 147464 | tf_op jit(solution)/shard_map/ppermute | solution.py:546
  50.1 0.0 copy-done.2
  50.1 2.5 %factor.1.factor_ref = f32[21,64,128]{2,1,0:T(8,128)S(1)} custom-call(f32[9,64]{1,0:T(8,128)S(1)} %fusion.refs_1_.table_ref, s32[64,64,128]{2,1,0:T(8,128)S(1)} %bitcast.4, f32[8,128]{1,0:T(8,128)S(1)} %get-tuple-element.34.refs_0_), custom_call_target="tpu_custom_call" | custom-call | flops 1000 | bytes 1000 | tf_op jit(solution)/shard_map/factor/pallas_call | solution.py:327
  52.6 0.0 collective-permute-done.9.refs_1_
  52.7 0.0 collective-permute-done.10.refs_2_
  52.7 2.1 %collective-permute-done.11.refs_3_ = f32[6,16,128]{2,1,0:T(8,128)S(1)} collective-permute-done((f32[6,16,128]{2,1,0:T(8,128)S(1)}, f32[6,16,128]{2,1,0:T(8,128)S(1)}, u32[]{:S(2)}, u32[]{:S(2)}) %collective-permute-start.11) | collective-permute-done | bytes 49184 | tf_op jit(solution)/shard_map/ppermute | solution.py:546
  54.7 0.8 %solve.1 = f32[6,64,128]{2,1,0:T(8,128)} custom-call(f32[21,64,128]{2,1,0:T(8,128)S(1)} %factor.1.factor_ref, f32[6,16,128]{2,1,0:T(8,128)S(1)} %get-tuple-element.51.refs_0_, f32[6,16,128]{2,1,0:T(8,128)S(1)} %collective-permute-done.9.refs_1_, f32[6,16,128]{2,1,0:T(8,128)S(1)} %collective-permute-done.10.refs_2_, ...), custom_call_target="tpu_custom_call" | custom-call | flops 1000 | bytes 1000 | tf_op jit(solution)/shard_map/solve/pallas_call | solution.py:516
  (3 shorter events, 0.0 us)
Async XLA Ops:
  0.0 14.8 %copy-start.3 = (f32[9]{0:T(128)S(1)}, f32[9]{0:T(128)}, u32[]{:S(2)}) copy-start(f32[9]{0:T(128)} %constant.10) | copy-start | bytes 112
  0.0 14.8 %copy-start.4 = (pred[9]{0:T(512)(128)(4,1)S(1)}, pred[9]{0:T(512)(128)(4,1)}, u32[]{:S(2)}) copy-start(pred[9]{0:T(512)(128)(4,1)} %constant.9) | copy-start | bytes 31
  0.0 15.0 %copy-start = (bf16[16,2,64,512]{3,2,1,0:T(8,128)(2,1)S(1)}, bf16[16,2,64,512]{3,2,1,0:T(8,128)(2,1)}, u32[]{:S(2)}) copy-start(bf16[16,2,64,512]{3,2,1,0:T(8,128)(2,1)} %x_ref.5) | copy-start | bytes 6291460
  0.0 14.8 %copy-start.5 = (s32[64]{0:T(128)S(1)}, s32[64]{0:T(128)}, u32[]{:S(2)}) copy-start(s32[64]{0:T(128)} %param.7) | copy-start | bytes 772
  1.5 19.0 %collective-permute-start = (bf16[128,512]{1,0:T(8,128)(2,1)S(1)}, bf16[128,512]{1,0:T(8,128)(2,1)S(1)}, u32[]{:S(2)}, u32[]{:S(2)}) collective-permute-start(bf16[128,512]{1,0:T(8,128)(2,1)S(1)} %get-tuple-element.30), channel_id=1, source_target_pairs={{0,1},{1,2},{2,3},{4,5},{5,6},{6,7},{9,8},{10,9},{11,10},{13,12},{... | collective-permute-start | bytes 393224 | tf_op jit(solution)/shard_map/ppermute | solution.py:558
  6.5 8.5 %collective-permute-start.1 = (bf16[128,512]{1,0:T(8,128)(2,1)S(1)}, bf16[128,512]{1,0:T(8,128)(2,1)S(1)}, u32[]{:S(2)}, u32[]{:S(2)}) collective-permute-start(bf16[128,512]{1,0:T(8,128)(2,1)S(1)} %get-tuple-element.31.refs_0_), channel_id=1, source_target_pairs={{1,0},{2,1},{3,2},{5,4},{6,5},{7,6},{8,9},{9,10},{10,11},{12,13},{... | collective-permute-start | bytes 393224 | tf_op jit(solution)/shard_map/ppermute | solution.py:558
  7.8 1.6 %copy-start.1 = (s32[64,4,1,2048]{3,2,1,0:T(1,128)S(1)}, s32[64,4,1,2048]{3,2,1,0:T(1,128)}, u32[]{:S(2)}) copy-start(s32[64,4,1,2048]{3,2,1,0:T(1,128)} %param.6) | copy-start | bytes 6291460
  9.5 14.8 %collective-permute-start.2 = (bf16[64,16,128]{2,1,0:T(8,128)(2,1)S(1)}, bf16[64,16,128]{2,1,0:T(8,128)(2,1)S(1)}, u32[]{:S(2)}, u32[]{:S(2)}) collective-permute-start(bf16[64,16,128]{2,1,0:T(8,128)(2,1)S(1)} %get-tuple-element.36), channel_id=1, source_target_pairs={{0,1},{1,0},{2,3},{3,2},{4,5},{5,4},{6,7},{7,6},{8,9},{9,8},{10,11... | collective-permute-start | bytes 786440 | tf_op jit(solution)/shard_map/ppermute | solution.py:546
  12.2 21.4 %collective-permute-start.3 = (bf16[64,16,128]{2,1,0:T(8,128)(2,1)S(1)}, bf16[64,16,128]{2,1,0:T(8,128)(2,1)S(1)}, u32[]{:S(2)}, u32[]{:S(2)}) collective-permute-start(bf16[64,16,128]{2,1,0:T(8,128)(2,1)S(1)} %get-tuple-element.37), channel_id=1, source_target_pairs={{0,2},{1,3},{2,0},{3,1},{4,6},{5,7},{6,4},{7,5},{8,10},{9,11},{10,... | collective-permute-start | bytes 786440 | tf_op jit(solution)/shard_map/ppermute | solution.py:546
  14.8 18.8 %collective-permute-start.4 = (bf16[64,16,128]{2,1,0:T(8,128)(2,1)S(1)}, bf16[64,16,128]{2,1,0:T(8,128)(2,1)S(1)}, u32[]{:S(2)}, u32[]{:S(2)}) collective-permute-start(bf16[64,16,128]{2,1,0:T(8,128)(2,1)S(1)} %get-tuple-element.38), channel_id=1, source_target_pairs={{0,3},{1,2},{2,1},{3,0},{4,7},{5,6},{6,5},{7,4},{8,11},{9,10},{10,... | collective-permute-start | bytes 786440 | tf_op jit(solution)/shard_map/ppermute | solution.py:546
  18.7 19.4 %collective-permute-start.7 = (s16[2,18,16,512]{3,2,1,0:T(8,128)(2,1)S(1)}, s16[2,18,16,512]{3,2,1,0:T(8,128)(2,1)S(1)}, u32[]{:S(2)}, u32[]{:S(2)}) collective-permute-start(s16[2,18,16,512]{3,2,1,0:T(8,128)(2,1)S(1)} %get-tuple-element.49), channel_id=1, source_target_pairs={{0,8},{4,12},{8,0},{12,4},{1,9},{5,13},{9,1},{13,5},{2,10},{6,14},... | collective-permute-start | bytes 1769480 | tf_op jit(solution)/shard_map/ppermute | solution.py:546
  20.5 23.8 %collective-permute-start.8 = (s16[2,18,16,512]{3,2,1,0:T(8,128)(2,1)S(1)}, s16[2,18,16,512]{3,2,1,0:T(8,128)(2,1)S(1)}, u32[]{:S(2)}, u32[]{:S(2)}) collective-permute-start(s16[2,18,16,512]{3,2,1,0:T(8,128)(2,1)S(1)} %get-tuple-element.50), channel_id=1, source_target_pairs={{0,12},{4,8},{8,4},{12,0},{1,13},{5,9},{9,5},{13,1},{2,14},{6,10},... | collective-permute-start | bytes 1769480 | tf_op jit(solution)/shard_map/ppermute | solution.py:546
  33.6 2.0 %collective-permute-start.5 = (s16[24,16,512]{2,1,0:T(8,128)(2,1)S(1)}, s16[24,16,512]{2,1,0:T(8,128)(2,1)S(1)}, u32[]{:S(2)}, u32[]{:S(2)}) collective-permute-start(s16[24,16,512]{2,1,0:T(8,128)(2,1)S(1)} %slice.8), channel_id=1, source_target_pairs={{0,4},{4,0},{8,12},{12,8},{1,5},{5,1},{9,13},{13,9},{2,6},{6,2},{1... | collective-permute-start | bytes 1179656 | tf_op jit(solution)/shard_map/ppermute | solution.py:546
  33.6 2.0 %collective-permute-start.6 = (s16[12,16,512]{2,1,0:T(8,128)(2,1)S(1)}, s16[12,16,512]{2,1,0:T(8,128)(2,1)S(1)}, u32[]{:S(2)}, u32[]{:S(2)}) collective-permute-start(s16[12,16,512]{2,1,0:T(8,128)(2,1)S(1)} %slice.9), channel_id=1, source_target_pairs={{0,4},{4,0},{8,12},{12,8},{1,5},{5,1},{9,13},{13,9},{2,6},{6,2},{1... | collective-permute-start | bytes 589832 | tf_op jit(solution)/shard_map/ppermute | solution.py:546
  35.6 14.6 %copy-start.2 = (s32[64,4,1,2048]{3,2,1,0:T(1,128)S(1)}, s32[64,4,1,2048]{3,2,1,0:T(1,128)}, u32[]{:S(2)}) copy-start(s32[64,4,1,2048]{3,2,1,0:T(1,128)} %param.6) | copy-start | bytes 6291460
  45.7 7.0 %collective-permute-start.9 = (f32[6,16,128]{2,1,0:T(8,128)S(1)}, f32[6,16,128]{2,1,0:T(8,128)S(1)}, u32[]{:S(2)}, u32[]{:S(2)}) collective-permute-start(f32[6,16,128]{2,1,0:T(8,128)S(1)} %get-tuple-element.52), channel_id=1, source_target_pairs={{0,1},{1,0},{2,3},{3,2},{4,5},{5,4},{6,7},{7,6},{8,9},{9,8},{10,11... | collective-permute-start | bytes 147464 | tf_op jit(solution)/shard_map/ppermute | solution.py:546
  46.4 6.2 %collective-permute-start.10 = (f32[6,16,128]{2,1,0:T(8,128)S(1)}, f32[6,16,128]{2,1,0:T(8,128)S(1)}, u32[]{:S(2)}, u32[]{:S(2)}) collective-permute-start(f32[6,16,128]{2,1,0:T(8,128)S(1)} %get-tuple-element.53), channel_id=1, source_target_pairs={{0,2},{1,3},{2,0},{3,1},{4,6},{5,7},{6,4},{7,5},{8,10},{9,11},{10,... | collective-permute-start | bytes 147464 | tf_op jit(solution)/shard_map/ppermute | solution.py:546
  48.7 6.0 %collective-permute-start.11 = (f32[6,16,128]{2,1,0:T(8,128)S(1)}, f32[6,16,128]{2,1,0:T(8,128)S(1)}, u32[]{:S(2)}, u32[]{:S(2)}) collective-permute-start(f32[6,16,128]{2,1,0:T(8,128)S(1)} %get-tuple-element.54), channel_id=1, source_target_pairs={{0,3},{1,2},{2,1},{3,0},{4,7},{5,6},{6,5},{7,4},{8,11},{9,10},{10,... | collective-permute-start | bytes 147464 | tf_op jit(solution)/shard_map/ppermute | solution.py:546

commit v3 on v2

--- a/solution.py
+++ b/solution.py
@@ -17,7 +17,6 @@
 HARMONICS = 9
 NOISE = 0.05
 CODE_STEPS = 8192.0
-REST_STEPS = 32768.0
 VMEM_BYTES = 16 * 1024 * 1024
 
 SHORT = pl.CostEstimate(flops=1000, bytes_accessed=1000, transcendentals=0)
@@ -32,10 +31,6 @@
     return [(i, i ^ k) for i in range(count)]
 
 
-def ratio_steps(dates):
-    return 2.0 ** math.floor(math.log2(32767 / ((2 * RADIUS + 1) ** 2 * dates)))
-
-
 def edge_count(positions, length):
     lower = jnp.maximum(positions - RADIUS, 0)
     upper = jnp.minimum(positions + RADIUS, length - 1)
@@ -62,50 +57,32 @@
     return [slice(c, c + LANES) for c in range(0, width, LANES)]
 
 
-def flags_kernel(pieces, mask_ref, *refs):
+def flags_kernel(ks, mask_ref, *refs):
     r = lax.axis_index("row")
-    for k, out_ref in enumerate(refs[-pieces:]):
+    for k, out_ref in zip(ks, refs[-len(ks) :]):
         chunks = out_ref.shape[1]
         at = pl.multiple_of((r ^ k) * chunks, 16)
         out_ref[...] = mask_ref[:, pl.ds(at, chunks)].astype(f32).astype(jnp.bfloat16)
 
 
-def cast_flags(lines, pieces, after=()):
+def cast_flags(lines, pieces, ks, after=()):
     dates, count, lanes = lines.shape
     return pl.pallas_call(
-        functools.partial(flags_kernel, pieces),
+        functools.partial(flags_kernel, ks),
         in_specs=[whole()] + [anywhere()] * len(after),
-        out_specs=[whole()] * pieces,
-        out_shape=[pltpu.VMEM((dates, count // pieces, lanes), jnp.bfloat16)] * pieces,
+        out_specs=[whole()] * len(ks),
+        out_shape=[pltpu.VMEM((dates, count // pieces, lanes), jnp.bfloat16)] * len(ks),
         compiler_params=params(),
         cost_estimate=SHORT,
         name="cast_flags",
     )(lines, *after)
 
 
-def box_kernel(ks, parts, x_ref, *refs):
-    first_call = 1 not in parts
-    if first_call:
-        outs = refs[-7:-5]
-        refs[-5][...] = jnp.zeros_like(refs[-5])
-        band, sums, cells_ref, arrived = refs[-4:]
-        batch = x_ref.shape[0] // arrived.shape[0]
-        copies = [
-            pltpu.make_async_copy(
-                x_ref.at[pl.ds(n * batch, batch)],
-                cells_ref.at[pl.ds(n * batch, batch)],
-                arrived.at[n],
-            )
-            for n in range(arrived.shape[0])
-        ]
-        for copy in copies:
-            copy.start()
-        x_ref = cells_ref
-    else:
-        outs = refs[-6:-4]
-        refs[-4][...] = jnp.zeros_like(refs[-4])
-        band, sums, edges = refs[-3:]
-        batch = 4
+def box_kernel(ks, x_ref, *refs):
+    halo_ref, band = refs[:2]
+    *outs, token, sums, edges, scale_ref = refs[-4 - len(ks) :]
+    token[...] = jnp.zeros_like(token)
+    batch = 4
     d = lax.axis_index("date")
     r = lax.axis_index("row")
     dates, pols, rows, cols = x_ref.shape
@@ -115,22 +92,12 @@
     first = pl.multiple_of(half * (rows // 2 - 16), 16)
     images = dates * pols
 
-    near = (
-        jnp.abs(
-            lax.broadcasted_iota(i32, (cols, cols), 0) - lax.broadcasted_iota(i32, (cols, cols), 1)
-        )
-        <= RADIUS
-    )
-    band[...] = near.astype(f32).astype(jnp.bfloat16)
-    if 1 in parts:
-        edges[...] = jnp.dot(refs[0][...], band[...], preferred_element_type=f32)
-        place = jnp.where(half == 0, GROUP - HALO, GROUP + span)
-        for i in range(images):
-            for c, lanes in enumerate(tiles_of(cols)):
-                sums[i, c, pl.ds(place, HALO)] = edges[i * HALO : (i + 1) * HALO, lanes]
+    edges[...] = jnp.dot(halo_ref[...], band[...], preferred_element_type=f32)
+    place = jnp.where(half == 0, GROUP - HALO, GROUP + span)
+    for i in range(images):
+        for c, lanes in enumerate(tiles_of(cols)):
+            sums[i, c, pl.ds(place, HALO)] = edges[i * HALO : (i + 1) * HALO, lanes]
     for t in range(0, dates, batch):
-        if first_call:
-            copies[t // batch].wait()
         x = x_ref[t : t + batch, :, pl.ds(first, span), :].reshape(batch * pols * span, cols)
         summed = jnp.dot(x, band[...], preferred_element_type=f32)
         for i in range(batch * pols):
@@ -140,46 +107,49 @@
                 ]
 
     height = rows * lax.axis_size("row")
-    col = edge_count(lax.broadcasted_iota(i32, (GROUP, cols), 1), cols)
-    steps = ratio_steps(dates)
+    col = edge_count(lax.broadcasted_iota(i32, (quarter, cols), 1), cols)
     for n, k in enumerate(ks):
         q = d ^ k
-        for p, part in enumerate(parts):
-            group = half if part else 1 - half
-            top = quarter * q + GROUP * group
-            base = GROUP + top - first
-            row = edge_count(r * rows + top + lax.broadcasted_iota(i32, (GROUP, cols), 0), height)
-            scale = 1.0 / (row * col)
-            out = outs[n].at[p] if len(parts) > 1 else outs[n]
-            cells_at = pl.multiple_of(quarter * q, 16)
-
-            def add_date(t, totals):
-                new = []
-                for c, lanes in enumerate(tiles_of(cols)):
+        top = pl.multiple_of(quarter * q, 16)
+        base = GROUP + top - first
+        row = edge_count(r * rows + top + lax.broadcasted_iota(i32, (quarter, cols), 0), height)
+        scale_ref[...] = 1.0 / (row * col)
+        groups = range(quarter // GROUP)
+        places = [jnp.where(half == 0, 1 - g, g) for g in groups]
+
+        def add_date(t, totals):
+            new = []
+            for c, lanes in enumerate(tiles_of(cols)):
+                cells = [
+                    x_ref[t, pol, pl.ds(top, quarter), lanes].astype(f32) for pol in range(pols)
+                ]
+                for g in groups:
+                    down = slice(g * GROUP, (g + 1) * GROUP)
                     codes = []
                     for pol in range(pols):
                         i = t * pols + pol
-                        window = sums[i, c, pl.ds(base - RADIUS, GROUP)]
+                        start = base + g * GROUP
+                        window = sums[i, c, pl.ds(start - RADIUS, GROUP)]
                         for shift in range(1 - RADIUS, RADIUS + 1):
-                            window = window + sums[i, c, pl.ds(base + shift, GROUP)]
-                        mean = window * scale[:, lanes]
-                        both = x_ref[t, pol, pl.ds(cells_at, quarter), lanes].astype(f32)
-                        cells = jnp.where(group == 0, both[:GROUP], both[GROUP:])
-                        new.append(totals[c * pols + pol] + cells / mean)
+                            window = window + sums[i, c, pl.ds(start + shift, GROUP)]
+                        mean = window * scale_ref[down, lanes]
+                        inverse = pl.reciprocal(mean, approx=True)
+                        inverse = inverse * (2.0 - mean * inverse)
+                        new.append(totals[len(new)] + cells[pol][down] * inverse)
                         codes.append((jnp.log(mean) * CODE_STEPS - 0.5).astype(i32))
-                    out[t, :, lanes] = jnp.concatenate(codes, axis=0).astype(jnp.int16)
-                return tuple(new)
-
-            zero = jnp.zeros((GROUP, LANES), f32)
-            totals = lax.fori_loop(
-                0, dates, add_date, (zero,) * (pols * (cols // LANES)), unroll=2
-            )
-            for c, lanes in enumerate(tiles_of(cols)):
-                total = jnp.concatenate(totals[c * pols : (c + 1) * pols], axis=0) * steps
-                high = total.astype(i32)
-                rest = ((total - high.astype(f32)) * REST_STEPS).astype(i32)
-                out[dates, :, lanes] = high.astype(jnp.int16)
-                out[dates + 1, :, lanes] = rest.astype(jnp.int16)
+                    codes = jnp.concatenate(codes, axis=0).astype(jnp.int16)
+                    outs[n][places[g], t, :, lanes] = codes
+            return tuple(new)
+
+        zero = jnp.zeros((GROUP, LANES), f32)
+        totals = (zero,) * (pols * quarter // GROUP * (cols // LANES))
+        totals = list(lax.fori_loop(0, dates, add_date, totals, unroll=4))
+        for lanes in tiles_of(cols):
+            for g in groups:
+                total = jnp.concatenate([totals.pop(0) for _ in range(pols)], axis=0)
+                logs = jnp.log(total * (1.0 / dates)) * CODE_STEPS
+                code = (logs + 32768.5).astype(i32) - 32768
+                outs[n][places[g], dates, :, lanes] = code.astype(jnp.int16)
 
 
 def copy_edges(x_ref, out, bottom, dates):
@@ -194,7 +164,7 @@
             out[line : line + 16, lanes] = jnp.concatenate(images, axis=0).astype(out.dtype)
 
 
-def edges_kernel(x_ref, far_ref, near_ref, rows_ref, arrived):
+def edges_kernel(x_ref, far_ref, near_ref, band_ref, rows_ref, arrived):
     half = lax.axis_index("date") // 2
     dates, _, rows, _ = x_ref.shape
     sides = (half, 1 - half)
@@ -205,6 +175,14 @@
             pltpu.make_async_copy(x_ref.at[:, :, pl.ds(at, 16)], rows_ref.at[n], arrived.at[n])
         )
         copies[n].start()
+    cols = x_ref.shape[3]
+    near = (
+        jnp.abs(
+            lax.broadcasted_iota(i32, (cols, cols), 0) - lax.broadcasted_iota(i32, (cols, cols), 1)
+        )
+        <= RADIUS
+    )
+    band_ref[...] = near.astype(f32).astype(jnp.bfloat16)
     for n, out_ref in enumerate((far_ref, near_ref)):
         copies[n].wait()
         copy_edges(rows_ref.at[n], out_ref, sides[n], dates)
@@ -215,8 +193,9 @@
     return pl.pallas_call(
         edges_kernel,
         in_specs=[pl.BlockSpec(memory_space=pltpu.HBM)],
-        out_specs=[whole()] * 2,
-        out_shape=[pltpu.VMEM((dates * pols * HALO, cols), intensity.dtype)] * 2,
+        out_specs=[whole()] * 3,
+        out_shape=[pltpu.VMEM((dates * pols * HALO, cols), intensity.dtype)] * 2
+        + [pltpu.VMEM((cols, cols), jnp.bfloat16)],
         scratch_shapes=[
             pltpu.VMEM((2, dates, pols, 16, cols), intensity.dtype),
             pltpu.SemaphoreType.DMA((2,)),
@@ -227,33 +206,24 @@
     )(intensity)
 
 
-def box_codes(intensity, halos, ks, parts, after=()):
+def box_codes(intensity, halo, band, ks, after=()):
     dates, pols, rows, cols = intensity.shape
-    shape = (dates + 2, pols * GROUP, cols)
-    if len(parts) > 1:
-        shape = (len(parts),) + shape
-    out_shape = [pltpu.VMEM(shape, jnp.int16)] * len(ks)
-    scratch = [
-        pltpu.VMEM((cols, cols), jnp.bfloat16),
-        pltpu.VMEM((dates * pols, cols // LANES, rows // 2 + 32, LANES), f32),
-    ]
-    first_spec = whole()
-    out_shape += [pltpu.VMEM((GROUP, LANES), f32)]
-    if halos:
-        scratch += [pltpu.VMEM((dates * pols * HALO, cols), f32)]
-    else:
-        first_spec = pl.BlockSpec(memory_space=pltpu.HBM)
-        scratch += [pltpu.VMEM(intensity.shape, intensity.dtype), pltpu.SemaphoreType.DMA((4,))]
-    return pl.pallas_call(
-        functools.partial(box_kernel, ks, parts),
-        in_specs=[first_spec] + [whole()] * len(halos) + [anywhere()] * len(after),
+    codes = pltpu.VMEM((2, dates + 1, pols * GROUP, cols), jnp.int16)
+    out_shape = [codes] * len(ks) + [pltpu.VMEM((GROUP, LANES), f32)]
+    return pl.pallas_call(
+        functools.partial(box_kernel, ks),
+        in_specs=[whole()] * 3 + [anywhere()] * len(after),
         out_specs=[whole()] * len(out_shape),
         out_shape=out_shape,
-        scratch_shapes=scratch,
+        scratch_shapes=[
+            pltpu.VMEM((dates * pols, cols // LANES, rows // 2 + 32, LANES), f32),
+            pltpu.VMEM((dates * pols * HALO, cols), f32),
+            pltpu.VMEM((2 * GROUP, cols), f32),
+        ],
         compiler_params=params(),
         cost_estimate=SHORT,
         name="box_codes",
-    )(intensity, *halos, *after)
+    )(intensity, halo, band, *after)
 
 
 def factor_kernel(table_ref, mask_ref, *refs):
@@ -346,14 +316,13 @@
         return ref[(n, *index[1:])]
 
 
-def decode_ratio(block, dates, lanes):
-    high = block[dates, :, lanes].astype(i32).astype(f32)
-    rest = block[dates + 1, :, lanes].astype(i32).astype(f32)
-    return high + rest * (1.0 / REST_STEPS)
+def ratio_of(block, lanes):
+    code = block[block.shape[0] - 1, :, lanes].astype(i32).astype(f32)
+    return jnp.exp(code * (1.0 / CODE_STEPS))
 
 
 def add_logs(block, table_ref, start, flag_of, sums, tiles):
-    for t in range(block.shape[0] - 2):
+    for t in range(block.shape[0] - 1):
         weights = [table_ref[n, start + t] for n in range(STATES - 1)]
         for c, lanes in enumerate(tiles):
             logs = block[t, :, lanes].astype(i32).astype(f32)
@@ -366,8 +335,8 @@
             sums[c][STATES - 1] = sums[c][STATES - 1] + vh
 
 
-def right_of(sums, flag_sums, ratio, steps):
-    logs = jnp.log(ratio * (1.0 / steps))
+def right_of(sums, flag_sums, ratio, blocks):
+    logs = jnp.log(ratio * (1.0 / blocks))
     both = logs[:GROUP] + logs[GROUP:]
     right = [total * (1.0 / CODE_STEPS) for total in sums]
     for n in range(STATES - 1):
@@ -384,7 +353,7 @@
     r = lax.axis_index("row")
     dates, chunks, _ = flags_refs[0].shape
     parts, count, _, cols = near_ref.shape
-    local = count - 2
+    local = count - 1
     tiles = tiles_of(cols)
     zero = jnp.zeros((GROUP, LANES), f32)
     for k, flags_ref in enumerate(flags_refs):
@@ -414,7 +383,7 @@
                     for c, lanes in enumerate(tiles):
                         weigh(t, c, lanes)
         for c, lanes in enumerate(tiles):
-            ratios = [decode_ratio(block, local, lanes) for block in blocks]
+            ratios = [ratio_of(block, lanes) for block in blocks]
             ratio_ref[part, :, lanes] = ratios[0] + ratios[1]
             for n, total in enumerate(sums[c] + flag_sums[c]):
                 part_ref[part, n, :, lanes] = total
@@ -423,7 +392,7 @@
 def right_sides(table, flags, near):
     dates, chunks, _ = flags[0].shape
     parts, _, _, cols = near[0].shape
-    local = near[0].shape[1] - 2
+    local = near[0].shape[1] - 1
     shapes = [
         (parts, 2 * STATES - 1, GROUP, cols),
         (parts, 2 * GROUP, cols),
@@ -446,7 +415,7 @@
     d = lax.axis_index("date")
     r = lax.axis_index("row")
     parts, _, _, cols = far_2.shape
-    local = far_2.shape[1] - 2
+    local = far_2.shape[1] - 1
     tiles = tiles_of(cols)
     for part in range(parts):
         sums = [[part_ref[part, n, :, lanes] for n in range(STATES)] for lanes in tiles]
@@ -461,9 +430,9 @@
         for c, lanes in enumerate(tiles):
             ratio = ratio_ref[part, :, lanes]
             for block in blocks:
-                ratio = ratio + decode_ratio(block, local, lanes)
+                ratio = ratio + ratio_of(block, lanes)
             flag_sums = [part_ref[part, STATES + n, :, lanes] for n in range(STATES - 1)]
-            rights = right_of(sums[c], flag_sums, ratio, ratio_steps(local) * dates)
+            rights = right_of(sums[c], flag_sums, ratio, dates // local)
             for n, total in enumerate(rights):
                 right[n, pl.ds(start + c, GROUP, stride=len(tiles))] = total
     for k, out_ref in enumerate(out_refs):
@@ -558,25 +527,34 @@
         return lax.ppermute(cells, ("date", "row"), pairs)
 
     in_hbm = pltpu.with_memory_space_constraint(intensity, pltpu.HBM)
-    far_edge, near_edge = edge_rows(in_hbm)
+    far_edge, near_edge, band = edge_rows(in_hbm)
     far_halo = halo(far_edge, True)
     near_halo = halo(near_edge, False)
+    last = row_devices - 1
+    ready = ()
     if direct:
-        flags = cast_flags(lines, row_devices, after=(far_edge,))
-        ready = flags[:1]
-        flags = [flags[0]] + [exchange(flags[k], "row", k) for k in range(1, row_devices)]
+        flags = dict(zip((0, last), cast_flags(lines, row_devices, (0, last), after=(far_edge,))))
+        ready = (flags[0],)
+        flags[last] = exchange(flags[last], "row", last)
+    *far, done = box_codes(intensity, far_halo, band, (2, 3), after=(table, *ready))
+    far = [exchange(far[0], "date", 2), exchange(far[1], "date", 3)]
+    if direct:
+        ks = tuple(range(1, last))
+        for k, piece in zip(ks, cast_flags(lines, row_devices, ks, after=(done,)) if ks else ()):
+            flags[k] = exchange(piece, "row", k)
+        flags = [flags[k] for k in range(row_devices)]
+        ready = (flags[last],)
     else:
-        ready = ()
         flags = lax.all_to_all(
             valid_mask.astype(jnp.bfloat16), "row", split_axis=1, concat_axis=2, tiled=True
         )
         flags = [flags.reshape(all_dates, lines_count, LANES)]
-    *far, done = box_codes(intensity, (far_halo,), (2, 3), (0, 1), after=(table, *ready))
-    far = [exchange(far[0], "date", 2), exchange(far[1], "date", 3)]
-    *near, done = box_codes(intensity, (near_halo,), (0, 1), (0, 1), after=(done,))
+    *near, done = box_codes(intensity, near_halo, band, (0, 1), after=(done, *ready))
+    near = [near[0], near[1]]
+    factors = factor(table, lines, after=(done,))
     other = near[1].reshape(-1, *near[1].shape[2:])
     count = other.shape[0]
-    cut = 2 * count // 3
+    cut = count // 2
     other = [other[:cut], other[cut:]]
     other, flags = lax.optimization_barrier((other, flags))
     near = [near[0]] + [exchange(codes, "date", 1) for codes in other]

time: 55.7 us -> 51.8 us (0.930)
  waiting for transfers between devices: 19 us -> 14.9 us
  starting transfers between devices: 18.3 us -> 19.6 us
  Pallas kernels: 16.3 us -> 15.3 us
    ppermute x10, waiting for transfers between devices: 19 us -> 14.9 us  [exchange(): return lax.ppermute(piece, axis, partners(lax.axis_size(axis), k))]
    ppermute x10, starting transfers between devices: 12 us -> 13.3 us  [exchange(): return lax.ppermute(piece, axis, partners(lax.axis_size(axis), k))]
    pallas_call x3 -> x4, Pallas kernels: 7.64 us -> 6.58 us  [the longest x2 6.44 us: box_codes(): pl.pallas_call(functools.partial(box_kernel, ks), in_specs=[whole()] * 3...]
  transfers between devices with their start and end apart: 12 -> 12, of which waited for: 4 -> 5; matrix products, arithmetic and copies ran while one was open for 0% -> 0% of each run, Pallas kernels for 23% -> 22%
where the time goes in v3:
time: 51.8 us; the launch traced here: 51.6 us
  starting transfers between devices  19.6 us (38%)
  Pallas kernels  15.3 us (30%)
  waiting for transfers between devices  14.9 us (29%)
  local copies, waits for them, and re-layouts  1.64 us (3%)
    ppermute x10, waiting for transfers between devices, exchange(): return lax.ppermute(piece, axis, partners(lax.axis_size(axis), k))  14.9 us
    ppermute x10, starting transfers between devices, exchange(): return lax.ppermute(piece, axis, partners(lax.axis_size(axis), k))  13.3 us
    pallas_call x2, Pallas kernels, box_codes(): pl.pallas_call(functools.partial(box_kernel, ks), in_specs=[whole()] * 3...  6.44 us
    ppermute x2, starting transfers between devices, halo(): return lax.ppermute(cells, ('date', 'row'), pairs)  6.24 us
    pallas_call x1, Pallas kernels, right_sides(): pl.pallas_call(functools.partial(right_kernel, len(flags)), in_specs=[sca...  2.54 us
    pallas_call x1, Pallas kernels, factor(): pl.pallas_call(factor_kernel, in_specs=[scalars(), whole()] + [anywhere()...  2.48 us
    unnamed x12, local copies, waits for them, and re-layouts  1.6 us
    pallas_call x1, Pallas kernels, edge_rows(): pl.pallas_call(edges_kernel, in_specs=[pl.BlockSpec(memory_space=pltpu.HB...  1.49 us
  transfers between devices with their start and end apart: 12, of which 5 were waited for; matrix products, arithmetic and copies ran while one was open for 0% of the time, Pallas kernels for 22%

profile of v3, /device:TPU:0, one launch (start us, length us, event | category | flops | bytes accessed | tf_op | source)
XLA Modules:
  0.0 51.6 jit_solution(12045342828141597897)
XLA Ops:
  0.0 0.0 copy-start.3
  0.0 0.0 copy-start.4
  0.0 0.0 copy-start
  0.0 0.0 copy-start.5
  0.0 1.5 %edge_rows.1 = (bf16[128,512]{1,0:T(8,128)(2,1)S(1)}, bf16[128,512]{1,0:T(8,128)(2,1)S(1)}, bf16[512,512]{1,0:T(8,128)(2,1)S(1)}) custom-call(bf16[16,2,64,512]{3,2,1,0:T(8,128)(2,1)} %x_ref.5), custom_call_target="tpu_custom_call" | custom-call | flops 1000 | bytes 1000 | tf_op jit(solution)/shard_map/edge_rows/pallas_call | solution.py:193
  1.5 4.9 %collective-permute-start = (bf16[128,512]{1,0:T(8,128)(2,1)S(1)}, bf16[128,512]{1,0:T(8,128)(2,1)S(1)}, u32[]{:S(2)}, u32[]{:S(2)}) collective-permute-start(bf16[128,512]{1,0:T(8,128)(2,1)S(1)} %get-tuple-element.31), channel_id=1, source_target_pairs={{0,1},{1,2},{2,3},{4,5},{5,6},{6,7},{9,8},{10,9},{11,10},{13,12},{... | collective-permute-start | bytes 393224 | tf_op jit(solution)/shard_map/ppermute | solution.py:527
  6.5 1.3 %collective-permute-start.1 = (bf16[128,512]{1,0:T(8,128)(2,1)S(1)}, bf16[128,512]{1,0:T(8,128)(2,1)S(1)}, u32[]{:S(2)}, u32[]{:S(2)}) collective-permute-start(bf16[128,512]{1,0:T(8,128)(2,1)S(1)} %get-tuple-element.33.refs_0_), channel_id=1, source_target_pairs={{1,0},{2,1},{3,2},{5,4},{6,5},{7,6},{8,9},{9,10},{10,11},{12,13},{... | collective-permute-start | bytes 393224 | tf_op jit(solution)/shard_map/ppermute | solution.py:527
  7.8 0.0 copy-start.1
  7.8 1.6 %copy-done.1 = s32[64,4,1,2048]{3,2,1,0:T(1,128)S(1)} copy-done((s32[64,4,1,2048]{3,2,1,0:T(1,128)S(1)}, s32[64,4,1,2048]{3,2,1,0:T(1,128)}, u32[]{:S(2)}) %copy-start.1) | copy-done | bytes 2097176
  9.4 0.0 copy-start.2
  9.4 0.1 cast_flags.2
  9.4 4.7 %collective-permute-start.2 = (bf16[64,16,128]{2,1,0:T(8,128)(2,1)S(1)}, bf16[64,16,128]{2,1,0:T(8,128)(2,1)S(1)}, u32[]{:S(2)}, u32[]{:S(2)}) collective-permute-start(bf16[64,16,128]{2,1,0:T(8,128)(2,1)S(1)} %get-tuple-element.36), channel_id=1, source_target_pairs={{0,3},{1,2},{2,1},{3,0},{4,7},{5,6},{6,5},{7,4},{8,11},{9,10},{10,... | collective-permute-start | bytes 786440 | tf_op jit(solution)/shard_map/ppermute | solution.py:515
  14.2 0.0 copy-done.5
  14.2 0.0 copy-done.3
  14.2 0.0 copy-done.4
  14.2 0.1 fusion.refs_2_.table_ref
  14.3 0.0 collective-permute-done.1.refs_0_
  14.3 0.0 copy-done
  14.3 3.2 %box_codes.2 = (s16[2,17,16,512]{3,2,1,0:T(8,128)(2,1)S(1)}, s16[2,17,16,512]{3,2,1,0:T(8,128)(2,1)S(1)}, f32[8,128]{1,0:T(8,128)S(1)}) custom-call(bf16[16,2,64,512]{3,2,1,0:T(8,128)(2,1)S(1)} %copy-done, bf16[128,512]{1,0:T(8,128)(2,1)S(1)} %collective-permute-done.1.refs_0_, bf16[512,512]{1,0:T(8,128)(2,1)S(1)} %get-tuple-element.32.refs_1_, ...), custom_call_target="tpu_custom_call" | custom-call | flops 1000 | bytes 1000 | tf_op jit(solution)/shard_map/box_codes/pallas_call | solution.py:213
  17.6 0.1 collective-permute-start.7
  17.6 0.3 collective-permute-start.8
  18.0 0.0 copy-done.2
  18.0 0.1 cast_flags.3
  18.0 2.4 %collective-permute-start.3 = (bf16[64,16,128]{2,1,0:T(8,128)(2,1)S(1)}, bf16[64,16,128]{2,1,0:T(8,128)(2,1)S(1)}, u32[]{:S(2)}, u32[]{:S(2)}) collective-permute-start(bf16[64,16,128]{2,1,0:T(8,128)(2,1)S(1)} %get-tuple-element.39), channel_id=1, source_target_pairs={{0,1},{1,0},{2,3},{3,2},{4,5},{5,4},{6,7},{7,6},{8,9},{9,8},{10,11... | collective-permute-start | bytes 786440 | tf_op jit(solution)/shard_map/ppermute | solution.py:515
  20.5 0.0 collective-permute-done.refs_0_
  20.5 0.8 %collective-permute-start.4 = (bf16[64,16,128]{2,1,0:T(8,128)(2,1)S(1)}, bf16[64,16,128]{2,1,0:T(8,128)(2,1)S(1)}, u32[]{:S(2)}, u32[]{:S(2)}) collective-permute-start(bf16[64,16,128]{2,1,0:T(8,128)(2,1)S(1)} %get-tuple-element.40), channel_id=1, source_target_pairs={{0,2},{1,3},{2,0},{3,1},{4,6},{5,7},{6,4},{7,5},{8,10},{9,11},{10,... | collective-permute-start | bytes 786440 | tf_op jit(solution)/shard_map/ppermute | solution.py:515
  21.3 0.0 collective-permute-done.2.refs_3_
  21.3 3.2 %box_codes.3 = (s16[2,17,16,512]{3,2,1,0:T(8,128)(2,1)S(1)}, s16[2,17,16,512]{3,2,1,0:T(8,128)(2,1)S(1)}, f32[8,128]{1,0:T(8,128)S(1)}) custom-call(bf16[16,2,64,512]{3,2,1,0:T(8,128)(2,1)S(1)} %copy-done, bf16[128,512]{1,0:T(8,128)(2,1)S(1)} %collective-permute-done.refs_0_, bf16[512,512]{1,0:T(8,128)(2,1)S(1)} %get-tuple-element.32.refs_1_, ...), custom_call_target="tpu_custom_call" | custom-call | flops 1000 | bytes 1000 | tf_op jit(solution)/shard_map/box_codes/pallas_call | solution.py:213
  24.6 4.8 %collective-permute-done.3.refs_1_ = bf16[64,16,128]{2,1,0:T(8,128)(2,1)S(1)} collective-permute-done((bf16[64,16,128]{2,1,0:T(8,128)(2,1)S(1)}, bf16[64,16,128]{2,1,0:T(8,128)(2,1)S(1)}, u32[]{:S(2)}, u32[]{:S(2)}) %collective-permute-start.3) | collective-permute-done | bytes 262176 | tf_op jit(solution)/shard_map/ppermute | solution.py:515
  29.4 7.3 %collective-permute-done.4.refs_2_ = bf16[64,16,128]{2,1,0:T(8,128)(2,1)S(1)} collective-permute-done((bf16[64,16,128]{2,1,0:T(8,128)(2,1)S(1)}, bf16[64,16,128]{2,1,0:T(8,128)(2,1)S(1)}, u32[]{:S(2)}, u32[]{:S(2)}) %collective-permute-start.4) | collective-permute-done | bytes 262176 | tf_op jit(solution)/shard_map/ppermute | solution.py:515
  36.6 0.1 collective-permute-start.5
  36.8 0.4 collective-permute-start.6
  37.1 1.0 %collective-permute-done.5.refs_5_ = s16[17,16,512]{2,1,0:T(8,128)(2,1)S(1)} collective-permute-done((s16[17,16,512]{2,1,0:T(8,128)(2,1)S(1)}, s16[17,16,512]{2,1,0:T(8,128)(2,1)S(1)}, u32[]{:S(2)}, u32[]{:S(2)}) %collective-permute-start.5) | collective-permute-done | bytes 278560 | tf_op jit(solution)/shard_map/ppermute | solution.py:515
  38.2 0.4 collective-permute-done.6.refs_6_
  38.6 2.5 %right_sides.1 = (f32[2,11,8,512]{3,2,1,0:T(8,128)S(1)}, f32[2,16,512]{2,1,0:T(8,128)S(1)}, f32[2,32,8,512]{3,2,1,0:T(8,128)S(1)}) custom-call(f32[9,64]{1,0:T(8,128)S(1)} %fusion.refs_2_.table_ref, bf16[64,16,128]{2,1,0:T(8,128)(2,1)S(1)} %get-tuple-element.41.refs_3_.refs_0_, bf16[64,16,128]{2,1,0:T(8,128)(2,1)S(1)} %collective-permute-done.3.refs_1_, ...), custom_call_target="tpu_custom_call" | custom-call | flops 1000 | bytes 1000 | tf_op jit(solution)/shard_map/right_sides/pallas_call | solution.py:401
  41.1 0.0 collective-permute-done.7.far_2
  41.2 0.0 collective-permute-done.8.far_3
  41.2 1.4 %finish_sides.1 = (f32[6,16,128]{2,1,0:T(8,128)S(1)}, f32[6,16,128]{2,1,0:T(8,128)S(1)}, f32[6,16,128]{2,1,0:T(8,128)S(1)}, f32[6,16,128]{2,1,0:T(8,128)S(1)}) custom-call(f32[9,64]{1,0:T(8,128)S(1)} %fusion.refs_2_.table_ref, f32[2,11,8,512]{3,2,1,0:T(8,128)S(1)} %get-tuple-element.48.part_ref, f32[2,16,512]{2,1,0:T(8,128)S(1)} %get-tuple-element.49.ratio_ref, ...), custom_call_target="tpu_custom_call" | custom-call | flops 1000 | bytes 1000 | tf_op jit(solution)/shard_map/finish_sides/pallas_call | solution.py:447
  42.5 0.5 %collective-permute-start.9 = (f32[6,16,128]{2,1,0:T(8,128)S(1)}, f32[6,16,128]{2,1,0:T(8,128)S(1)}, u32[]{:S(2)}, u32[]{:S(2)}) collective-permute-start(f32[6,16,128]{2,1,0:T(8,128)S(1)} %get-tuple-element.54), channel_id=1, source_target_pairs={{0,1},{1,0},{2,3},{3,2},{4,5},{5,4},{6,7},{7,6},{8,9},{9,8},{10,11... | collective-permute-start | bytes 147464 | tf_op jit(solution)/shard_map/ppermute | solution.py:515
  43.1 1.9 %collective-permute-start.10 = (f32[6,16,128]{2,1,0:T(8,128)S(1)}, f32[6,16,128]{2,1,0:T(8,128)S(1)}, u32[]{:S(2)}, u32[]{:S(2)}) collective-permute-start(f32[6,16,128]{2,1,0:T(8,128)S(1)} %get-tuple-element.55), channel_id=1, source_target_pairs={{0,2},{1,3},{2,0},{3,1},{4,6},{5,7},{6,4},{7,5},{8,10},{9,11},{10,... | collective-permute-start | bytes 147464 | tf_op jit(solution)/shard_map/ppermute | solution.py:515
  45.0 2.0 %collective-permute-start.11 = (f32[6,16,128]{2,1,0:T(8,128)S(1)}, f32[6,16,128]{2,1,0:T(8,128)S(1)}, u32[]{:S(2)}, u32[]{:S(2)}) collective-permute-start(f32[6,16,128]{2,1,0:T(8,128)S(1)} %get-tuple-element.56), channel_id=1, source_target_pairs={{0,3},{1,2},{2,1},{3,0},{4,7},{5,6},{6,5},{7,4},{8,11},{9,10},{10,... | collective-permute-start | bytes 147464 | tf_op jit(solution)/shard_map/ppermute | solution.py:515
  47.0 2.5 %factor.1.factor_ref = f32[21,64,128]{2,1,0:T(8,128)S(1)} custom-call(f32[9,64]{1,0:T(8,128)S(1)} %fusion.refs_2_.table_ref, s32[64,64,128]{2,1,0:T(8,128)S(1)} %bitcast.8, f32[8,128]{1,0:T(8,128)S(1)} %get-tuple-element.37.refs_0_), custom_call_target="tpu_custom_call" | custom-call | flops 1000 | bytes 1000 | tf_op jit(solution)/shard_map/factor/pallas_call | solution.py:297
  49.5 0.0 collective-permute-done.9.refs_1_
  49.5 0.0 collective-permute-done.10.refs_2_
  49.5 1.3 %collective-permute-done.11.refs_3_ = f32[6,16,128]{2,1,0:T(8,128)S(1)} collective-permute-done((f32[6,16,128]{2,1,0:T(8,128)S(1)}, f32[6,16,128]{2,1,0:T(8,128)S(1)}, u32[]{:S(2)}, u32[]{:S(2)}) %collective-permute-start.11) | collective-permute-done | bytes 49184 | tf_op jit(solution)/shard_map/ppermute | solution.py:515
  50.9 0.8 %solve.1 = f32[6,64,128]{2,1,0:T(8,128)} custom-call(f32[21,64,128]{2,1,0:T(8,128)S(1)} %factor.1.factor_ref, f32[6,16,128]{2,1,0:T(8,128)S(1)} %get-tuple-element.53.refs_0_, f32[6,16,128]{2,1,0:T(8,128)S(1)} %collective-permute-done.9.refs_1_, f32[6,16,128]{2,1,0:T(8,128)S(1)} %collective-permute-done.10.refs_2_, ...), custom_call_target="tpu_custom_call" | custom-call | flops 1000 | bytes 1000 | tf_op jit(solution)/shard_map/solve/pallas_call | solution.py:485
  (2 shorter events, 0.0 us)
Async XLA Ops:
  0.0 14.2 %copy-start.3 = (f32[9]{0:T(128)S(1)}, f32[9]{0:T(128)}, u32[]{:S(2)}) copy-start(f32[9]{0:T(128)} %constant.10) | copy-start | bytes 112
  0.0 14.2 %copy-start.4 = (pred[9]{0:T(512)(128)(4,1)S(1)}, pred[9]{0:T(512)(128)(4,1)}, u32[]{:S(2)}) copy-start(pred[9]{0:T(512)(128)(4,1)} %constant.9) | copy-start | bytes 31
  0.0 14.3 %copy-start = (bf16[16,2,64,512]{3,2,1,0:T(8,128)(2,1)S(1)}, bf16[16,2,64,512]{3,2,1,0:T(8,128)(2,1)}, u32[]{:S(2)}) copy-start(bf16[16,2,64,512]{3,2,1,0:T(8,128)(2,1)} %x_ref.5) | copy-start | bytes 6291460
  0.0 14.2 %copy-start.5 = (s32[64]{0:T(128)S(1)}, s32[64]{0:T(128)}, u32[]{:S(2)}) copy-start(s32[64]{0:T(128)} %param.7) | copy-start | bytes 772
  1.5 19.0 %collective-permute-start = (bf16[128,512]{1,0:T(8,128)(2,1)S(1)}, bf16[128,512]{1,0:T(8,128)(2,1)S(1)}, u32[]{:S(2)}, u32[]{:S(2)}) collective-permute-start(bf16[128,512]{1,0:T(8,128)(2,1)S(1)} %get-tuple-element.31), channel_id=1, source_target_pairs={{0,1},{1,2},{2,3},{4,5},{5,6},{6,7},{9,8},{10,9},{11,10},{13,12},{... | collective-permute-start | bytes 393224 | tf_op jit(solution)/shard_map/ppermute | solution.py:527
  6.5 7.9 %collective-permute-start.1 = (bf16[128,512]{1,0:T(8,128)(2,1)S(1)}, bf16[128,512]{1,0:T(8,128)(2,1)S(1)}, u32[]{:S(2)}, u32[]{:S(2)}) collective-permute-start(bf16[128,512]{1,0:T(8,128)(2,1)S(1)} %get-tuple-element.33.refs_0_), channel_id=1, source_target_pairs={{1,0},{2,1},{3,2},{5,4},{6,5},{7,6},{8,9},{9,10},{10,11},{12,13},{... | collective-permute-start | bytes 393224 | tf_op jit(solution)/shard_map/ppermute | solution.py:527
  7.8 1.6 %copy-start.1 = (s32[64,4,1,2048]{3,2,1,0:T(1,128)S(1)}, s32[64,4,1,2048]{3,2,1,0:T(1,128)}, u32[]{:S(2)}) copy-start(s32[64,4,1,2048]{3,2,1,0:T(1,128)} %param.6) | copy-start | bytes 6291460
  9.4 8.6 %copy-start.2 = (s32[64,4,1,2048]{3,2,1,0:T(1,128)S(1)}, s32[64,4,1,2048]{3,2,1,0:T(1,128)}, u32[]{:S(2)}) copy-start(s32[64,4,1,2048]{3,2,1,0:T(1,128)} %param.6) | copy-start | bytes 6291460
  9.4 11.9 %collective-permute-start.2 = (bf16[64,16,128]{2,1,0:T(8,128)(2,1)S(1)}, bf16[64,16,128]{2,1,0:T(8,128)(2,1)S(1)}, u32[]{:S(2)}, u32[]{:S(2)}) collective-permute-start(bf16[64,16,128]{2,1,0:T(8,128)(2,1)S(1)} %get-tuple-element.36), channel_id=1, source_target_pairs={{0,3},{1,2},{2,1},{3,0},{4,7},{5,6},{6,5},{7,4},{8,11},{9,10},{10,... | collective-permute-start | bytes 786440 | tf_op jit(solution)/shard_map/ppermute | solution.py:515
  17.6 23.6 %collective-permute-start.7 = (s16[2,17,16,512]{3,2,1,0:T(8,128)(2,1)S(1)}, s16[2,17,16,512]{3,2,1,0:T(8,128)(2,1)S(1)}, u32[]{:S(2)}, u32[]{:S(2)}) collective-permute-start(s16[2,17,16,512]{3,2,1,0:T(8,128)(2,1)S(1)} %get-tuple-element.51), channel_id=1, source_target_pairs={{0,8},{4,12},{8,0},{12,4},{1,9},{5,13},{9,1},{13,5},{2,10},{6,14},... | collective-permute-start | bytes 1671176 | tf_op jit(solution)/shard_map/ppermute | solution.py:515
  17.6 23.5 %collective-permute-start.8 = (s16[2,17,16,512]{3,2,1,0:T(8,128)(2,1)S(1)}, s16[2,17,16,512]{3,2,1,0:T(8,128)(2,1)S(1)}, u32[]{:S(2)}, u32[]{:S(2)}) collective-permute-start(s16[2,17,16,512]{3,2,1,0:T(8,128)(2,1)S(1)} %get-tuple-element.52), channel_id=1, source_target_pairs={{0,12},{4,8},{8,4},{12,0},{1,13},{5,9},{9,5},{13,1},{2,14},{6,10},... | collective-permute-start | bytes 1671176 | tf_op jit(solution)/shard_map/ppermute | solution.py:515
  18.0 11.3 %collective-permute-start.3 = (bf16[64,16,128]{2,1,0:T(8,128)(2,1)S(1)}, bf16[64,16,128]{2,1,0:T(8,128)(2,1)S(1)}, u32[]{:S(2)}, u32[]{:S(2)}) collective-permute-start(bf16[64,16,128]{2,1,0:T(8,128)(2,1)S(1)} %get-tuple-element.39), channel_id=1, source_target_pairs={{0,1},{1,0},{2,3},{3,2},{4,5},{5,4},{6,7},{7,6},{8,9},{9,8},{10,11... | collective-permute-start | bytes 786440 | tf_op jit(solution)/shard_map/ppermute | solution.py:515
  20.5 16.2 %collective-permute-start.4 = (bf16[64,16,128]{2,1,0:T(8,128)(2,1)S(1)}, bf16[64,16,128]{2,1,0:T(8,128)(2,1)S(1)}, u32[]{:S(2)}, u32[]{:S(2)}) collective-permute-start(bf16[64,16,128]{2,1,0:T(8,128)(2,1)S(1)} %get-tuple-element.40), channel_id=1, source_target_pairs={{0,2},{1,3},{2,0},{3,1},{4,6},{5,7},{6,4},{7,5},{8,10},{9,11},{10,... | collective-permute-start | bytes 786440 | tf_op jit(solution)/shard_map/ppermute | solution.py:515
  36.6 1.6 %collective-permute-start.5 = (s16[17,16,512]{2,1,0:T(8,128)(2,1)S(1)}, s16[17,16,512]{2,1,0:T(8,128)(2,1)S(1)}, u32[]{:S(2)}, u32[]{:S(2)}) collective-permute-start(s16[17,16,512]{2,1,0:T(8,128)(2,1)S(1)} %get-tuple-element.46), channel_id=1, source_target_pairs={{0,4},{4,0},{8,12},{12,8},{1,5},{5,1},{9,13},{13,9},{2,6},{6,2},{1... | collective-permute-start | bytes 835592 | tf_op jit(solution)/shard_map/ppermute | solution.py:515
  36.8 1.8 %collective-permute-start.6 = (s16[17,16,512]{2,1,0:T(8,128)(2,1)S(1)}, s16[17,16,512]{2,1,0:T(8,128)(2,1)S(1)}, u32[]{:S(2)}, u32[]{:S(2)}) collective-permute-start(s16[17,16,512]{2,1,0:T(8,128)(2,1)S(1)} %get-tuple-element.47), channel_id=1, source_target_pairs={{0,4},{4,0},{8,12},{12,8},{1,5},{5,1},{9,13},{13,9},{2,6},{6,2},{1... | collective-permute-start | bytes 835592 | tf_op jit(solution)/shard_map/ppermute | solution.py:515
  42.5 6.9 %collective-permute-start.9 = (f32[6,16,128]{2,1,0:T(8,128)S(1)}, f32[6,16,128]{2,1,0:T(8,128)S(1)}, u32[]{:S(2)}, u32[]{:S(2)}) collective-permute-start(f32[6,16,128]{2,1,0:T(8,128)S(1)} %get-tuple-element.54), channel_id=1, source_target_pairs={{0,1},{1,0},{2,3},{3,2},{4,5},{5,4},{6,7},{7,6},{8,9},{9,8},{10,11... | collective-permute-start | bytes 147464 | tf_op jit(solution)/shard_map/ppermute | solution.py:515
  43.1 6.4 %collective-permute-start.10 = (f32[6,16,128]{2,1,0:T(8,128)S(1)}, f32[6,16,128]{2,1,0:T(8,128)S(1)}, u32[]{:S(2)}, u32[]{:S(2)}) collective-permute-start(f32[6,16,128]{2,1,0:T(8,128)S(1)} %get-tuple-element.55), channel_id=1, source_target_pairs={{0,2},{1,3},{2,0},{3,1},{4,6},{5,7},{6,4},{7,5},{8,10},{9,11},{10,... | collective-permute-start | bytes 147464 | tf_op jit(solution)/shard_map/ppermute | solution.py:515
  45.0 5.9 %collective-permute-start.11 = (f32[6,16,128]{2,1,0:T(8,128)S(1)}, f32[6,16,128]{2,1,0:T(8,128)S(1)}, u32[]{:S(2)}, u32[]{:S(2)}) collective-permute-start(f32[6,16,128]{2,1,0:T(8,128)S(1)} %get-tuple-element.56), channel_id=1, source_target_pairs={{0,3},{1,2},{2,1},{3,0},{4,7},{5,6},{6,5},{7,4},{8,11},{9,10},{10,... | collective-permute-start | bytes 147464 | tf_op jit(solution)/shard_map/ppermute | solution.py:515

commit v4 on v3

--- a/solution.py
+++ b/solution.py
@@ -321,11 +321,13 @@
     return jnp.exp(code * (1.0 / CODE_STEPS))
 
 
-def add_logs(block, table_ref, start, flag_of, sums, tiles):
+def add_logs(block, table_ref, start, flag_of, sums, tiles, more=None):
     for t in range(block.shape[0] - 1):
         weights = [table_ref[n, start + t] for n in range(STATES - 1)]
         for c, lanes in enumerate(tiles):
             logs = block[t, :, lanes].astype(i32).astype(f32)
+            if more is not None:
+                logs = logs + more[c]
             flag = flag_of(t, c, lanes)
             vh = logs[GROUP:] * flag
             both = logs[:GROUP] * flag + vh
@@ -333,16 +335,6 @@
             for n in range(1, STATES - 1):
                 sums[c][n] = sums[c][n] + both * weights[n]
             sums[c][STATES - 1] = sums[c][STATES - 1] + vh
-
-
-def right_of(sums, flag_sums, ratio, blocks):
-    logs = jnp.log(ratio * (1.0 / blocks))
-    both = logs[:GROUP] + logs[GROUP:]
-    right = [total * (1.0 / CODE_STEPS) for total in sums]
-    for n in range(STATES - 1):
-        right[n] = right[n] + both * flag_sums[n]
-    right[STATES - 1] = right[STATES - 1] + logs[GROUP:] * flag_sums[0]
-    return right
 
 
 def right_kernel(pieces, table_ref, *refs):
@@ -369,8 +361,6 @@
 
             def weigh(t, c, lanes):
                 flag = lines[date + t, pl.ds(start + c, GROUP, stride=len(tiles))]
-                if k >= 2:
-                    flags_out[part, (k - 2) * local + t, :, lanes] = flag
                 flag_sums[c][0] = flag_sums[c][0] + flag
                 for n in range(1, STATES - 1):
                     flag_sums[c][n] = flag_sums[c][n] + flag * table_ref[n, date + t]
@@ -381,7 +371,8 @@
             else:
                 for t in range(local):
                     for c, lanes in enumerate(tiles):
-                        weigh(t, c, lanes)
+                        flag = lines[date + t, pl.ds(start + c, GROUP, stride=len(tiles))]
+                        flags_out[part, (k - 2) * local + t, :, lanes] = flag
         for c, lanes in enumerate(tiles):
             ratios = [ratio_of(block, lanes) for block in blocks]
             ratio_ref[part, :, lanes] = ratios[0] + ratios[1]
@@ -420,19 +411,26 @@
     for part in range(parts):
         sums = [[part_ref[part, n, :, lanes] for n in range(STATES)] for lanes in tiles]
         blocks = (far_2.at[part], far_3.at[part])
-        for k, block in enumerate(blocks):
-
-            def flag_of(t, c, lanes):
-                return flags_ref[part, k * local + t, :, lanes]
-
-            add_logs(block, table_ref, (d ^ (k + 2)) * local, flag_of, sums, tiles)
-        start = (d // 2 if part else 1 - d // 2) * GROUP * len(tiles)
-        for c, lanes in enumerate(tiles):
+        more = []
+        for lanes in tiles:
             ratio = ratio_ref[part, :, lanes]
             for block in blocks:
                 ratio = ratio + ratio_of(block, lanes)
+            more.append(jnp.log(ratio * (local / dates)) * CODE_STEPS)
+        for k, block in enumerate(blocks):
+
+            def flag_of(t, c, lanes):
+                return flags_ref[part, k * local + t, :, lanes]
+
+            add_logs(block, table_ref, (d ^ (k + 2)) * local, flag_of, sums, tiles, more)
+        start = (d // 2 if part else 1 - d // 2) * GROUP * len(tiles)
+        for c, lanes in enumerate(tiles):
             flag_sums = [part_ref[part, STATES + n, :, lanes] for n in range(STATES - 1)]
-            rights = right_of(sums[c], flag_sums, ratio, dates // local)
+            more_vh = more[c][GROUP:]
+            both = more[c][:GROUP] + more_vh
+            rights = [sums[c][n] + both * flag_sums[n] for n in range(STATES - 1)]
+            rights.append(sums[c][STATES - 1] + more_vh * flag_sums[0])
+            rights = [total * (1.0 / CODE_STEPS) for total in rights]
             for n, total in enumerate(rights):
                 right[n, pl.ds(start + c, GROUP, stride=len(tiles))] = total
     for k, out_ref in enumerate(out_refs):

time: 51.8 us -> 51.9 us (level)
  Pallas kernels: 15.3 us -> 14.6 us
  waiting for transfers between devices: 14.9 us -> 15.6 us
    ppermute x10, waiting for transfers between devices: 14.9 us -> 15.6 us  [exchange(): return lax.ppermute(piece, axis, partners(lax.axis_size(axis), k))]
    pallas_call x1, Pallas kernels: 2.54 us -> 1.79 us  [right_sides(): pl.pallas_call(functools.partial(right_kernel, len(flags)), in_specs=[sca...]
  transfers between devices with their start and end apart: 12 -> 12, of which waited for: 5 -> 6; matrix products, arithmetic and copies ran while one was open for 0% -> 0% of each run, Pallas kernels for 22% -> 21%
where the time goes in v4:
time: 51.9 us; the launch traced here: 51.7 us
  starting transfers between devices  19.6 us (38%)
  waiting for transfers between devices  15.6 us (30%)
  Pallas kernels  14.6 us (28%)
  local copies, waits for them, and re-layouts  1.64 us (3%)
    ppermute x10, waiting for transfers between devices, exchange(): return lax.ppermute(piece, axis, partners(lax.axis_size(axis), k))  15.6 us
    ppermute x10, starting transfers between devices, exchange(): return lax.ppermute(piece, axis, partners(lax.axis_size(axis), k))  13.3 us
    pallas_call x2, Pallas kernels, box_codes(): pl.pallas_call(functools.partial(box_kernel, ks), in_specs=[whole()] * 3...  6.44 us
    ppermute x2, starting transfers between devices, halo(): return lax.ppermute(cells, ('date', 'row'), pairs)  6.24 us
    pallas_call x1, Pallas kernels, factor(): pl.pallas_call(factor_kernel, in_specs=[scalars(), whole()] + [anywhere()...  2.48 us
    pallas_call x1, Pallas kernels, right_sides(): pl.pallas_call(functools.partial(right_kernel, len(flags)), in_specs=[sca...  1.79 us
    unnamed x12, local copies, waits for them, and re-layouts  1.6 us
    pallas_call x1, Pallas kernels, edge_rows(): pl.pallas_call(edges_kernel, in_specs=[pl.BlockSpec(memory_space=pltpu.HB...  1.49 us
  transfers between devices with their start and end apart: 12, of which 6 were waited for; matrix products, arithmetic and copies ran while one was open for 0% of the time, Pallas kernels for 21%

profile of v4, /device:TPU:0, one launch (start us, length us, event | category | flops | bytes accessed | tf_op | source)
XLA Modules:
  0.0 51.7 jit_solution(14970192772081805576)
XLA Ops:
  0.0 0.0 copy-start.3
  0.0 0.0 copy-start.4
  0.0 0.0 copy-start
  0.0 0.0 copy-start.5
  0.0 1.5 %edge_rows.1 = (bf16[128,512]{1,0:T(8,128)(2,1)S(1)}, bf16[128,512]{1,0:T(8,128)(2,1)S(1)}, bf16[512,512]{1,0:T(8,128)(2,1)S(1)}) custom-call(bf16[16,2,64,512]{3,2,1,0:T(8,128)(2,1)} %x_ref.5), custom_call_target="tpu_custom_call" | custom-call | flops 1000 | bytes 1000 | tf_op jit(solution)/shard_map/edge_rows/pallas_call | solution.py:193
  1.5 4.9 %collective-permute-start = (bf16[128,512]{1,0:T(8,128)(2,1)S(1)}, bf16[128,512]{1,0:T(8,128)(2,1)S(1)}, u32[]{:S(2)}, u32[]{:S(2)}) collective-permute-start(bf16[128,512]{1,0:T(8,128)(2,1)S(1)} %get-tuple-element.31), channel_id=1, source_target_pairs={{0,1},{1,2},{2,3},{4,5},{5,6},{6,7},{9,8},{10,9},{11,10},{13,12},{... | collective-permute-start | bytes 393224 | tf_op jit(solution)/shard_map/ppermute | solution.py:525
  6.5 1.3 %collective-permute-start.1 = (bf16[128,512]{1,0:T(8,128)(2,1)S(1)}, bf16[128,512]{1,0:T(8,128)(2,1)S(1)}, u32[]{:S(2)}, u32[]{:S(2)}) collective-permute-start(bf16[128,512]{1,0:T(8,128)(2,1)S(1)} %get-tuple-element.33.refs_0_), channel_id=1, source_target_pairs={{1,0},{2,1},{3,2},{5,4},{6,5},{7,6},{8,9},{9,10},{10,11},{12,13},{... | collective-permute-start | bytes 393224 | tf_op jit(solution)/shard_map/ppermute | solution.py:525
  7.8 0.0 copy-start.1
  7.8 1.6 %copy-done.1 = s32[64,4,1,2048]{3,2,1,0:T(1,128)S(1)} copy-done((s32[64,4,1,2048]{3,2,1,0:T(1,128)S(1)}, s32[64,4,1,2048]{3,2,1,0:T(1,128)}, u32[]{:S(2)}) %copy-start.1) | copy-done | bytes 2097176
  9.4 0.0 copy-start.2
  9.4 0.1 cast_flags.2
  9.4 4.7 %collective-permute-start.2 = (bf16[64,16,128]{2,1,0:T(8,128)(2,1)S(1)}, bf16[64,16,128]{2,1,0:T(8,128)(2,1)S(1)}, u32[]{:S(2)}, u32[]{:S(2)}) collective-permute-start(bf16[64,16,128]{2,1,0:T(8,128)(2,1)S(1)} %get-tuple-element.36), channel_id=1, source_target_pairs={{0,3},{1,2},{2,1},{3,0},{4,7},{5,6},{6,5},{7,4},{8,11},{9,10},{10,... | collective-permute-start | bytes 786440 | tf_op jit(solution)/shard_map/ppermute | solution.py:513
  14.2 0.0 copy-done.5
  14.2 0.0 copy-done.3
  14.2 0.0 copy-done.4
  14.2 0.1 fusion.refs_2_.table_ref
  14.3 0.0 collective-permute-done.1.refs_0_
  14.3 0.0 copy-done
  14.3 3.2 %box_codes.2 = (s16[2,17,16,512]{3,2,1,0:T(8,128)(2,1)S(1)}, s16[2,17,16,512]{3,2,1,0:T(8,128)(2,1)S(1)}, f32[8,128]{1,0:T(8,128)S(1)}) custom-call(bf16[16,2,64,512]{3,2,1,0:T(8,128)(2,1)S(1)} %copy-done, bf16[128,512]{1,0:T(8,128)(2,1)S(1)} %collective-permute-done.1.refs_0_, bf16[512,512]{1,0:T(8,128)(2,1)S(1)} %get-tuple-element.32.refs_1_, ...), custom_call_target="tpu_custom_call" | custom-call | flops 1000 | bytes 1000 | tf_op jit(solution)/shard_map/box_codes/pallas_call | solution.py:213
  17.6 0.1 collective-permute-start.7
  17.6 0.3 collective-permute-start.8
  18.0 0.0 copy-done.2
  18.0 0.1 cast_flags.3
  18.0 2.4 %collective-permute-start.3 = (bf16[64,16,128]{2,1,0:T(8,128)(2,1)S(1)}, bf16[64,16,128]{2,1,0:T(8,128)(2,1)S(1)}, u32[]{:S(2)}, u32[]{:S(2)}) collective-permute-start(bf16[64,16,128]{2,1,0:T(8,128)(2,1)S(1)} %get-tuple-element.39), channel_id=1, source_target_pairs={{0,1},{1,0},{2,3},{3,2},{4,5},{5,4},{6,7},{7,6},{8,9},{9,8},{10,11... | collective-permute-start | bytes 786440 | tf_op jit(solution)/shard_map/ppermute | solution.py:513
  20.5 0.0 collective-permute-done.refs_0_
  20.5 0.8 %collective-permute-start.4 = (bf16[64,16,128]{2,1,0:T(8,128)(2,1)S(1)}, bf16[64,16,128]{2,1,0:T(8,128)(2,1)S(1)}, u32[]{:S(2)}, u32[]{:S(2)}) collective-permute-start(bf16[64,16,128]{2,1,0:T(8,128)(2,1)S(1)} %get-tuple-element.40), channel_id=1, source_target_pairs={{0,2},{1,3},{2,0},{3,1},{4,6},{5,7},{6,4},{7,5},{8,10},{9,11},{10,... | collective-permute-start | bytes 786440 | tf_op jit(solution)/shard_map/ppermute | solution.py:513
  21.3 0.0 collective-permute-done.2.refs_3_
  21.3 3.2 %box_codes.3 = (s16[2,17,16,512]{3,2,1,0:T(8,128)(2,1)S(1)}, s16[2,17,16,512]{3,2,1,0:T(8,128)(2,1)S(1)}, f32[8,128]{1,0:T(8,128)S(1)}) custom-call(bf16[16,2,64,512]{3,2,1,0:T(8,128)(2,1)S(1)} %copy-done, bf16[128,512]{1,0:T(8,128)(2,1)S(1)} %collective-permute-done.refs_0_, bf16[512,512]{1,0:T(8,128)(2,1)S(1)} %get-tuple-element.32.refs_1_, ...), custom_call_target="tpu_custom_call" | custom-call | flops 1000 | bytes 1000 | tf_op jit(solution)/shard_map/box_codes/pallas_call | solution.py:213
  24.6 4.8 %collective-permute-done.3.refs_1_ = bf16[64,16,128]{2,1,0:T(8,128)(2,1)S(1)} collective-permute-done((bf16[64,16,128]{2,1,0:T(8,128)(2,1)S(1)}, bf16[64,16,128]{2,1,0:T(8,128)(2,1)S(1)}, u32[]{:S(2)}, u32[]{:S(2)}) %collective-permute-start.3) | collective-permute-done | bytes 262176 | tf_op jit(solution)/shard_map/ppermute | solution.py:513
  29.4 7.3 %collective-permute-done.4.refs_2_ = bf16[64,16,128]{2,1,0:T(8,128)(2,1)S(1)} collective-permute-done((bf16[64,16,128]{2,1,0:T(8,128)(2,1)S(1)}, bf16[64,16,128]{2,1,0:T(8,128)(2,1)S(1)}, u32[]{:S(2)}, u32[]{:S(2)}) %collective-permute-start.4) | collective-permute-done | bytes 262176 | tf_op jit(solution)/shard_map/ppermute | solution.py:513
  36.6 0.1 collective-permute-start.5
  36.8 0.4 collective-permute-start.6
  37.1 1.0 %collective-permute-done.5.refs_5_ = s16[17,16,512]{2,1,0:T(8,128)(2,1)S(1)} collective-permute-done((s16[17,16,512]{2,1,0:T(8,128)(2,1)S(1)}, s16[17,16,512]{2,1,0:T(8,128)(2,1)S(1)}, u32[]{:S(2)}, u32[]{:S(2)}) %collective-permute-start.5) | collective-permute-done | bytes 278560 | tf_op jit(solution)/shard_map/ppermute | solution.py:513
  38.2 0.4 collective-permute-done.6.refs_6_
  38.6 1.8 %right_sides.1 = (f32[2,11,8,512]{3,2,1,0:T(8,128)S(1)}, f32[2,16,512]{2,1,0:T(8,128)S(1)}, f32[2,32,8,512]{3,2,1,0:T(8,128)S(1)}) custom-call(f32[9,64]{1,0:T(8,128)S(1)} %fusion.refs_2_.table_ref, bf16[64,16,128]{2,1,0:T(8,128)(2,1)S(1)} %get-tuple-element.41.refs_3_.refs_0_, bf16[64,16,128]{2,1,0:T(8,128)(2,1)S(1)} %collective-permute-done.3.refs_1_, ...), custom_call_target="tpu_custom_call" | custom-call | flops 1000 | bytes 1000 | tf_op jit(solution)/shard_map/right_sides/pallas_call | solution.py:392
  40.4 0.0 collective-permute-done.7.far_2
  40.4 0.6 %collective-permute-done.8.far_3 = s16[2,17,16,512]{3,2,1,0:T(8,128)(2,1)S(1)} collective-permute-done((s16[2,17,16,512]{3,2,1,0:T(8,128)(2,1)S(1)}, s16[2,17,16,512]{3,2,1,0:T(8,128)(2,1)S(1)}, u32[]{:S(2)}, u32[]{:S(2)}) %collective-permute-start.8) | collective-permute-done | bytes 557088 | tf_op jit(solution)/shard_map/ppermute | solution.py:513
  41.0 1.4 %finish_sides.1 = (f32[6,16,128]{2,1,0:T(8,128)S(1)}, f32[6,16,128]{2,1,0:T(8,128)S(1)}, f32[6,16,128]{2,1,0:T(8,128)S(1)}, f32[6,16,128]{2,1,0:T(8,128)S(1)}) custom-call(f32[9,64]{1,0:T(8,128)S(1)} %fusion.refs_2_.table_ref, f32[2,11,8,512]{3,2,1,0:T(8,128)S(1)} %get-tuple-element.48.part_ref, f32[2,16,512]{2,1,0:T(8,128)S(1)} %get-tuple-element.49.ratio_ref, ...), custom_call_target="tpu_custom_call" | custom-call | flops 1000 | bytes 1000 | tf_op jit(solution)/shard_map/finish_sides/pallas_call | solution.py:445
  42.5 0.7 %collective-permute-start.9 = (f32[6,16,128]{2,1,0:T(8,128)S(1)}, f32[6,16,128]{2,1,0:T(8,128)S(1)}, u32[]{:S(2)}, u32[]{:S(2)}) collective-permute-start(f32[6,16,128]{2,1,0:T(8,128)S(1)} %get-tuple-element.54), channel_id=1, source_target_pairs={{0,1},{1,0},{2,3},{3,2},{4,5},{5,4},{6,7},{7,6},{8,9},{9,8},{10,11... | collective-permute-start | bytes 147464 | tf_op jit(solution)/shard_map/ppermute | solution.py:513
  43.1 1.9 %collective-permute-start.10 = (f32[6,16,128]{2,1,0:T(8,128)S(1)}, f32[6,16,128]{2,1,0:T(8,128)S(1)}, u32[]{:S(2)}, u32[]{:S(2)}) collective-permute-start(f32[6,16,128]{2,1,0:T(8,128)S(1)} %get-tuple-element.55), channel_id=1, source_target_pairs={{0,2},{1,3},{2,0},{3,1},{4,6},{5,7},{6,4},{7,5},{8,10},{9,11},{10,... | collective-permute-start | bytes 147464 | tf_op jit(solution)/shard_map/ppermute | solution.py:513
  45.0 1.9 %collective-permute-start.11 = (f32[6,16,128]{2,1,0:T(8,128)S(1)}, f32[6,16,128]{2,1,0:T(8,128)S(1)}, u32[]{:S(2)}, u32[]{:S(2)}) collective-permute-start(f32[6,16,128]{2,1,0:T(8,128)S(1)} %get-tuple-element.56), channel_id=1, source_target_pairs={{0,3},{1,2},{2,1},{3,0},{4,7},{5,6},{6,5},{7,4},{8,11},{9,10},{10,... | collective-permute-start | bytes 147464 | tf_op jit(solution)/shard_map/ppermute | solution.py:513
  46.9 2.5 %factor.1.factor_ref = f32[21,64,128]{2,1,0:T(8,128)S(1)} custom-call(f32[9,64]{1,0:T(8,128)S(1)} %fusion.refs_2_.table_ref, s32[64,64,128]{2,1,0:T(8,128)S(1)} %bitcast.8, f32[8,128]{1,0:T(8,128)S(1)} %get-tuple-element.37.refs_0_), custom_call_target="tpu_custom_call" | custom-call | flops 1000 | bytes 1000 | tf_op jit(solution)/shard_map/factor/pallas_call | solution.py:297
  49.4 0.0 collective-permute-done.9.refs_1_
  49.4 0.0 collective-permute-done.10.refs_2_
  49.4 1.5 %collective-permute-done.11.refs_3_ = f32[6,16,128]{2,1,0:T(8,128)S(1)} collective-permute-done((f32[6,16,128]{2,1,0:T(8,128)S(1)}, f32[6,16,128]{2,1,0:T(8,128)S(1)}, u32[]{:S(2)}, u32[]{:S(2)}) %collective-permute-start.11) | collective-permute-done | bytes 49184 | tf_op jit(solution)/shard_map/ppermute | solution.py:513
  50.9 0.8 %solve.1 = f32[6,64,128]{2,1,0:T(8,128)} custom-call(f32[21,64,128]{2,1,0:T(8,128)S(1)} %factor.1.factor_ref, f32[6,16,128]{2,1,0:T(8,128)S(1)} %get-tuple-element.53.refs_0_, f32[6,16,128]{2,1,0:T(8,128)S(1)} %collective-permute-done.9.refs_1_, f32[6,16,128]{2,1,0:T(8,128)S(1)} %collective-permute-done.10.refs_2_, ...), custom_call_target="tpu_custom_call" | custom-call | flops 1000 | bytes 1000 | tf_op jit(solution)/shard_map/solve/pallas_call | solution.py:483
  (2 shorter events, 0.0 us)
Async XLA Ops:
  0.0 14.2 %copy-start.3 = (f32[9]{0:T(128)S(1)}, f32[9]{0:T(128)}, u32[]{:S(2)}) copy-start(f32[9]{0:T(128)} %constant.10) | copy-start | bytes 112
  0.0 14.2 %copy-start.4 = (pred[9]{0:T(512)(128)(4,1)S(1)}, pred[9]{0:T(512)(128)(4,1)}, u32[]{:S(2)}) copy-start(pred[9]{0:T(512)(128)(4,1)} %constant.9) | copy-start | bytes 31
  0.0 14.3 %copy-start = (bf16[16,2,64,512]{3,2,1,0:T(8,128)(2,1)S(1)}, bf16[16,2,64,512]{3,2,1,0:T(8,128)(2,1)}, u32[]{:S(2)}) copy-start(bf16[16,2,64,512]{3,2,1,0:T(8,128)(2,1)} %x_ref.5) | copy-start | bytes 6291460
  0.0 14.2 %copy-start.5 = (s32[64]{0:T(128)S(1)}, s32[64]{0:T(128)}, u32[]{:S(2)}) copy-start(s32[64]{0:T(128)} %param.7) | copy-start | bytes 772
  1.5 19.0 %collective-permute-start = (bf16[128,512]{1,0:T(8,128)(2,1)S(1)}, bf16[128,512]{1,0:T(8,128)(2,1)S(1)}, u32[]{:S(2)}, u32[]{:S(2)}) collective-permute-start(bf16[128,512]{1,0:T(8,128)(2,1)S(1)} %get-tuple-element.31), channel_id=1, source_target_pairs={{0,1},{1,2},{2,3},{4,5},{5,6},{6,7},{9,8},{10,9},{11,10},{13,12},{... | collective-permute-start | bytes 393224 | tf_op jit(solution)/shard_map/ppermute | solution.py:525
  6.5 7.9 %collective-permute-start.1 = (bf16[128,512]{1,0:T(8,128)(2,1)S(1)}, bf16[128,512]{1,0:T(8,128)(2,1)S(1)}, u32[]{:S(2)}, u32[]{:S(2)}) collective-permute-start(bf16[128,512]{1,0:T(8,128)(2,1)S(1)} %get-tuple-element.33.refs_0_), channel_id=1, source_target_pairs={{1,0},{2,1},{3,2},{5,4},{6,5},{7,6},{8,9},{9,10},{10,11},{12,13},{... | collective-permute-start | bytes 393224 | tf_op jit(solution)/shard_map/ppermute | solution.py:525
  7.8 1.6 %copy-start.1 = (s32[64,4,1,2048]{3,2,1,0:T(1,128)S(1)}, s32[64,4,1,2048]{3,2,1,0:T(1,128)}, u32[]{:S(2)}) copy-start(s32[64,4,1,2048]{3,2,1,0:T(1,128)} %param.6) | copy-start | bytes 6291460
  9.4 8.6 %copy-start.2 = (s32[64,4,1,2048]{3,2,1,0:T(1,128)S(1)}, s32[64,4,1,2048]{3,2,1,0:T(1,128)}, u32[]{:S(2)}) copy-start(s32[64,4,1,2048]{3,2,1,0:T(1,128)} %param.6) | copy-start | bytes 6291460
  9.4 11.9 %collective-permute-start.2 = (bf16[64,16,128]{2,1,0:T(8,128)(2,1)S(1)}, bf16[64,16,128]{2,1,0:T(8,128)(2,1)S(1)}, u32[]{:S(2)}, u32[]{:S(2)}) collective-permute-start(bf16[64,16,128]{2,1,0:T(8,128)(2,1)S(1)} %get-tuple-element.36), channel_id=1, source_target_pairs={{0,3},{1,2},{2,1},{3,0},{4,7},{5,6},{6,5},{7,4},{8,11},{9,10},{10,... | collective-permute-start | bytes 786440 | tf_op jit(solution)/shard_map/ppermute | solution.py:513
  17.6 22.8 %collective-permute-start.7 = (s16[2,17,16,512]{3,2,1,0:T(8,128)(2,1)S(1)}, s16[2,17,16,512]{3,2,1,0:T(8,128)(2,1)S(1)}, u32[]{:S(2)}, u32[]{:S(2)}) collective-permute-start(s16[2,17,16,512]{3,2,1,0:T(8,128)(2,1)S(1)} %get-tuple-element.51), channel_id=1, source_target_pairs={{0,8},{4,12},{8,0},{12,4},{1,9},{5,13},{9,1},{13,5},{2,10},{6,14},... | collective-permute-start | bytes 1671176 | tf_op jit(solution)/shard_map/ppermute | solution.py:513
  17.6 23.4 %collective-permute-start.8 = (s16[2,17,16,512]{3,2,1,0:T(8,128)(2,1)S(1)}, s16[2,17,16,512]{3,2,1,0:T(8,128)(2,1)S(1)}, u32[]{:S(2)}, u32[]{:S(2)}) collective-permute-start(s16[2,17,16,512]{3,2,1,0:T(8,128)(2,1)S(1)} %get-tuple-element.52), channel_id=1, source_target_pairs={{0,12},{4,8},{8,4},{12,0},{1,13},{5,9},{9,5},{13,1},{2,14},{6,10},... | collective-permute-start | bytes 1671176 | tf_op jit(solution)/shard_map/ppermute | solution.py:513
  18.0 11.3 %collective-permute-start.3 = (bf16[64,16,128]{2,1,0:T(8,128)(2,1)S(1)}, bf16[64,16,128]{2,1,0:T(8,128)(2,1)S(1)}, u32[]{:S(2)}, u32[]{:S(2)}) collective-permute-start(bf16[64,16,128]{2,1,0:T(8,128)(2,1)S(1)} %get-tuple-element.39), channel_id=1, source_target_pairs={{0,1},{1,0},{2,3},{3,2},{4,5},{5,4},{6,7},{7,6},{8,9},{9,8},{10,11... | collective-permute-start | bytes 786440 | tf_op jit(solution)/shard_map/ppermute | solution.py:513
  20.5 16.2 %collective-permute-start.4 = (bf16[64,16,128]{2,1,0:T(8,128)(2,1)S(1)}, bf16[64,16,128]{2,1,0:T(8,128)(2,1)S(1)}, u32[]{:S(2)}, u32[]{:S(2)}) collective-permute-start(bf16[64,16,128]{2,1,0:T(8,128)(2,1)S(1)} %get-tuple-element.40), channel_id=1, source_target_pairs={{0,2},{1,3},{2,0},{3,1},{4,6},{5,7},{6,4},{7,5},{8,10},{9,11},{10,... | collective-permute-start | bytes 786440 | tf_op jit(solution)/shard_map/ppermute | solution.py:513
  36.6 1.6 %collective-permute-start.5 = (s16[17,16,512]{2,1,0:T(8,128)(2,1)S(1)}, s16[17,16,512]{2,1,0:T(8,128)(2,1)S(1)}, u32[]{:S(2)}, u32[]{:S(2)}) collective-permute-start(s16[17,16,512]{2,1,0:T(8,128)(2,1)S(1)} %get-tuple-element.46), channel_id=1, source_target_pairs={{0,4},{4,0},{8,12},{12,8},{1,5},{5,1},{9,13},{13,9},{2,6},{6,2},{1... | collective-permute-start | bytes 835592 | tf_op jit(solution)/shard_map/ppermute | solution.py:513
  36.8 1.8 %collective-permute-start.6 = (s16[17,16,512]{2,1,0:T(8,128)(2,1)S(1)}, s16[17,16,512]{2,1,0:T(8,128)(2,1)S(1)}, u32[]{:S(2)}, u32[]{:S(2)}) collective-permute-start(s16[17,16,512]{2,1,0:T(8,128)(2,1)S(1)} %get-tuple-element.47), channel_id=1, source_target_pairs={{0,4},{4,0},{8,12},{12,8},{1,5},{5,1},{9,13},{13,9},{2,6},{6,2},{1... | collective-permute-start | bytes 835592 | tf_op jit(solution)/shard_map/ppermute | solution.py:513
  42.5 6.9 %collective-permute-start.9 = (f32[6,16,128]{2,1,0:T(8,128)S(1)}, f32[6,16,128]{2,1,0:T(8,128)S(1)}, u32[]{:S(2)}, u32[]{:S(2)}) collective-permute-start(f32[6,16,128]{2,1,0:T(8,128)S(1)} %get-tuple-element.54), channel_id=1, source_target_pairs={{0,1},{1,0},{2,3},{3,2},{4,5},{5,4},{6,7},{7,6},{8,9},{9,8},{10,11... | collective-permute-start | bytes 147464 | tf_op jit(solution)/shard_map/ppermute | solution.py:513
  43.1 6.3 %collective-permute-start.10 = (f32[6,16,128]{2,1,0:T(8,128)S(1)}, f32[6,16,128]{2,1,0:T(8,128)S(1)}, u32[]{:S(2)}, u32[]{:S(2)}) collective-permute-start(f32[6,16,128]{2,1,0:T(8,128)S(1)} %get-tuple-element.55), channel_id=1, source_target_pairs={{0,2},{1,3},{2,0},{3,1},{4,6},{5,7},{6,4},{7,5},{8,10},{9,11},{10,... | collective-permute-start | bytes 147464 | tf_op jit(solution)/shard_map/ppermute | solution.py:513
  45.0 5.9 %collective-permute-start.11 = (f32[6,16,128]{2,1,0:T(8,128)S(1)}, f32[6,16,128]{2,1,0:T(8,128)S(1)}, u32[]{:S(2)}, u32[]{:S(2)}) collective-permute-start(f32[6,16,128]{2,1,0:T(8,128)S(1)} %get-tuple-element.56), channel_id=1, source_target_pairs={{0,3},{1,2},{2,1},{3,0},{4,7},{5,6},{6,5},{7,4},{8,11},{9,10},{10,... | collective-permute-start | bytes 147464 | tf_op jit(solution)/shard_map/ppermute | solution.py:513

commit v5 on v4

--- a/solution.py
+++ b/solution.py
@@ -11,7 +11,7 @@
 
 RADIUS = 3
 STATES = 6
-HALO = 4
+HALO = 3
 GROUP = 8
 LANES = 128
 HARMONICS = 9
@@ -154,14 +154,15 @@
 
 def copy_edges(x_ref, out, bottom, dates):
     pols = x_ref.shape[1]
-    for t in range(0, dates, 2):
+    step = 16 // pols
+    for t in range(0, dates, step):
         for lanes in tiles_of(x_ref.shape[3]):
             images = []
-            for n in range(2 * pols):
+            for n in range(step * pols):
                 image = x_ref[t + n // pols, n % pols, :, lanes].astype(f32)
                 images.append(jnp.where(bottom == 1, image[16 - HALO :], image[:HALO]))
             line = t * pols * HALO
-            out[line : line + 16, lanes] = jnp.concatenate(images, axis=0).astype(out.dtype)
+            out[line : line + 16 * HALO, lanes] = jnp.concatenate(images, axis=0).astype(out.dtype)
 
 
 def edges_kernel(x_ref, far_ref, near_ref, band_ref, rows_ref, arrived):

time: 51.9 us -> 51.6 us (level)
  no operation moved by 1% of the time
where the time goes in v5:
time: 51.6 us; the launch traced here: 51.5 us
  starting transfers between devices  19.2 us (37%)
  waiting for transfers between devices  15.8 us (31%)
  Pallas kernels  14.5 us (28%)
  local copies, waits for them, and re-layouts  1.64 us (3%)
    ppermute x10, waiting for transfers between devices, exchange(): return lax.ppermute(piece, axis, partners(lax.axis_size(axis), k))  15.7 us
    ppermute x10, starting transfers between devices, exchange(): return lax.ppermute(piece, axis, partners(lax.axis_size(axis), k))  13 us
    pallas_call x2, Pallas kernels, box_codes(): pl.pallas_call(functools.partial(box_kernel, ks), in_specs=[whole()] * 3...  6.42 us
    ppermute x2, starting transfers between devices, halo(): return lax.ppermute(cells, ('date', 'row'), pairs)  6.23 us
    pallas_call x1, Pallas kernels, factor(): pl.pallas_call(factor_kernel, in_specs=[scalars(), whole()] + [anywhere()...  2.48 us
    pallas_call x1, Pallas kernels, right_sides(): pl.pallas_call(functools.partial(right_kernel, len(flags)), in_specs=[sca...  1.79 us
    unnamed x12, local copies, waits for them, and re-layouts  1.6 us
    pallas_call x1, Pallas kernels, edge_rows(): pl.pallas_call(edges_kernel, in_specs=[pl.BlockSpec(memory_space=pltpu.HB...  1.5 us
  transfers between devices with their start and end apart: 12, of which 6 were waited for; matrix products, arithmetic and copies ran while one was open for 0% of the time, Pallas kernels for 21%

profile of v5, /device:TPU:0, one launch (start us, length us, event | category | flops | bytes accessed | tf_op | source)
XLA Modules:
  0.0 51.5 jit_solution(3763951716799462604)
XLA Ops:
  0.0 0.0 copy-start.3
  0.0 0.0 copy-start.4
  0.0 0.0 copy-start
  0.0 0.0 copy-start.5
  0.0 1.5 %edge_rows.1 = (bf16[96,512]{1,0:T(8,128)(2,1)S(1)}, bf16[96,512]{1,0:T(8,128)(2,1)S(1)}, bf16[512,512]{1,0:T(8,128)(2,1)S(1)}) custom-call(bf16[16,2,64,512]{3,2,1,0:T(8,128)(2,1)} %x_ref.5), custom_call_target="tpu_custom_call" | custom-call | flops 1000 | bytes 1000 | tf_op jit(solution)/shard_map/edge_rows/pallas_call | solution.py:194
  1.5 4.9 %collective-permute-start = (bf16[96,512]{1,0:T(8,128)(2,1)S(1)}, bf16[96,512]{1,0:T(8,128)(2,1)S(1)}, u32[]{:S(2)}, u32[]{:S(2)}) collective-permute-start(bf16[96,512]{1,0:T(8,128)(2,1)S(1)} %get-tuple-element.31), channel_id=1, source_target_pairs={{0,1},{1,2},{2,3},{4,5},{5,6},{6,7},{9,8},{10,9},{11,10},{13,12},{... | collective-permute-start | bytes 294920 | tf_op jit(solution)/shard_map/ppermute | solution.py:526
  6.5 1.3 %collective-permute-start.1 = (bf16[96,512]{1,0:T(8,128)(2,1)S(1)}, bf16[96,512]{1,0:T(8,128)(2,1)S(1)}, u32[]{:S(2)}, u32[]{:S(2)}) collective-permute-start(bf16[96,512]{1,0:T(8,128)(2,1)S(1)} %get-tuple-element.33.refs_0_), channel_id=1, source_target_pairs={{1,0},{2,1},{3,2},{5,4},{6,5},{7,6},{8,9},{9,10},{10,11},{12,13},{... | collective-permute-start | bytes 294920 | tf_op jit(solution)/shard_map/ppermute | solution.py:526
  7.8 0.0 copy-start.1
  7.8 1.6 %copy-done.1 = s32[64,4,1,2048]{3,2,1,0:T(1,128)S(1)} copy-done((s32[64,4,1,2048]{3,2,1,0:T(1,128)S(1)}, s32[64,4,1,2048]{3,2,1,0:T(1,128)}, u32[]{:S(2)}) %copy-start.1) | copy-done | bytes 2097176
  9.4 0.0 copy-start.2
  9.4 0.1 cast_flags.2
  9.4 4.7 %collective-permute-start.2 = (bf16[64,16,128]{2,1,0:T(8,128)(2,1)S(1)}, bf16[64,16,128]{2,1,0:T(8,128)(2,1)S(1)}, u32[]{:S(2)}, u32[]{:S(2)}) collective-permute-start(bf16[64,16,128]{2,1,0:T(8,128)(2,1)S(1)} %get-tuple-element.36), channel_id=1, source_target_pairs={{0,3},{1,2},{2,1},{3,0},{4,7},{5,6},{6,5},{7,4},{8,11},{9,10},{10,... | collective-permute-start | bytes 786440 | tf_op jit(solution)/shard_map/ppermute | solution.py:514
  14.2 0.0 copy-done.5
  14.2 0.0 copy-done.3
  14.2 0.0 copy-done.4
  14.2 0.1 fusion.refs_2_.table_ref
  14.3 0.0 collective-permute-done.1.refs_0_
  14.3 0.0 copy-done
  14.3 3.2 %box_codes.2 = (s16[2,17,16,512]{3,2,1,0:T(8,128)(2,1)S(1)}, s16[2,17,16,512]{3,2,1,0:T(8,128)(2,1)S(1)}, f32[8,128]{1,0:T(8,128)S(1)}) custom-call(bf16[16,2,64,512]{3,2,1,0:T(8,128)(2,1)S(1)} %copy-done, bf16[96,512]{1,0:T(8,128)(2,1)S(1)} %collective-permute-done.1.refs_0_, bf16[512,512]{1,0:T(8,128)(2,1)S(1)} %get-tuple-element.32.refs_1_, ...), custom_call_target="tpu_custom_call" | custom-call | flops 1000 | bytes 1000 | tf_op jit(solution)/shard_map/box_codes/pallas_call | solution.py:214
  17.6 0.1 collective-permute-start.7
  17.6 0.3 collective-permute-start.8
  18.0 0.0 copy-done.2
  18.0 0.1 cast_flags.3
  18.1 1.0 %collective-permute-start.3 = (bf16[64,16,128]{2,1,0:T(8,128)(2,1)S(1)}, bf16[64,16,128]{2,1,0:T(8,128)(2,1)S(1)}, u32[]{:S(2)}, u32[]{:S(2)}) collective-permute-start(bf16[64,16,128]{2,1,0:T(8,128)(2,1)S(1)} %get-tuple-element.39), channel_id=1, source_target_pairs={{0,1},{1,0},{2,3},{3,2},{4,5},{5,4},{6,7},{7,6},{8,9},{9,8},{10,11... | collective-permute-start | bytes 786440 | tf_op jit(solution)/shard_map/ppermute | solution.py:514
  19.1 0.0 collective-permute-done.refs_0_
  19.1 1.9 %collective-permute-start.4 = (bf16[64,16,128]{2,1,0:T(8,128)(2,1)S(1)}, bf16[64,16,128]{2,1,0:T(8,128)(2,1)S(1)}, u32[]{:S(2)}, u32[]{:S(2)}) collective-permute-start(bf16[64,16,128]{2,1,0:T(8,128)(2,1)S(1)} %get-tuple-element.40), channel_id=1, source_target_pairs={{0,2},{1,3},{2,0},{3,1},{4,6},{5,7},{6,4},{7,5},{8,10},{9,11},{10,... | collective-permute-start | bytes 786440 | tf_op jit(solution)/shard_map/ppermute | solution.py:514
  21.0 0.0 collective-permute-done.2.refs_3_
  21.0 3.2 %box_codes.3 = (s16[2,17,16,512]{3,2,1,0:T(8,128)(2,1)S(1)}, s16[2,17,16,512]{3,2,1,0:T(8,128)(2,1)S(1)}, f32[8,128]{1,0:T(8,128)S(1)}) custom-call(bf16[16,2,64,512]{3,2,1,0:T(8,128)(2,1)S(1)} %copy-done, bf16[96,512]{1,0:T(8,128)(2,1)S(1)} %collective-permute-done.refs_0_, bf16[512,512]{1,0:T(8,128)(2,1)S(1)} %get-tuple-element.32.refs_1_, ...), custom_call_target="tpu_custom_call" | custom-call | flops 1000 | bytes 1000 | tf_op jit(solution)/shard_map/box_codes/pallas_call | solution.py:214
  24.2 5.6 %collective-permute-done.3.refs_1_ = bf16[64,16,128]{2,1,0:T(8,128)(2,1)S(1)} collective-permute-done((bf16[64,16,128]{2,1,0:T(8,128)(2,1)S(1)}, bf16[64,16,128]{2,1,0:T(8,128)(2,1)S(1)}, u32[]{:S(2)}, u32[]{:S(2)}) %collective-permute-start.3) | collective-permute-done | bytes 262176 | tf_op jit(solution)/shard_map/ppermute | solution.py:514
  29.8 6.7 %collective-permute-done.4.refs_2_ = bf16[64,16,128]{2,1,0:T(8,128)(2,1)S(1)} collective-permute-done((bf16[64,16,128]{2,1,0:T(8,128)(2,1)S(1)}, bf16[64,16,128]{2,1,0:T(8,128)(2,1)S(1)}, u32[]{:S(2)}, u32[]{:S(2)}) %collective-permute-start.4) | collective-permute-done | bytes 262176 | tf_op jit(solution)/shard_map/ppermute | solution.py:514
  36.5 0.0 collective-permute-start.5
  36.5 0.5 collective-permute-start.6
  37.0 1.0 %collective-permute-done.5.refs_5_ = s16[17,16,512]{2,1,0:T(8,128)(2,1)S(1)} collective-permute-done((s16[17,16,512]{2,1,0:T(8,128)(2,1)S(1)}, s16[17,16,512]{2,1,0:T(8,128)(2,1)S(1)}, u32[]{:S(2)}, u32[]{:S(2)}) %collective-permute-start.5) | collective-permute-done | bytes 278560 | tf_op jit(solution)/shard_map/ppermute | solution.py:514
  38.1 0.4 collective-permute-done.6.refs_6_
  38.5 1.8 %right_sides.1 = (f32[2,11,8,512]{3,2,1,0:T(8,128)S(1)}, f32[2,16,512]{2,1,0:T(8,128)S(1)}, f32[2,32,8,512]{3,2,1,0:T(8,128)S(1)}) custom-call(f32[9,64]{1,0:T(8,128)S(1)} %fusion.refs_2_.table_ref, bf16[64,16,128]{2,1,0:T(8,128)(2,1)S(1)} %get-tuple-element.41.refs_3_.refs_0_, bf16[64,16,128]{2,1,0:T(8,128)(2,1)S(1)} %collective-permute-done.3.refs_1_, ...), custom_call_target="tpu_custom_call" | custom-call | flops 1000 | bytes 1000 | tf_op jit(solution)/shard_map/right_sides/pallas_call | solution.py:393
  40.3 0.0 collective-permute-done.7.far_2
  40.3 0.8 %collective-permute-done.8.far_3 = s16[2,17,16,512]{3,2,1,0:T(8,128)(2,1)S(1)} collective-permute-done((s16[2,17,16,512]{3,2,1,0:T(8,128)(2,1)S(1)}, s16[2,17,16,512]{3,2,1,0:T(8,128)(2,1)S(1)}, u32[]{:S(2)}, u32[]{:S(2)}) %collective-permute-start.8) | collective-permute-done | bytes 557088 | tf_op jit(solution)/shard_map/ppermute | solution.py:514
  41.0 1.4 %finish_sides.1 = (f32[6,16,128]{2,1,0:T(8,128)S(1)}, f32[6,16,128]{2,1,0:T(8,128)S(1)}, f32[6,16,128]{2,1,0:T(8,128)S(1)}, f32[6,16,128]{2,1,0:T(8,128)S(1)}) custom-call(f32[9,64]{1,0:T(8,128)S(1)} %fusion.refs_2_.table_ref, f32[2,11,8,512]{3,2,1,0:T(8,128)S(1)} %get-tuple-element.48.part_ref, f32[2,16,512]{2,1,0:T(8,128)S(1)} %get-tuple-element.49.ratio_ref, ...), custom_call_target="tpu_custom_call" | custom-call | flops 1000 | bytes 1000 | tf_op jit(solution)/shard_map/finish_sides/pallas_call | solution.py:446
  42.5 0.7 %collective-permute-start.9 = (f32[6,16,128]{2,1,0:T(8,128)S(1)}, f32[6,16,128]{2,1,0:T(8,128)S(1)}, u32[]{:S(2)}, u32[]{:S(2)}) collective-permute-start(f32[6,16,128]{2,1,0:T(8,128)S(1)} %get-tuple-element.54), channel_id=1, source_target_pairs={{0,1},{1,0},{2,3},{3,2},{4,5},{5,4},{6,7},{7,6},{8,9},{9,8},{10,11... | collective-permute-start | bytes 147464 | tf_op jit(solution)/shard_map/ppermute | solution.py:514
  43.1 1.5 %collective-permute-start.10 = (f32[6,16,128]{2,1,0:T(8,128)S(1)}, f32[6,16,128]{2,1,0:T(8,128)S(1)}, u32[]{:S(2)}, u32[]{:S(2)}) collective-permute-start(f32[6,16,128]{2,1,0:T(8,128)S(1)} %get-tuple-element.55), channel_id=1, source_target_pairs={{0,2},{1,3},{2,0},{3,1},{4,6},{5,7},{6,4},{7,5},{8,10},{9,11},{10,... | collective-permute-start | bytes 147464 | tf_op jit(solution)/shard_map/ppermute | solution.py:514
  44.7 2.2 %collective-permute-start.11 = (f32[6,16,128]{2,1,0:T(8,128)S(1)}, f32[6,16,128]{2,1,0:T(8,128)S(1)}, u32[]{:S(2)}, u32[]{:S(2)}) collective-permute-start(f32[6,16,128]{2,1,0:T(8,128)S(1)} %get-tuple-element.56), channel_id=1, source_target_pairs={{0,3},{1,2},{2,1},{3,0},{4,7},{5,6},{6,5},{7,4},{8,11},{9,10},{10,... | collective-permute-start | bytes 147464 | tf_op jit(solution)/shard_map/ppermute | solution.py:514
  46.9 2.5 %factor.1.factor_ref = f32[21,64,128]{2,1,0:T(8,128)S(1)} custom-call(f32[9,64]{1,0:T(8,128)S(1)} %fusion.refs_2_.table_ref, s32[64,64,128]{2,1,0:T(8,128)S(1)} %bitcast.8, f32[8,128]{1,0:T(8,128)S(1)} %get-tuple-element.37.refs_0_), custom_call_target="tpu_custom_call" | custom-call | flops 1000 | bytes 1000 | tf_op jit(solution)/shard_map/factor/pallas_call | solution.py:298
  49.4 0.0 collective-permute-done.9.refs_1_
  49.4 0.0 collective-permute-done.10.refs_2_
  49.4 1.2 %collective-permute-done.11.refs_3_ = f32[6,16,128]{2,1,0:T(8,128)S(1)} collective-permute-done((f32[6,16,128]{2,1,0:T(8,128)S(1)}, f32[6,16,128]{2,1,0:T(8,128)S(1)}, u32[]{:S(2)}, u32[]{:S(2)}) %collective-permute-start.11) | collective-permute-done | bytes 49184 | tf_op jit(solution)/shard_map/ppermute | solution.py:514
  50.7 0.8 %solve.1 = f32[6,64,128]{2,1,0:T(8,128)} custom-call(f32[21,64,128]{2,1,0:T(8,128)S(1)} %factor.1.factor_ref, f32[6,16,128]{2,1,0:T(8,128)S(1)} %get-tuple-element.53.refs_0_, f32[6,16,128]{2,1,0:T(8,128)S(1)} %collective-permute-done.9.refs_1_, f32[6,16,128]{2,1,0:T(8,128)S(1)} %collective-permute-done.10.refs_2_, ...), custom_call_target="tpu_custom_call" | custom-call | flops 1000 | bytes 1000 | tf_op jit(solution)/shard_map/solve/pallas_call | solution.py:484
  (2 shorter events, 0.0 us)
Async XLA Ops:
  0.0 14.2 %copy-start.3 = (f32[9]{0:T(128)S(1)}, f32[9]{0:T(128)}, u32[]{:S(2)}) copy-start(f32[9]{0:T(128)} %constant.10) | copy-start | bytes 112
  0.0 14.2 %copy-start.4 = (pred[9]{0:T(512)(128)(4,1)S(1)}, pred[9]{0:T(512)(128)(4,1)}, u32[]{:S(2)}) copy-start(pred[9]{0:T(512)(128)(4,1)} %constant.9) | copy-start | bytes 31
  0.0 14.3 %copy-start = (bf16[16,2,64,512]{3,2,1,0:T(8,128)(2,1)S(1)}, bf16[16,2,64,512]{3,2,1,0:T(8,128)(2,1)}, u32[]{:S(2)}) copy-start(bf16[16,2,64,512]{3,2,1,0:T(8,128)(2,1)} %x_ref.5) | copy-start | bytes 6291460
  0.0 14.2 %copy-start.5 = (s32[64]{0:T(128)S(1)}, s32[64]{0:T(128)}, u32[]{:S(2)}) copy-start(s32[64]{0:T(128)} %param.7) | copy-start | bytes 772
  1.5 17.6 %collective-permute-start = (bf16[96,512]{1,0:T(8,128)(2,1)S(1)}, bf16[96,512]{1,0:T(8,128)(2,1)S(1)}, u32[]{:S(2)}, u32[]{:S(2)}) collective-permute-start(bf16[96,512]{1,0:T(8,128)(2,1)S(1)} %get-tuple-element.31), channel_id=1, source_target_pairs={{0,1},{1,2},{2,3},{4,5},{5,6},{6,7},{9,8},{10,9},{11,10},{13,12},{... | collective-permute-start | bytes 294920 | tf_op jit(solution)/shard_map/ppermute | solution.py:526
  6.5 7.9 %collective-permute-start.1 = (bf16[96,512]{1,0:T(8,128)(2,1)S(1)}, bf16[96,512]{1,0:T(8,128)(2,1)S(1)}, u32[]{:S(2)}, u32[]{:S(2)}) collective-permute-start(bf16[96,512]{1,0:T(8,128)(2,1)S(1)} %get-tuple-element.33.refs_0_), channel_id=1, source_target_pairs={{1,0},{2,1},{3,2},{5,4},{6,5},{7,6},{8,9},{9,10},{10,11},{12,13},{... | collective-permute-start | bytes 294920 | tf_op jit(solution)/shard_map/ppermute | solution.py:526
  7.8 1.6 %copy-start.1 = (s32[64,4,1,2048]{3,2,1,0:T(1,128)S(1)}, s32[64,4,1,2048]{3,2,1,0:T(1,128)}, u32[]{:S(2)}) copy-start(s32[64,4,1,2048]{3,2,1,0:T(1,128)} %param.6) | copy-start | bytes 6291460
  9.4 8.6 %copy-start.2 = (s32[64,4,1,2048]{3,2,1,0:T(1,128)S(1)}, s32[64,4,1,2048]{3,2,1,0:T(1,128)}, u32[]{:S(2)}) copy-start(s32[64,4,1,2048]{3,2,1,0:T(1,128)} %param.6) | copy-start | bytes 6291460
  9.4 11.5 %collective-permute-start.2 = (bf16[64,16,128]{2,1,0:T(8,128)(2,1)S(1)}, bf16[64,16,128]{2,1,0:T(8,128)(2,1)S(1)}, u32[]{:S(2)}, u32[]{:S(2)}) collective-permute-start(bf16[64,16,128]{2,1,0:T(8,128)(2,1)S(1)} %get-tuple-element.36), channel_id=1, source_target_pairs={{0,3},{1,2},{2,1},{3,0},{4,7},{5,6},{6,5},{7,4},{8,11},{9,10},{10,... | collective-permute-start | bytes 786440 | tf_op jit(solution)/shard_map/ppermute | solution.py:514
  17.6 22.7 %collective-permute-start.7 = (s16[2,17,16,512]{3,2,1,0:T(8,128)(2,1)S(1)}, s16[2,17,16,512]{3,2,1,0:T(8,128)(2,1)S(1)}, u32[]{:S(2)}, u32[]{:S(2)}) collective-permute-start(s16[2,17,16,512]{3,2,1,0:T(8,128)(2,1)S(1)} %get-tuple-element.51), channel_id=1, source_target_pairs={{0,8},{4,12},{8,0},{12,4},{1,9},{5,13},{9,1},{13,5},{2,10},{6,14},... | collective-permute-start | bytes 1671176 | tf_op jit(solution)/shard_map/ppermute | solution.py:514
  17.6 23.4 %collective-permute-start.8 = (s16[2,17,16,512]{3,2,1,0:T(8,128)(2,1)S(1)}, s16[2,17,16,512]{3,2,1,0:T(8,128)(2,1)S(1)}, u32[]{:S(2)}, u32[]{:S(2)}) collective-permute-start(s16[2,17,16,512]{3,2,1,0:T(8,128)(2,1)S(1)} %get-tuple-element.52), channel_id=1, source_target_pairs={{0,12},{4,8},{8,4},{12,0},{1,13},{5,9},{9,5},{13,1},{2,14},{6,10},... | collective-permute-start | bytes 1671176 | tf_op jit(solution)/shard_map/ppermute | solution.py:514
  18.1 11.8 %collective-permute-start.3 = (bf16[64,16,128]{2,1,0:T(8,128)(2,1)S(1)}, bf16[64,16,128]{2,1,0:T(8,128)(2,1)S(1)}, u32[]{:S(2)}, u32[]{:S(2)}) collective-permute-start(bf16[64,16,128]{2,1,0:T(8,128)(2,1)S(1)} %get-tuple-element.39), channel_id=1, source_target_pairs={{0,1},{1,0},{2,3},{3,2},{4,5},{5,4},{6,7},{7,6},{8,9},{9,8},{10,11... | collective-permute-start | bytes 786440 | tf_op jit(solution)/shard_map/ppermute | solution.py:514
  19.1 17.4 %collective-permute-start.4 = (bf16[64,16,128]{2,1,0:T(8,128)(2,1)S(1)}, bf16[64,16,128]{2,1,0:T(8,128)(2,1)S(1)}, u32[]{:S(2)}, u32[]{:S(2)}) collective-permute-start(bf16[64,16,128]{2,1,0:T(8,128)(2,1)S(1)} %get-tuple-element.40), channel_id=1, source_target_pairs={{0,2},{1,3},{2,0},{3,1},{4,6},{5,7},{6,4},{7,5},{8,10},{9,11},{10,... | collective-permute-start | bytes 786440 | tf_op jit(solution)/shard_map/ppermute | solution.py:514
  36.5 1.6 %collective-permute-start.5 = (s16[17,16,512]{2,1,0:T(8,128)(2,1)S(1)}, s16[17,16,512]{2,1,0:T(8,128)(2,1)S(1)}, u32[]{:S(2)}, u32[]{:S(2)}) collective-permute-start(s16[17,16,512]{2,1,0:T(8,128)(2,1)S(1)} %get-tuple-element.46), channel_id=1, source_target_pairs={{0,4},{4,0},{8,12},{12,8},{1,5},{5,1},{9,13},{13,9},{2,6},{6,2},{1... | collective-permute-start | bytes 835592 | tf_op jit(solution)/shard_map/ppermute | solution.py:514
  36.5 2.0 %collective-permute-start.6 = (s16[17,16,512]{2,1,0:T(8,128)(2,1)S(1)}, s16[17,16,512]{2,1,0:T(8,128)(2,1)S(1)}, u32[]{:S(2)}, u32[]{:S(2)}) collective-permute-start(s16[17,16,512]{2,1,0:T(8,128)(2,1)S(1)} %get-tuple-element.47), channel_id=1, source_target_pairs={{0,4},{4,0},{8,12},{12,8},{1,5},{5,1},{9,13},{13,9},{2,6},{6,2},{1... | collective-permute-start | bytes 835592 | tf_op jit(solution)/shard_map/ppermute | solution.py:514
  42.5 6.9 %collective-permute-start.9 = (f32[6,16,128]{2,1,0:T(8,128)S(1)}, f32[6,16,128]{2,1,0:T(8,128)S(1)}, u32[]{:S(2)}, u32[]{:S(2)}) collective-permute-start(f32[6,16,128]{2,1,0:T(8,128)S(1)} %get-tuple-element.54), channel_id=1, source_target_pairs={{0,1},{1,0},{2,3},{3,2},{4,5},{5,4},{6,7},{7,6},{8,9},{9,8},{10,11... | collective-permute-start | bytes 147464 | tf_op jit(solution)/shard_map/ppermute | solution.py:514
  43.1 6.3 %collective-permute-start.10 = (f32[6,16,128]{2,1,0:T(8,128)S(1)}, f32[6,16,128]{2,1,0:T(8,128)S(1)}, u32[]{:S(2)}, u32[]{:S(2)}) collective-permute-start(f32[6,16,128]{2,1,0:T(8,128)S(1)} %get-tuple-element.55), channel_id=1, source_target_pairs={{0,2},{1,3},{2,0},{3,1},{4,6},{5,7},{6,4},{7,5},{8,10},{9,11},{10,... | collective-permute-start | bytes 147464 | tf_op jit(solution)/shard_map/ppermute | solution.py:514
  44.7 6.0 %collective-permute-start.11 = (f32[6,16,128]{2,1,0:T(8,128)S(1)}, f32[6,16,128]{2,1,0:T(8,128)S(1)}, u32[]{:S(2)}, u32[]{:S(2)}) collective-permute-start(f32[6,16,128]{2,1,0:T(8,128)S(1)} %get-tuple-element.56), channel_id=1, source_target_pairs={{0,3},{1,2},{2,1},{3,0},{4,7},{5,6},{6,5},{7,4},{8,11},{9,10},{10,... | collective-permute-start | bytes 147464 | tf_op jit(solution)/shard_map/ppermute | solution.py:514
